TPU v7x, 32 devices: a whole 2x2x4 slice. The times are simulated.
32 devices in a mesh: basis: 8 (over y, x, core), orb: 4 (over z).
Axes of the slice: x: 2, y: 2, z: 4, core: 2. Of those that a mesh axis runs over, the one named last changes fastest.
Arguments:
- cont_orbitals: bfloat16 [32768, 2048], P('basis', 'orb'), may hold values from -6 to 6
- target_orbitals: bfloat16 [32768, 1024], P('basis'), may hold values from -0.09375 to 0.09375
- margin_blocks: bfloat16 [128, 4, 256, 256], P('basis'), may hold values from -0.1875 to 0.1875
- dipole_blocks: bfloat16 [128, 4, 256, 256], P('basis'), may hold values from -0.1875 to 0.1875
- band_offsets: int32 [128, 4], P('basis'), may hold values from -2 to 2, as said below
Outputs:
- cont_orth: bfloat16 [32768, 2048], P('basis', 'orb')
- dipole_mo: bfloat16 [1024, 2048], P('basis', 'orb')
Inputs may be any that keep to these rules, and one draw needn't show every extreme that they name: `band_offsets`: each block row names 4 different offsets.
All inputs are finite; a program needn't handle non-finite values.
Results may differ from a plain program's by a relative error of at most 0.012.
Values may be sent and summed in bfloat16 or wider, within the bound.
No kernel may reach another device: no remote copies, remote signals or barrier semaphores. Data moves between devices by JAX's collectives and lax.ppermute only.
A program may use at most 128 MiB of HBM per device.

v0:
```python
import jax
import jax.numpy as jnp
from jax import lax
from jax.sharding import PartitionSpec as P

BK = 256
KB = 4


def padded_2(block, sides, width):
    for axis, dim in sides:
        count = lax.axis_size(axis)
        forward = [(i, i + 1) for i in range(count - 1)]
        backward = [(target, source) for source, target in forward]
        low = lax.ppermute(
            lax.slice_in_dim(block, block.shape[dim] - width, None, axis=dim), axis, forward
        )
        high = lax.ppermute(lax.slice_in_dim(block, 0, width, axis=dim), axis, backward)
        block = jnp.concatenate([low, block, high], axis=dim)
    return block


def band_local(blocks, offsets, padded):
    nblk = blocks.shape[0]
    width = padded.shape[1]
    stacked = padded.reshape(nblk + 4, BK, width)
    total = jnp.zeros((nblk, BK, width), jnp.float32)
    for k in range(KB):
        index = jnp.arange(nblk, dtype=jnp.int32) + 2 + offsets[:, k]
        taken = stacked[index]
        total = total + jnp.einsum(
            "bij,bjc->bic", blocks[:, k], taken, preferred_element_type=jnp.float32
        )
    return total.reshape(nblk * BK, width)


def on_device(cont_orbitals, target_orbitals, margin_blocks, dipole_blocks, band_offsets):
    cont_padded = padded_2(cont_orbitals, (("basis", 0),), 2 * BK)
    margin_cont = band_local(margin_blocks, band_offsets, cont_padded).astype(jnp.bfloat16)
    partial_proj = lax.dot_general(
        target_orbitals, margin_cont, (((0,), (0,)), ((), ())), preferred_element_type=jnp.float32
    )
    projection = lax.psum(partial_proj, "basis")
    projection_b = projection.astype(jnp.bfloat16)
    removed = jnp.dot(target_orbitals, projection_b, preferred_element_type=jnp.float32)
    cont_orth = (cont_orbitals.astype(jnp.float32) - removed).astype(jnp.bfloat16)
    squares = jnp.sum(jnp.square(cont_orth.astype(jnp.float32)), axis=0)
    orth_padded = padded_2(cont_orth, (("basis", 0),), 2 * BK)
    total_squares = lax.psum(squares, "basis")
    col_norm = 1.0 / jnp.sqrt(
        total_squares / (band_offsets.shape[0] * BK * lax.axis_size("basis")) + 1e-06
    )
    dipole_cont = band_local(dipole_blocks, band_offsets, orth_padded).astype(jnp.bfloat16)
    dipole_raw = lax.psum_scatter(
        lax.dot_general(
            target_orbitals,
            dipole_cont,
            (((0,), (0,)), ((), ())),
            preferred_element_type=jnp.float32,
        ),
        "basis",
        scatter_dimension=0,
        tiled=True,
    )
    dipole_mo = (dipole_raw * col_norm[None, :]).astype(jnp.bfloat16)
    return (cont_orth, dipole_mo)


def solution(mesh):
    return jax.shard_map(
        on_device,
        mesh=mesh,
        in_specs=(
            P("basis", "orb"),
            P("basis", None),
            P("basis", None, None, None),
            P("basis", None, None, None),
            P("basis", None),
        ),
        out_specs=(P("basis", "orb"), P("basis", "orb")),
        check_vma=False,
    )
```

profile of v0, /device:TPU:0, one launch (start us, length us, event | category | flops | bytes accessed | tf_op | source)
XLA Modules:
  0.0 304.1 jit_solution(10531297364489178491)
XLA Ops:
  8.5 2.4 collective-permute-start
  10.9 1.3 collective-permute-start.1
  12.2 6.4 %copy.18 = bf16[4096,512]{0,1:T(8,128)(2,1)} copy(bf16[4096,512]{1,0:T(8,128)(2,1)} %param.5) | data formatting | bytes 8388608 | tf_op args[0]
  18.7 10.0 %pad_maximum_fusion = bf16[5120,512]{1,0:T(8,128)(2,1)} fusion(bf16[512,512]{1,0:T(8,128)(2,1)S(1)} %collective-permute-done.1, bf16[4096,512]{1,0:T(8,128)(2,1)} %param.5, bf16[512,512]{1,0:T(8,128)(2,1)S(1)} %collective-permute-done), kind=kLoop, calls=%fused_computation.13 | loop fusion | flops 15728640 | bytes 10485760 | tf_op jit(solution)/shard_map/concatenate | solution.py:19
  28.7 5.2 %gather_fusion.3 = bf16[16,256,512]{2,1,0:T(8,128)(2,1)} fusion(bf16[20,256,512]{2,1,0:T(8,128)(2,1)} %bitcast.82, s32[1024]{0:T(1024)S(1)} %get-tuple-element.16), kind=kCustom, calls=%fused_computation.3 | custom fusion | bytes 8388672 | tf_op jit(solution)/shard_map/gather | solution.py:30
  33.9 5.3 %gather_fusion.2 = bf16[16,256,512]{2,1,0:T(8,128)(2,1)} fusion(bf16[20,256,512]{2,1,0:T(8,128)(2,1)} %bitcast.83, s32[1024]{0:T(1024)S(1)} %get-tuple-element.17), kind=kCustom, calls=%fused_computation.2 | custom fusion | bytes 8388672 | tf_op jit(solution)/shard_map/gather | solution.py:30
  39.2 5.2 %gather_fusion.1 = bf16[16,256,512]{2,1,0:T(8,128)(2,1)} fusion(bf16[20,256,512]{2,1,0:T(8,128)(2,1)} %bitcast.84, s32[1024]{0:T(1024)S(1)} %get-tuple-element.18), kind=kCustom, calls=%fused_computation.1 | custom fusion | bytes 8388672 | tf_op jit(solution)/shard_map/gather | solution.py:30
  44.5 5.3 %gather_fusion = bf16[16,256,512]{2,1,0:T(8,128)(2,1)} fusion(bf16[20,256,512]{2,1,0:T(8,128)(2,1)} %bitcast.85, s32[1024]{0:T(1024)S(1)} %get-tuple-element.19), kind=kCustom, calls=%fused_computation | custom fusion | bytes 8388672 | tf_op jit(solution)/shard_map/gather | solution.py:30
  49.7 7.5 %fusion.9 = f32[16,512,256]{1,2,0:T(8,128)} fusion(bf16[16,256,512]{2,1,0:T(8,128)(2,1)} %gather_fusion.2, bf16[16,4,256,256]{3,2,1,0:T(8,128)(2,1)} %param.7), kind=kOutput, calls=%fused_computation.23 | convolution fusion | flops 1073741824 | bytes 14680064 | tf_op jit(solution)/shard_map/bij,bjc->bic/dot_general | solution.py:31
  57.2 6.2 %fusion.13 = f32[16,512,256]{1,2,0:T(8,128)} fusion(bf16[16,256,512]{2,1,0:T(8,128)(2,1)S(1)} %copy-done.6, bf16[16,4,256,256]{3,2,1,0:T(8,128)(2,1)} %param.7), kind=kOutput, calls=%fused_computation.27 | convolution fusion | flops 1073741824 | bytes 14680064 | tf_op jit(solution)/shard_map/bij,bjc->bic/dot_general | solution.py:31
  63.4 6.2 %fusion.11 = f32[16,512,256]{1,2,0:T(8,128)} fusion(bf16[16,256,512]{2,1,0:T(8,128)(2,1)S(1)} %copy-done.4, bf16[16,4,256,256]{3,2,1,0:T(8,128)(2,1)} %param.7), kind=kOutput, calls=%fused_computation.25 | convolution fusion | flops 1073741824 | bytes 14680064 | tf_op jit(solution)/shard_map/bij,bjc->bic/dot_general | solution.py:31
  69.7 12.0 %add_convert_fusion.1 = bf16[16,512,256]{1,2,0:T(8,128)(2,1)} fusion(f32[16,512,256]{1,2,0:T(8,128)} %fusion.9, f32[16,512,256]{1,2,0:T(8,128)} %fusion.13, f32[16,512,256]{1,2,0:T(8,128)} %fusion.11, bf16[16,256,512]{2,1,0:T(8,128)(2,1)S(1)} %copy-done.2, bf16[16,4,256,256]{3,2,1,0:T(8,128)(2,1)} %param.7), kind=kOutput, calls=%fused_computation.12 | convolution fusion | flops 1082130432 | bytes 35651584 | tf_op jit(solution)/shard_map/bij,bjc->bic/dot_general | solution.py:31
  81.7 8.2 %convolution_bitcast_fusion.1 = f32[1024,512]{0,1:T(8,128)S(1)} fusion(bf16[4096,512]{1,0:T(8,128)(2,1)} %bitcast.86, bf16[4096,1024]{1,0:T(8,128)(2,1)} %param.6), kind=kOutput, calls=%fused_computation.38 | convolution fusion | flops 4294967296 | bytes 14680064 | tf_op jit(solution)/shard_map/dot_general | solution.py:40
  89.9 63.9 %all-reduce.1 = bf16[1024,512]{0,1:T(8,128)(2,1)S(1)} all-reduce(f32[1024,512]{0,1:T(8,128)S(1)} %convolution_bitcast_fusion.1), channel_id=1, replica_groups=mesh['basis'=8,'orb'=4] {'basis'}, use_global_device_ids=true, to_apply=%region_0.0 | all-reduce | flops 524288 | bytes 3145728 | tf_op jit(solution)/shard_map/psum | solution.py:43
  153.8 9.3 %multiply_reduce_fusion = (f32[512]{0:T(512)S(1)}, bf16[4096,512]{0,1:T(8,128)(2,1)S(1)}) fusion(bf16[1024,512]{0,1:T(8,128)(2,1)S(1)} %all-reduce.1, bf16[4096,1024]{1,0:T(8,128)(2,1)} %param.6, bf16[4096,512]{0,1:T(8,128)(2,1)} %copy.18), kind=kOutput, calls=%fused_computation.10 | convolution fusion | flops 4307549696 | bytes 17827840 | tf_op jit(solution)/shard_map/dot_general | solution.py:45
  163.2 1.3 collective-permute-start.2
  164.5 1.3 collective-permute-start.3
  166.0 2.3 collective-permute-done.3
  168.3 3.1 %pad_maximum_fusion.1 = bf16[5120,512]{0,1:T(8,128)(2,1)} fusion(bf16[512,512]{0,1:T(8,128)(2,1)S(1)} %collective-permute-done.3, bf16[4096,512]{0,1:T(8,128)(2,1)S(1)} %get-tuple-element.15, bf16[512,512]{0,1:T(8,128)(2,1)S(1)} %collective-permute-done.2), kind=kLoop, calls=%fused_computation.14 | loop fusion | flops 15728640 | bytes 10485760 | tf_op jit(solution)/shard_map/concatenate | solution.py:19
  171.5 7.9 %copy.23 = bf16[5120,512]{1,0:T(8,128)(2,1)} copy(bf16[5120,512]{0,1:T(8,128)(2,1)} %pad_maximum_fusion.1) | data formatting | bytes 10485760 | tf_op jit(solution)/shard_map/concatenate | solution.py:19
  179.4 5.2 %gather_fusion.7 = bf16[16,256,512]{2,1,0:T(8,128)(2,1)} fusion(bf16[20,256,512]{2,1,0:T(8,128)(2,1)} %bitcast.78, s32[1024]{0:T(1024)S(1)} %get-tuple-element.16), kind=kCustom, calls=%fused_computation.7 | custom fusion | bytes 8388672 | tf_op jit(solution)/shard_map/gather | solution.py:30
  184.6 5.3 %gather_fusion.6 = bf16[16,256,512]{2,1,0:T(8,128)(2,1)} fusion(bf16[20,256,512]{2,1,0:T(8,128)(2,1)} %bitcast.79, s32[1024]{0:T(1024)S(1)} %get-tuple-element.17), kind=kCustom, calls=%fused_computation.6 | custom fusion | bytes 8388672 | tf_op jit(solution)/shard_map/gather | solution.py:30
  189.9 5.3 %gather_fusion.5 = bf16[16,256,512]{2,1,0:T(8,128)(2,1)} fusion(bf16[20,256,512]{2,1,0:T(8,128)(2,1)} %bitcast.80, s32[1024]{0:T(1024)S(1)} %get-tuple-element.18), kind=kCustom, calls=%fused_computation.5 | custom fusion | bytes 8388672 | tf_op jit(solution)/shard_map/gather | solution.py:30
  195.2 5.2 %gather_fusion.4 = bf16[16,256,512]{2,1,0:T(8,128)(2,1)} fusion(bf16[20,256,512]{2,1,0:T(8,128)(2,1)} %bitcast.81, s32[1024]{0:T(1024)S(1)} %get-tuple-element.19), kind=kCustom, calls=%fused_computation.4 | custom fusion | bytes 8388672 | tf_op jit(solution)/shard_map/gather | solution.py:30
  200.4 7.5 %fusion.6 = f32[16,512,256]{1,2,0:T(8,128)} fusion(bf16[16,256,512]{2,1,0:T(8,128)(2,1)} %gather_fusion.4, bf16[16,4,256,256]{3,2,1,0:T(8,128)(2,1)} %param.8), kind=kOutput, calls=%fused_computation.20 | convolution fusion | flops 1073741824 | bytes 14680064 | tf_op jit(solution)/shard_map/bij,bjc->bic/dot_general | solution.py:31
  207.9 6.2 %fusion.4 = f32[16,512,256]{1,2,0:T(8,128)} fusion(bf16[16,256,512]{2,1,0:T(8,128)(2,1)S(1)} %copy-done.5, bf16[16,4,256,256]{3,2,1,0:T(8,128)(2,1)} %param.8), kind=kOutput, calls=%fused_computation.18 | convolution fusion | flops 1073741824 | bytes 14680064 | tf_op jit(solution)/shard_map/bij,bjc->bic/dot_general | solution.py:31
  214.1 6.2 %fusion.2 = f32[16,512,256]{1,2,0:T(8,128)} fusion(bf16[16,256,512]{2,1,0:T(8,128)(2,1)S(1)} %copy-done.3, bf16[16,4,256,256]{3,2,1,0:T(8,128)(2,1)} %param.8), kind=kOutput, calls=%fused_computation.16 | convolution fusion | flops 1073741824 | bytes 14680064 | tf_op jit(solution)/shard_map/bij,bjc->bic/dot_general | solution.py:31
  220.3 12.0 %add_convert_fusion = bf16[16,512,256]{1,2,0:T(8,128)(2,1)} fusion(f32[16,512,256]{1,2,0:T(8,128)} %fusion.2, f32[16,512,256]{1,2,0:T(8,128)} %fusion.6, f32[16,512,256]{1,2,0:T(8,128)} %fusion.4, bf16[16,256,512]{2,1,0:T(8,128)(2,1)S(1)} %copy-done.1, bf16[16,4,256,256]{3,2,1,0:T(8,128)(2,1)} %param.8), kind=kOutput, calls=%fused_computation.11 | convolution fusion | flops 1082130432 | bytes 35651584 | tf_op jit(solution)/shard_map/bij,bjc->bic/dot_general | solution.py:31
  232.4 10.5 %convolution_bitcast_fusion = f32[1024,512]{0,1:T(8,128)} fusion(bf16[4096,512]{1,0:T(8,128)(2,1)} %bitcast.87, bf16[4096,1024]{1,0:T(8,128)(2,1)} %param.6), kind=kOutput, calls=%fused_computation.37 | convolution fusion | flops 4294967296 | bytes 14680064 | tf_op jit(solution)/shard_map/dot_general | solution.py:55
  242.9 6.4 %copy.28 = bf16[4096,512]{1,0:T(8,128)(2,1)} copy(bf16[4096,512]{0,1:T(8,128)(2,1)} %copy-done) | data formatting | bytes 8388608
  249.3 23.4 %psum.15 = f32[512]{0:T(512)S(1)} all-reduce(f32[512]{0:T(512)S(1)} %get-tuple-element.14), channel_id=1, replica_groups=mesh['basis'=8,'orb'=4] {'basis'}, use_global_device_ids=true, to_apply=%region_3.0 | all-reduce | flops 512 | bytes 4096 | tf_op jit(solution)/shard_map/psum | solution.py:49
  272.7 22.7 %reduce-scatter.2.cloned.1.call-done = f32[128,512]{0,1:T(8,128)} async-done(((f32[1024,512]{0,1:T(8,128)}), f32[128,512]{0,1:T(8,128)}) %reduce-scatter.2.cloned.1.call-update) | async-done | bytes 262160 | tf_op jit(solution)/shard_map/reduce_scatter | solution.py:54
  (29 shorter events, 3.5 us)
Async XLA Ops:
  7.2 288.2 %reduce-scatter.2.cloned.1.call-start = ((), (), s32[]{:S(2)}) async-start(), calls=%async_computation.1 | async-start | bytes 2359296 | tf_op jit(solution)/shard_map/reduce_scatter | solution.py:54
  8.5 10.2 %collective-permute-start = (bf16[512,512]{1,0:T(8,128)(2,1)S(1)}, bf16[512,512]{1,0:T(8,128)(2,1)S(1)}, u32[]{:S(2)}, u32[]{:S(2)}) collective-permute-start(bf16[512,512]{1,0:T(8,128)(2,1)S(1)} %get-tuple-element.8), channel_id=1, source_target_pairs={{0,4},{4,8},{8,12},{12,16},{16,20},{20,24},{24,28},{1,5},{5,9},{9,... | collective-permute-start | bytes 1572872 | tf_op jit(solution)/shard_map/ppermute | solution.py:15
  10.9 7.7 %copy-start.7 = (s32[16,4]{0,1:T(4,128)S(1)}, s32[16,4]{0,1:T(4,128)}, u32[]{:S(2)}) copy-start(s32[16,4]{0,1:T(4,128)} %param.9) | copy-start | bytes 772
  10.9 7.8 %collective-permute-start.1 = (bf16[512,512]{1,0:T(8,128)(2,1)S(1)}, bf16[512,512]{1,0:T(8,128)(2,1)S(1)}, u32[]{:S(2)}, u32[]{:S(2)}) collective-permute-start(bf16[512,512]{1,0:T(8,128)(2,1)S(1)} %get-tuple-element.9), channel_id=1, source_target_pairs={{4,0},{8,4},{12,8},{16,12},{20,16},{24,20},{28,24},{5,1},{9,5},{13... | collective-permute-start | bytes 1572872 | tf_op jit(solution)/shard_map/ppermute | solution.py:18
  49.7 7.5 %copy-start.6 = (bf16[16,256,512]{2,1,0:T(8,128)(2,1)S(1)}, bf16[16,256,512]{2,1,0:T(8,128)(2,1)}, u32[]{:S(2)}) copy-start(bf16[16,256,512]{2,1,0:T(8,128)(2,1)} %gather_fusion) | copy-start | bytes 12582916
  57.2 6.2 %copy-start.4 = (bf16[16,256,512]{2,1,0:T(8,128)(2,1)S(1)}, bf16[16,256,512]{2,1,0:T(8,128)(2,1)}, u32[]{:S(2)}) copy-start(bf16[16,256,512]{2,1,0:T(8,128)(2,1)} %gather_fusion.1) | copy-start | bytes 12582916
  63.4 6.2 %copy-start.2 = (bf16[16,256,512]{2,1,0:T(8,128)(2,1)S(1)}, bf16[16,256,512]{2,1,0:T(8,128)(2,1)}, u32[]{:S(2)}) copy-start(bf16[16,256,512]{2,1,0:T(8,128)(2,1)} %gather_fusion.3) | copy-start | bytes 12582916
  163.1 5.2 %copy-start = (bf16[4096,512]{0,1:T(8,128)(2,1)}, bf16[4096,512]{0,1:T(8,128)(2,1)S(1)}, u32[]{:S(2)}) copy-start(bf16[4096,512]{0,1:T(8,128)(2,1)S(1)} %get-tuple-element.15) | copy-start | bytes 12582916
  163.2 2.8 collective-permute-start.2
  164.5 3.8 %collective-permute-start.3 = (bf16[512,512]{0,1:T(8,128)(2,1)S(1)}, bf16[512,512]{0,1:T(8,128)(2,1)S(1)}, u32[]{:S(2)}, u32[]{:S(2)}) collective-permute-start(bf16[512,512]{0,1:T(8,128)(2,1)S(1)} %get-tuple-element.7), channel_id=1, source_target_pairs={{4,0},{8,4},{12,8},{16,12},{20,16},{24,20},{28,24},{5,1},{9,5},{13... | collective-permute-start | bytes 1572872 | tf_op jit(solution)/shard_map/ppermute | solution.py:18
  200.4 7.5 %copy-start.5 = (bf16[16,256,512]{2,1,0:T(8,128)(2,1)S(1)}, bf16[16,256,512]{2,1,0:T(8,128)(2,1)}, u32[]{:S(2)}) copy-start(bf16[16,256,512]{2,1,0:T(8,128)(2,1)} %gather_fusion.5) | copy-start | bytes 12582916
  207.9 6.2 %copy-start.3 = (bf16[16,256,512]{2,1,0:T(8,128)(2,1)S(1)}, bf16[16,256,512]{2,1,0:T(8,128)(2,1)}, u32[]{:S(2)}) copy-start(bf16[16,256,512]{2,1,0:T(8,128)(2,1)} %gather_fusion.6) | copy-start | bytes 12582916
  214.1 6.2 %copy-start.1 = (bf16[16,256,512]{2,1,0:T(8,128)(2,1)S(1)}, bf16[16,256,512]{2,1,0:T(8,128)(2,1)}, u32[]{:S(2)}) copy-start(bf16[16,256,512]{2,1,0:T(8,128)(2,1)} %gather_fusion.7) | copy-start | bytes 12582916
Sparse Core Ops, SparseCore 0:
  243.0 52.3 reduce-scatter.1
where the time goes:
time: 305 us; the launch traced here: 304 us
  matrix products  91.9 us (30%)
  blocking collectives  87.3 us (29%)
  local copies, waits for them, and re-layouts  65 us (21%)
  waiting for transfers between devices  25.2 us (8%)
  other arithmetic  14.2 us (5%)
  between operations  14.2 us (5%)
  starting transfers between devices  6.33 us (2%)
    psum x1, blocking collectives, on_device(): projection = lax.psum(partial_proj, 'basis')  63.9 us
    dot_general x8, matrix products, band_local(): jnp.einsum('bij,bjc->bic', blocks[:, k], taken, preferred_element_type=jn...  63.9 us
    gather x8, local copies, waits for them, and re-layouts, band_local(): taken = stacked[index]  42.1 us
    psum x1, blocking collectives, on_device(): total_squares = lax.psum(squares, 'basis')  23.4 us
    reduce_scatter x1, waiting for transfers between devices, on_device(): lax.psum_scatter(lax.dot_general(target_orbitals, dipole_cont, (((0,), (0...  22.7 us
    unnamed x19, local copies, waits for them, and re-layouts  13.6 us
    concatenate x2, other arithmetic, padded_2(): block = jnp.concatenate([low, block, high], axis=dim)  13.1 us
    dot_general x1, matrix products, on_device(): lax.dot_general(target_orbitals, dipole_cont, (((0,), (0,)), ((), ())), p...  10.5 us
  transfers between devices with their start and end apart: 5, of which 3 were waited for; matrix products, arithmetic and copies ran while one was open for 4% of the time, Pallas kernels for 0%

commit v1 on v0

v1 whole, which is shorter than its diff:
```python
import functools

import jax
import jax.numpy as jnp
from jax import lax
from jax.experimental import pallas as pl
from jax.experimental.pallas import tpu as pltpu
from jax.sharding import PartitionSpec as P

BK = 256
KB = 4
PAD = 16
F32 = jnp.float32
BF16 = jnp.bfloat16
ANY = pl.BlockSpec(memory_space=pl.ANY)
VMEM = pl.BlockSpec(memory_space=pltpu.VMEM)
SMEM = pl.BlockSpec(memory_space=pltpu.SMEM)


def params(mib=40):
    return pltpu.CompilerParams(vmem_limit_bytes=mib * 2**20)


def cost(macs, data):
    return pl.CostEstimate(flops=2 * macs, bytes_accessed=data, transcendentals=0)


def dot(a, b, dims=((1,), (0,))):
    return lax.dot_general(a, b, (dims, ((), ())), preferred_element_type=F32)


class Loads:
    def __init__(self, sems):
        self.sems, self.copies, self.done = sems, [], set()

    def start(self, src, dst):
        copy = pltpu.make_async_copy(src, dst, self.sems.at[len(self.copies)])
        copy.start()
        self.copies.append(copy)
        return len(self.copies) - 1

    def wait(self, *which):
        for i in which:
            if i not in self.done:
                self.copies[i].wait()
                self.done.add(i)


def band_rows(rows, slots, off, field, blocks, base, ys):
    for r, (b, slot) in enumerate(zip(rows, slots)):
        total = None
        for k in range(KB):
            term = dot(blocks[slot, k], field[b + off[k, b] + base])
            total = term if total is None else total + term
        ys[r * BK : (r + 1) * BK, :] = total.astype(BF16)


def groups_of(nblk):
    inner = list(range(2, nblk - 2))
    return [inner[i : i + 4] for i in range(0, len(inner), 4)]


def interior_kernel(nblk, off, c, t, m, out, c_v, t_v, m_v, ys, sems):
    loads = Loads(sems)
    have, needs = 0, []
    for rows in groups_of(nblk):
        lo, hi = rows[0], rows[-1] + 1
        mid = min(lo + 2, hi)
        want = []
        for part in ((lo, mid), (mid, hi)):
            if part[0] == part[1]:
                continue
            upto = part[1] + 2
            ids = []
            if upto > have:
                ids.append(loads.start(c.at[have:upto], c_v.at[have:upto]))
                have = upto
            ids.append(
                loads.start(m.at[part[0] : part[1]], m_v.at[part[0] - 2 : part[1] - 2])
            )
            want.append((list(range(*part)), ids))
        t_id = loads.start(t.at[lo:hi], t_v.at[lo - 2 : hi - 2])
        needs.append((rows, want, t_id))
    for g, (rows, want, t_id) in enumerate(needs):
        at = 0
        for part, ids in want:
            loads.wait(*ids)
            band_rows(
                part, [b - 2 for b in part], off, c_v, m_v, 0,
                ys.at[at * BK : (at + len(part)) * BK],
            )
            at += len(part)
        loads.wait(t_id)
        lo, size = rows[0] - 2, len(rows) * BK
        piece = dot(ys[0:size, :], t_v[lo : lo + len(rows)].reshape(size, -1), ((0,), (0,)))
        if g == 0:
            out[...] = piece
        else:
            out[...] += piece


def project_interior(off, c, t, m):
    nblk, _, w = c.shape
    nt = t.shape[2]
    inner = nblk - 4
    return pl.pallas_call(
        functools.partial(interior_kernel, nblk),
        out_shape=jax.ShapeDtypeStruct((w, nt), F32),
        in_specs=[SMEM, ANY, ANY, ANY],
        out_specs=VMEM,
        scratch_shapes=[
            pltpu.VMEM((nblk, BK, w), BF16),
            pltpu.VMEM((inner, BK, nt), BF16),
            pltpu.VMEM((inner, KB, BK, BK), BF16),
            pltpu.VMEM((4 * BK, w), BF16),
            pltpu.SemaphoreType.DMA((5 * len(groups_of(nblk)),)),
        ],
        compiler_params=params(),
        cost_estimate=cost(inner * BK * w * (KB * BK + nt), 2 * (c.size + t.size + m.size)),
    )(off, c, t, m)


def boundary_rows(nblk, core, off, f, intra, inter, t, m, f_v, t_v, m_v, ys, sems):
    loads = Loads(sems)
    parts = []
    for side, at, home in ((0, 0, 2), (1, nblk - 2, 6)):
        ids = [loads.start(m.at[at : at + 2], m_v.at[2 * side : 2 * side + 2])]
        near = 0 if side == 0 else nblk - 4
        ids.append(loads.start(f.at[near : near + 4], f_v.at[home : home + 4]))
        parts.append(ids)
    low = 10 * (1 - core)
    parts[0].append(loads.start(intra, f_v.at[pl.ds(low, 2)]))
    parts[0].append(loads.start(inter, f_v.at[pl.ds(10 - low, 2)]))
    for side, at in ((0, 0), (1, nblk - 2)):
        parts[1].append(loads.start(t.at[at : at + 2], t_v.at[2 * side : 2 * side + 2]))
    loads.wait(*parts[0])
    band_rows([0, 1], [0, 1], off, f_v, m_v, 2, ys.at[0 : 2 * BK])
    loads.wait(*parts[1])
    band_rows(
        [nblk - 2, nblk - 1], [2, 3], off, f_v, m_v, 10 - nblk, ys.at[2 * BK : 4 * BK]
    )
    return dot(ys[...], t_v[...].reshape(4 * BK, -1), ((0,), (0,)))


def boundary_scratch(w, nt):
    return [
        pltpu.VMEM((12, BK, w), BF16),
        pltpu.VMEM((4, BK, nt), BF16),
        pltpu.VMEM((4, KB, BK, BK), BF16),
        pltpu.VMEM((4 * BK, w), BF16),
        pltpu.SemaphoreType.DMA((8,)),
    ]


def boundary_kernel(nblk, core, off, acc, c, intra, inter, t, m, send, keep, total, *scratch):
    half = send.shape[0]
    total[...] = acc[...] + boundary_rows(
        nblk, core[0], off, c, intra, inter, t, m, *scratch
    )
    here = pl.multiple_of(core[0] * half, half)
    there = pl.multiple_of((1 - core[0]) * half, half)
    send[...] = total[pl.ds(there, half), :].astype(BF16)
    keep[...] = total[pl.ds(here, half), :]


def project_boundary(core, off, acc, c, intra, inter, t, m):
    nblk, _, w = c.shape
    nt = t.shape[2]
    return pl.pallas_call(
        functools.partial(boundary_kernel, nblk),
        out_shape=(
            jax.ShapeDtypeStruct((w // 2, nt), BF16),
            jax.ShapeDtypeStruct((w // 2, nt), F32),
        ),
        in_specs=[SMEM, SMEM, VMEM, ANY, ANY, ANY, ANY, ANY],
        out_specs=(VMEM, VMEM),
        scratch_shapes=[pltpu.VMEM((w, nt), F32)] + boundary_scratch(w, nt),
        compiler_params=params(),
        cost_estimate=cost(4 * BK * w * (KB * BK + nt), 8 * 2**20),
    )(core, off, acc, c, intra, inter, t, m)


def orth_rows(c, t, p):
    return (c.astype(F32) - dot(t, p, ((1,), (1,)))).astype(BF16)


def place_projection(core, mine, other, p):
    half = mine.shape[0]
    p[pl.ds(pl.multiple_of(core * half, half), half), :] = mine[...]
    p[pl.ds(pl.multiple_of((1 - core) * half, half), half), :] = other[...]


def square_sum(x):
    x = x.astype(F32)
    return jnp.sum(x * x, axis=0, keepdims=True)


def edge_kernel(nblk, core, mine, other, c, t, edge, intra, inter, sq, c_v, t_v, p, sems):
    loads = Loads(sems)
    ids = []
    for side, at in ((0, 0), (1, nblk - 2)):
        ids.append(
            (
                loads.start(c.at[at : at + 2], c_v.at[2 * side : 2 * side + 2]),
                loads.start(t.at[at : at + 2], t_v.at[2 * side : 2 * side + 2]),
            )
        )
    place_projection(core[0], mine, other, p)
    sq[...] = jnp.zeros_like(sq)
    for side in range(2):
        loads.wait(*ids[side])
        for r in range(2):
            i = 2 * side + r
            x = orth_rows(c_v[i], t_v[i], p[...])
            edge[i] = x
            sq[...] += square_sum(x)

            @pl.when(core[0] == side)
            def _(x=x, r=r):
                inter[r] = x

            @pl.when(core[0] != side)
            def _(x=x, r=r):
                intra[r] = x


def orth_edges(core, mine, other, c, t):
    nblk, _, w = c.shape
    nt = t.shape[2]
    pair = jax.ShapeDtypeStruct((2, BK, w), BF16)
    return pl.pallas_call(
        functools.partial(edge_kernel, nblk),
        out_shape=(
            jax.ShapeDtypeStruct((4, BK, w), BF16),
            pair,
            pair,
            jax.ShapeDtypeStruct((1, w), F32),
        ),
        in_specs=[SMEM, VMEM, VMEM, ANY, ANY],
        out_specs=(VMEM,) * 4,
        scratch_shapes=[
            pltpu.VMEM((4, BK, w), BF16),
            pltpu.VMEM((4, BK, nt), BF16),
            pltpu.VMEM((w, nt), BF16),
            pltpu.SemaphoreType.DMA((4,)),
        ],
        compiler_params=params(),
        cost_estimate=cost(4 * BK * w * nt, 4 * 2**20),
    )(core, mine, other, c, t)


def orth_dipole_kernel(
    nblk, core, off, mine, other, c, t, d, edge, sq_in, x_out, out, sq,
    c_v, t_v, d_v, x_v, ys, p, sems, out_sems,
):
    loads = Loads(sems)
    groups = groups_of(nblk)
    low = loads.start(edge.at[0:2], x_v.at[0:2])
    high = loads.start(edge.at[2:4], x_v.at[nblk - 2 : nblk])
    ct_ids, d_ids = [], []
    for rows in groups:
        lo, hi = rows[0], rows[-1] + 1
        ct_ids.append(
            (
                loads.start(c.at[lo:hi], c_v.at[lo - 2 : hi - 2]),
                loads.start(t.at[lo:hi], t_v.at[lo - 2 : hi - 2]),
            )
        )
    for rows in groups:
        lo, hi = rows[0], rows[-1] + 1
        d_ids.append(loads.start(d.at[lo:hi], d_v.at[lo - 2 : hi - 2]))
    place_projection(core[0], mine, other, p)
    sq[...] = sq_in[...]
    stores = Loads(out_sems)
    for rows, ids in zip(groups, ct_ids):
        loads.wait(*ids)
        for b in rows:
            x = orth_rows(c_v[b - 2], t_v[b - 2], p[...])
            x_v[b] = x
            sq[...] += square_sum(x)
        stores.start(
            x_v.at[rows[0] : rows[-1] + 1], x_out.at[rows[0] : rows[-1] + 1]
        )
    loads.wait(low, high)
    stores.start(x_v.at[0:2], x_out.at[0:2])
    stores.start(x_v.at[nblk - 2 : nblk], x_out.at[nblk - 2 : nblk])
    for g, (rows, d_id) in enumerate(zip(groups, d_ids)):
        loads.wait(d_id)
        lo, size = rows[0] - 2, len(rows) * BK
        band_rows(rows, [b - 2 for b in rows], off, x_v, d_v, 0, ys.at[0:size])
        piece = dot(ys[0:size, :], t_v[lo : lo + len(rows)].reshape(size, -1), ((0,), (0,)))
        if g == 0:
            out[...] = piece
        else:
            out[...] += piece
    stores.wait(*range(len(stores.copies)))


def orth_dipole_interior(core, off, mine, other, c, t, d, edge, sq):
    nblk, _, w = c.shape
    nt = t.shape[2]
    inner = nblk - 4
    count = len(groups_of(nblk))
    return pl.pallas_call(
        functools.partial(orth_dipole_kernel, nblk),
        out_shape=(
            jax.ShapeDtypeStruct((nblk, BK, w), BF16),
            jax.ShapeDtypeStruct((w, nt), F32),
            jax.ShapeDtypeStruct((1, w), F32),
        ),
        in_specs=[SMEM, SMEM, VMEM, VMEM, ANY, ANY, ANY, ANY, VMEM],
        out_specs=(ANY, VMEM, VMEM),
        scratch_shapes=[
            pltpu.VMEM((inner, BK, w), BF16),
            pltpu.VMEM((inner, BK, nt), BF16),
            pltpu.VMEM((inner, KB, BK, BK), BF16),
            pltpu.VMEM((nblk, BK, w), BF16),
            pltpu.VMEM((4 * BK, w), BF16),
            pltpu.VMEM((w, nt), BF16),
            pltpu.SemaphoreType.DMA((2 + 3 * count,)),
            pltpu.SemaphoreType.DMA((2 + count,)),
        ],
        compiler_params=params(),
        cost_estimate=cost(inner * BK * w * (KB * BK + 2 * nt), 24 * 2**20),
    )(core, off, mine, other, c, t, d, edge, sq)


def put_squares(msg, g, sq, w):
    lanes = msg.shape[2]
    hi = sq.astype(BF16).astype(F32)
    lo = sq - hi
    rows = [part[:, q * lanes : (q + 1) * lanes] for part in (hi, lo) for q in range(w // lanes)]
    if len(rows) < PAD:
        rows.append(jnp.zeros((PAD - len(rows), lanes), F32))
    msg[g, w : w + PAD, :] = jnp.concatenate(rows, axis=0).astype(BF16)


def get_squares(msg, g, w):
    tail = msg[g, w : w + PAD, :].astype(F32)
    count = w // msg.shape[2]
    rows = [tail[q : q + 1] + tail[count + q : count + q + 1] for q in range(count)]
    return jnp.concatenate(rows, axis=1)


def dipole_boundary_kernel(
    nblk, core, off, acc, x, intra, inter, t, d, sq, send, keep, total, *scratch
):
    groups, w, lanes = keep.shape
    bits = groups.bit_length() - 1
    total[...] = acc[...] + boundary_rows(
        nblk, core[0], off, x, intra, inter, t, d, *scratch
    )
    for g in range(groups):
        orders = [chip_order(bits, side) for side in (0, 1)]
        places = [
            sum(((g >> (bits - 1 - s)) & 1) << orders[side][s] for s in range(bits))
            for side in (0, 1)
        ]
        owned = [
            total[:, (2 * places[side] + side) * lanes : (2 * places[side] + side + 1) * lanes]
            for side in (0, 1)
        ]
        keep[g] = jnp.where(core[0] == 0, owned[0], owned[1])
        send[g, 0:w, :] = jnp.where(core[0] == 0, owned[1], owned[0]).astype(BF16)
        put_squares(send, g, sq[...], w)


def chip_order(bits, side):
    return [(s + side) % bits for s in range(bits)]


def dipole_boundary(core, off, acc, x, intra, inter, t, d, sq, groups):
    nblk, _, w = x.shape
    nt = t.shape[2]
    lanes = nt // (2 * groups)
    return pl.pallas_call(
        functools.partial(dipole_boundary_kernel, nblk),
        out_shape=(
            jax.ShapeDtypeStruct((groups, w + PAD, lanes), BF16),
            jax.ShapeDtypeStruct((groups, w, lanes), F32),
        ),
        in_specs=[SMEM, SMEM, VMEM, ANY, ANY, ANY, ANY, ANY, VMEM],
        out_specs=(VMEM, VMEM),
        scratch_shapes=[pltpu.VMEM((w, nt), F32)] + boundary_scratch(w, nt),
        compiler_params=params(),
        cost_estimate=cost(4 * BK * w * (KB * BK + nt), 8 * 2**20),
    )(core, off, acc, x, intra, inter, t, d, sq)


def halve_kernel(bit, keep, got, sq, send, kept, sq_out):
    half, w, _ = kept.shape
    total = sq[...] + get_squares(got, 0, w)
    sq_out[...] = total
    for g in range(half):
        here, there = bit[0] * half + g, (1 - bit[0]) * half + g
        kept[g] = keep[here] + got[here, 0:w, :].astype(F32)
        send[g, 0:w, :] = (keep[there] + got[there, 0:w, :].astype(F32)).astype(BF16)
        put_squares(send, g, total, w)


def halve(bit, keep, got, sq):
    groups, w, lanes = keep.shape
    half = groups // 2
    return pl.pallas_call(
        halve_kernel,
        out_shape=(
            jax.ShapeDtypeStruct((half, w + PAD, lanes), BF16),
            jax.ShapeDtypeStruct((half, w, lanes), F32),
            jax.ShapeDtypeStruct((1, w), F32),
        ),
        in_specs=[SMEM, VMEM, VMEM, VMEM],
        out_specs=(VMEM,) * 3,
        compiler_params=params(16),
    )(bit, keep, got, sq)


def finish_kernel(rows, keep, got, sq, out):
    w = keep.shape[1]
    total = sq[...] + get_squares(got, 0, w)
    norm = 1.0 / jnp.sqrt(total / rows + 1e-06)
    raw = keep[0] + got[0, 0:w, :].astype(F32)
    out[...] = (raw.T * norm).astype(BF16)


def finish(rows, keep, got, sq):
    _, w, lanes = keep.shape
    return pl.pallas_call(
        functools.partial(finish_kernel, rows),
        out_shape=jax.ShapeDtypeStruct((lanes, w), BF16),
        in_specs=[VMEM] * 3,
        out_specs=VMEM,
        compiler_params=params(16),
    )(keep, got, sq)


def swap(block, count, mask):
    return lax.ppermute(block, "basis", [(i, i ^ mask[i % 2]) for i in range(count)])


def meet(block, count):
    pairs = [(i, i + 1) for i in range(1, count - 1, 2)]
    return lax.ppermute(block, "basis", pairs + [(b, a) for a, b in pairs])


def on_device(cont_orbitals, target_orbitals, margin_blocks, dipole_blocks, band_offsets):
    count = lax.axis_size("basis")
    rows, w = cont_orbitals.shape
    nblk = rows // BK
    nt = target_orbitals.shape[1]
    chips = count // 2
    bits = chips.bit_length() - 1
    place = lax.axis_index("basis")
    core = lax.rem(place, 2)
    chip = lax.div(place, 2)
    core_s = core.astype(jnp.int32).reshape(1)
    off = band_offsets.astype(jnp.int32).T
    c = cont_orbitals.reshape(nblk, BK, w)
    t = target_orbitals.reshape(nblk, BK, nt)
    both = (1, 1)

    first, last = c[:2], c[nblk - 2 :]
    inter = meet(jnp.where(core == 0, first, last), count)
    intra = swap(jnp.where(core == 0, last, first), count, both)
    acc = project_interior(off, c, t, margin_blocks)
    send, keep = project_boundary(core_s, off, acc, c, intra, inter, t, margin_blocks)

    part = (keep + swap(send, count, both).astype(F32)).astype(BF16)
    orders = [chip_order(bits, side) for side in (0, 1)]
    for s in range(bits):
        got = swap(part, count, (2 << orders[0][s], 2 << orders[1][s]))
        part = (part.astype(F32) + got.astype(F32)).astype(BF16)
    other = swap(part, count, both)

    edge, intra_send, inter_send, sq = orth_edges(core_s, part, other, c, t)
    inter = meet(inter_send, count)
    intra = swap(intra_send, count, both)
    x, acc, sq = orth_dipole_interior(
        core_s, off, part, other, c, t, dipole_blocks, edge, sq
    )
    send, keep = dipole_boundary(
        core_s, off, acc, x, intra, inter, t, dipole_blocks, sq, chips
    )
    got = swap(send, count, both)
    for s in range(bits):
        which = jnp.where(core == 0, orders[0][s], orders[1][s])
        bit = jnp.bitwise_and(jnp.right_shift(chip, which), 1).astype(jnp.int32).reshape(1)
        send, keep, sq = halve(bit, keep, got, sq)
        got = swap(send, count, (2 << orders[0][s], 2 << orders[1][s]))
    dipole_mo = finish(rows * count, keep, got, sq)
    return (x.reshape(rows, w), dipole_mo)


def solution(mesh):
    return jax.shard_map(
        on_device,
        mesh=mesh,
        in_specs=(
            P("basis", "orb"),
            P("basis", None),
            P("basis", None, None, None),
            P("basis", None, None, None),
            P("basis", None),
        ),
        out_specs=(P("basis", "orb"), P("basis", "orb")),
        check_vma=False,
    )
```

time: 305 us -> 90.4 us (0.30)
  matrix products: 91.9 us -> 0 us
  blocking collectives: 87.3 us -> 0 us
  local copies, waits for them, and re-layouts: 65 us -> 5.05 us
  Pallas kernels: 0 us -> 37.9 us
  between operations: 14.2 us -> 0.8 us
  other arithmetic: 14.2 us -> 1.79 us
  starting transfers between devices: 6.33 us -> 16.5 us
    dot_general x11 -> x0, matrix products: 91.9 us -> none  [the longest x8 63.9 us: band_local(): jnp.einsum('bij,bjc->bic', blocks[:, k], taken, preferred_element_type=jn...]
    psum x2 -> x0, blocking collectives: 87.3 us -> none  [the longest x1 63.9 us: on_device(): projection = lax.psum(partial_proj, 'basis')]
    gather x8 -> x0, local copies, waits for them, and re-layouts: 42.1 us -> none  [band_local(): taken = stacked[index]]
    pallas_call x0 -> x8, Pallas kernels: none -> 37.9 us  [the longest x1 14 us: orth_dipole_interior(): pl.pallas_call(functools.partial(orth_dipole_kernel, nblk), out_shape=(ja...]
    ppermute x4 -> x11, waiting for transfers between devices: 2.51 us -> 28.1 us  [the longest x9 28 us: swap(): lax.ppermute(block, 'basis', [(i, i ^ mask[i % 2]) for i in range(count)])]
    reduce_scatter x1 -> x0, waiting for transfers between devices: 22.7 us -> none  [on_device(): lax.psum_scatter(lax.dot_general(target_orbitals, dipole_cont, (((0,), (0...]
    concatenate x2 -> x0, other arithmetic: 13.1 us -> none  [padded_2(): block = jnp.concatenate([low, block, high], axis=dim)]
    ppermute x4 -> x11, starting transfers between devices: 6.3 us -> 16.5 us  [the longest x9 15 us: swap(): lax.ppermute(block, 'basis', [(i, i ^ mask[i % 2]) for i in range(count)])]
  transfers between devices with their start and end apart: 5 -> 11, of which waited for: 3 -> 7; matrix products, arithmetic and copies ran while one was open for 4% -> 0% of each run, Pallas kernels for 0% -> 27%
where the time goes in v1:
time: 90.4 us; the launch traced here: 90.1 us
  Pallas kernels  37.9 us (42%)
  waiting for transfers between devices  28.1 us (31%)
  starting transfers between devices  16.5 us (18%)
  local copies, waits for them, and re-layouts  5.05 us (6%)
  other arithmetic  1.79 us (2%)
    ppermute x9, waiting for transfers between devices, swap(): lax.ppermute(block, 'basis', [(i, i ^ mask[i % 2]) for i in range(count)])  28 us
    ppermute x9, starting transfers between devices, swap(): lax.ppermute(block, 'basis', [(i, i ^ mask[i % 2]) for i in range(count)])  15 us
    pallas_call x1, Pallas kernels, orth_dipole_interior(): pl.pallas_call(functools.partial(orth_dipole_kernel, nblk), out_shape=(ja...  14 us
    pallas_call x1, Pallas kernels, project_interior(): pl.pallas_call(functools.partial(interior_kernel, nblk), out_shape=jax.Sh...  10.1 us
    unnamed x8, local copies, waits for them, and re-layouts  5.05 us
    pallas_call x1, Pallas kernels, project_boundary(): pl.pallas_call(functools.partial(boundary_kernel, nblk), out_shape=(jax.S...  4.8 us
    pallas_call x1, Pallas kernels, dipole_boundary(): pl.pallas_call(functools.partial(dipole_boundary_kernel, nblk), out_shape...  4.68 us
    pallas_call x1, Pallas kernels, orth_edges(): pl.pallas_call(functools.partial(edge_kernel, nblk), out_shape=(jax.Shape...  3.37 us
  transfers between devices with their start and end apart: 11, of which 7 were waited for; matrix products, arithmetic and copies ran while one was open for 0% of the time, Pallas kernels for 27%

profile of v1, /device:TPU:0, one launch (start us, length us, event | category | flops | bytes accessed | tf_op | source)
XLA Modules:
  0.0 90.1 jit_solution(2845376034206293427)
XLA Ops:
  0.6 1.3 %broadcast_select_fusion = (bf16[512,512]{1,0:T(8,128)(2,1)S(1)}, bf16[512,512]{1,0:T(8,128)(2,1)S(1)}) fusion(pred[]{:T(512)S(6)} %eq.2, bf16[4096,512]{1,0:T(8,128)(2,1)} %param.5), kind=kLoop, calls=%fused_computation.3 | loop fusion | flops 524288 | bytes 2097153 | tf_op jit(solution)/shard_map/jit(_where)/select_n | solution.py:462
  1.9 0.5 collective-permute-start
  2.4 0.7 collective-permute-start.1
  3.1 2.2 %copy-done = bf16[4096,512]{1,0:T(8,128)(2,1)S(1)} copy-done((bf16[4096,512]{1,0:T(8,128)(2,1)S(1)}, bf16[4096,512]{1,0:T(8,128)(2,1)}, u32[]{:S(2)}) %copy-start) | copy-done | bytes 4194328
  5.3 0.7 copy-done.2
  6.0 10.1 %shard_map.68.acc = f32[512,1024]{1,0:T(8,128)S(1)} custom-call(s32[4,16]{1,0:T(4,128)S(1)} %bitcast.14, bf16[16,256,512]{2,1,0:T(8,128)(2,1)S(1)} %bitcast.9, bf16[16,256,1024]{2,1,0:T(8,128)(2,1)} %bitcast.18, bf16[16,4,256,256]{3,2,1,0:T(8,128)(2,1)} %m.3), custom_call_target="tpu_custom_call" | custom-call | flops 6442450944 | bytes 20971520 | tf_op jit(solution)/shard_map/pallas_call | solution.py:106
  16.2 4.8 %shard_map.69 = (bf16[256,1024]{1,0:T(8,128)(2,1)S(1)}, f32[256,1024]{1,0:T(8,128)S(1)}) custom-call(s32[1]{0:T(128)} %bitcast.core, s32[4,16]{1,0:T(4,128)S(1)} %bitcast.15, f32[512,1024]{1,0:T(8,128)S(1)} %shard_map.68.acc, bf16[16,256,512]{2,1,0:T(8,128)(2,1)S(1)} %bitcast.10, bf16[2,256,512]{2,1,0:T(8,128)(2,1)S(1)} %collective-permute-done.intra, ...), custom_call_target="tpu_custom_call" | custom-call | flops 2147483648 | bytes 8388608 | tf_op jit(solution)/shard_map/pallas_call | solution.py:169
  21.0 3.9 %collective-permute-start.2 = (bf16[256,1024]{1,0:T(8,128)(2,1)S(1)}, bf16[256,1024]{1,0:T(8,128)(2,1)S(1)}, u32[]{:S(2)}, u32[]{:S(2)}) collective-permute-start(bf16[256,1024]{1,0:T(8,128)(2,1)S(1)} %get-tuple-element.20), channel_id=1, source_target_pairs={{0,4},{4,0},{8,12},{12,8},{16,20},{20,16},{24,28},{28,24},{1,5},{5... | collective-permute-start | bytes 1572872 | tf_op jit(solution)/shard_map/ppermute | solution.py:437
  24.9 1.5 %collective-permute-done.2 = bf16[256,1024]{1,0:T(8,128)(2,1)S(1)} collective-permute-done((bf16[256,1024]{1,0:T(8,128)(2,1)S(1)}, bf16[256,1024]{1,0:T(8,128)(2,1)S(1)}, u32[]{:S(2)}, u32[]{:S(2)}) %collective-permute-start.2) | collective-permute-done | bytes 524320 | tf_op jit(solution)/shard_map/ppermute | solution.py:437
  26.4 0.1 add_convert_fusion.2
  26.6 1.9 %collective-permute-start.3 = (bf16[256,1024]{1,0:T(8,128)(2,1)S(1)}, bf16[256,1024]{1,0:T(8,128)(2,1)S(1)}, u32[]{:S(2)}, u32[]{:S(2)}) collective-permute-start(bf16[256,1024]{1,0:T(8,128)(2,1)S(1)} %add_convert_fusion.2), channel_id=1, source_target_pairs={{0,8},{4,20},{8,0},{12,28},{16,24},{20,4},{24,16},{28,12},{1,9},{5... | collective-permute-start | bytes 1572872 | tf_op jit(solution)/shard_map/ppermute | solution.py:437
  28.5 7.4 %collective-permute-done.3 = bf16[256,1024]{1,0:T(8,128)(2,1)S(1)} collective-permute-done((bf16[256,1024]{1,0:T(8,128)(2,1)S(1)}, bf16[256,1024]{1,0:T(8,128)(2,1)S(1)}, u32[]{:S(2)}, u32[]{:S(2)}) %collective-permute-start.3) | collective-permute-done | bytes 524320 | tf_op jit(solution)/shard_map/ppermute | solution.py:437
  35.8 0.2 add_convert_fusion.1
  36.0 1.9 %collective-permute-start.4 = (bf16[256,1024]{1,0:T(8,128)(2,1)S(1)}, bf16[256,1024]{1,0:T(8,128)(2,1)S(1)}, u32[]{:S(2)}, u32[]{:S(2)}) collective-permute-start(bf16[256,1024]{1,0:T(8,128)(2,1)S(1)} %add_convert_fusion.1), channel_id=1, source_target_pairs={{0,16},{4,12},{8,24},{12,4},{16,0},{20,28},{24,8},{28,20},{1,17},{... | collective-permute-start | bytes 1572872 | tf_op jit(solution)/shard_map/ppermute | solution.py:437
  37.9 7.4 %collective-permute-done.4 = bf16[256,1024]{1,0:T(8,128)(2,1)S(1)} collective-permute-done((bf16[256,1024]{1,0:T(8,128)(2,1)S(1)}, bf16[256,1024]{1,0:T(8,128)(2,1)S(1)}, u32[]{:S(2)}, u32[]{:S(2)}) %collective-permute-start.4) | collective-permute-done | bytes 524320 | tf_op jit(solution)/shard_map/ppermute | solution.py:437
  45.2 0.2 add_convert_fusion.mine
  45.4 0.1 collective-permute-start.5
  45.5 1.9 %collective-permute-done.5.other = bf16[256,1024]{1,0:T(8,128)(2,1)S(1)} collective-permute-done((bf16[256,1024]{1,0:T(8,128)(2,1)S(1)}, bf16[256,1024]{1,0:T(8,128)(2,1)S(1)}, u32[]{:S(2)}, u32[]{:S(2)}) %collective-permute-start.5) | collective-permute-done | bytes 524320 | tf_op jit(solution)/shard_map/ppermute | solution.py:437
  47.4 3.4 %shard_map.70 = (bf16[4,256,512]{2,1,0:T(8,128)(2,1)S(1)}, bf16[2,256,512]{2,1,0:T(8,128)(2,1)S(1)}, bf16[2,256,512]{2,1,0:T(8,128)(2,1)S(1)}, f32[1,512]{1,0:T(1,128)S(1)}) custom-call(s32[1]{0:T(128)} %bitcast.core, bf16[256,1024]{1,0:T(8,128)(2,1)S(1)} %add_convert_fusion.mine, bf16[256,1024]{1,0:T(8,128)(2,1)S(1)} %collective-permute-done.5.other, ...), custom_call_target="tpu_custom_call" | custom-call | flops 1073741824 | bytes 4194304 | tf_op jit(solution)/shard_map/pallas_call | solution.py:231
  50.8 0.2 collective-permute-start.6
  51.0 0.9 collective-permute-start.7
  51.9 14.0 %shard_map.71 = (bf16[16,256,512]{2,1,0:T(8,128)(2,1)}, f32[512,1024]{1,0:T(8,128)S(1)}, f32[1,512]{1,0:T(1,128)S(1)}) custom-call(s32[1]{0:T(128)} %bitcast.core, s32[4,16]{1,0:T(4,128)S(1)} %bitcast.16, bf16[256,1024]{1,0:T(8,128)(2,1)S(1)} %add_convert_fusion.mine, bf16[256,1024]{1,0:T(8,128)(2,1)S(1)} %collective-permute-done.5.other, ...), custom_call_target="tpu_custom_call" | custom-call | flops 9663676416 | bytes 25165824 | tf_op jit(solution)/shard_map/pallas_call | solution.py:304
  65.9 2.2 %copy-done.1 = bf16[16,256,512]{2,1,0:T(8,128)(2,1)S(1)} copy-done((bf16[16,256,512]{2,1,0:T(8,128)(2,1)S(1)}, bf16[16,256,512]{2,1,0:T(8,128)(2,1)}, u32[]{:S(2)}) %copy-start.1) | copy-done | bytes 4194328
  68.1 4.7 %shard_map.72 = (bf16[4,528,128]{2,1,0:T(8,128)(2,1)S(1)}, f32[4,512,128]{2,1,0:T(8,128)S(1)}) custom-call(s32[1]{0:T(128)} %bitcast.core, s32[4,16]{1,0:T(4,128)S(1)} %bitcast.17, f32[512,1024]{1,0:T(8,128)S(1)} %get-tuple-element.24.acc, bf16[16,256,512]{2,1,0:T(8,128)(2,1)S(1)} %copy-done.1, bf16[2,256,512]{2,1,0:T(8,128)(2,1)S(1)} %collective-permute-done.6.intra, ...), custom_call_target="tpu_custom_call" | custom-call | flops 2147483648 | bytes 8388608 | tf_op jit(solution)/shard_map/pallas_call | solution.py:376
  72.8 3.2 %collective-permute-start.8 = (bf16[4,528,128]{2,1,0:T(8,128)(2,1)S(1)}, bf16[4,528,128]{2,1,0:T(8,128)(2,1)S(1)}, u32[]{:S(2)}, u32[]{:S(2)}) collective-permute-start(bf16[4,528,128]{2,1,0:T(8,128)(2,1)S(1)} %get-tuple-element.29), channel_id=1, source_target_pairs={{0,4},{4,0},{8,12},{12,8},{16,20},{20,16},{24,28},{28,24},{1,5},{5... | collective-permute-start | bytes 1622024 | tf_op jit(solution)/shard_map/ppermute | solution.py:437
  76.0 1.6 %collective-permute-done.8.got = bf16[4,528,128]{2,1,0:T(8,128)(2,1)S(1)} collective-permute-done((bf16[4,528,128]{2,1,0:T(8,128)(2,1)S(1)}, bf16[4,528,128]{2,1,0:T(8,128)(2,1)S(1)}, u32[]{:S(2)}, u32[]{:S(2)}) %collective-permute-start.8) | collective-permute-done | bytes 540704 | tf_op jit(solution)/shard_map/ppermute | solution.py:437
  77.5 0.1 shard_map.73
  77.7 1.5 %collective-permute-start.9 = (bf16[2,528,128]{2,1,0:T(8,128)(2,1)S(1)}, bf16[2,528,128]{2,1,0:T(8,128)(2,1)S(1)}, u32[]{:S(2)}, u32[]{:S(2)}) collective-permute-start(bf16[2,528,128]{2,1,0:T(8,128)(2,1)S(1)} %get-tuple-element.31), channel_id=1, source_target_pairs={{0,8},{4,20},{8,0},{12,28},{16,24},{20,4},{24,16},{28,12},{1,9},{5... | collective-permute-start | bytes 811016 | tf_op jit(solution)/shard_map/ppermute | solution.py:437
  79.2 5.0 %collective-permute-done.9.got = bf16[2,528,128]{2,1,0:T(8,128)(2,1)S(1)} collective-permute-done((bf16[2,528,128]{2,1,0:T(8,128)(2,1)S(1)}, bf16[2,528,128]{2,1,0:T(8,128)(2,1)S(1)}, u32[]{:S(2)}, u32[]{:S(2)}) %collective-permute-start.9) | collective-permute-done | bytes 270368 | tf_op jit(solution)/shard_map/ppermute | solution.py:437
  84.2 1.8 %collective-permute-start.10 = (bf16[1,528,128]{2,1,0:T(8,128)(2,1)S(1)}, bf16[1,528,128]{2,1,0:T(8,128)(2,1)S(1)}, u32[]{:S(2)}, u32[]{:S(2)}) collective-permute-start(bf16[1,528,128]{2,1,0:T(8,128)(2,1)S(1)} %get-tuple-element.34), channel_id=1, source_target_pairs={{0,16},{4,12},{8,24},{12,4},{16,0},{20,28},{24,8},{28,20},{1,17},{... | collective-permute-start | bytes 405512 | tf_op jit(solution)/shard_map/ppermute | solution.py:437
  86.0 3.3 %collective-permute-done.10.got = bf16[1,528,128]{2,1,0:T(8,128)(2,1)S(1)} collective-permute-done((bf16[1,528,128]{2,1,0:T(8,128)(2,1)S(1)}, bf16[1,528,128]{2,1,0:T(8,128)(2,1)S(1)}, u32[]{:S(2)}, u32[]{:S(2)}) %collective-permute-start.10) | collective-permute-done | bytes 135200 | tf_op jit(solution)/shard_map/ppermute | solution.py:437
  89.3 0.8 shard_map.75
  (10 shorter events, 0.1 us)
Async XLA Ops:
  1.9 14.2 %collective-permute-start = (bf16[2,256,512]{2,1,0:T(8,128)(2,1)S(1)}, bf16[2,256,512]{2,1,0:T(8,128)(2,1)S(1)}, u32[]{:S(2)}, u32[]{:S(2)}) collective-permute-start(bf16[2,256,512]{2,1,0:T(8,128)(2,1)S(1)} %bitcast.24), channel_id=1, source_target_pairs={{0,4},{4,0},{8,12},{12,8},{16,20},{20,16},{24,28},{28,24},{1,5},{5... | collective-permute-start | bytes 1572872 | tf_op jit(solution)/shard_map/ppermute | solution.py:437
  2.4 13.7 %collective-permute-start.1 = (bf16[2,256,512]{2,1,0:T(8,128)(2,1)S(1)}, bf16[2,256,512]{2,1,0:T(8,128)(2,1)S(1)}, u32[]{:S(2)}, u32[]{:S(2)}) collective-permute-start(bf16[2,256,512]{2,1,0:T(8,128)(2,1)S(1)} %bitcast.23), channel_id=1, source_target_pairs={{4,8},{12,16},{20,24},{8,4},{16,12},{24,20},{5,9},{13,17},{21,25},... | collective-permute-start | bytes 1572872 | tf_op jit(solution)/shard_map/ppermute | solution.py:442
  3.1 2.2 %copy-start = (bf16[4096,512]{1,0:T(8,128)(2,1)S(1)}, bf16[4096,512]{1,0:T(8,128)(2,1)}, u32[]{:S(2)}) copy-start(bf16[4096,512]{1,0:T(8,128)(2,1)} %param.5) | copy-start | bytes 12582916
  5.3 0.7 copy-start.2
  6.0 10.2 %copy-start.3 = (s32[16,4]{0,1:T(4,128)S(1)}, s32[16,4]{0,1:T(4,128)}, u32[]{:S(2)}) copy-start(s32[16,4]{0,1:T(4,128)} %param.9) | copy-start | bytes 772
  21.0 5.4 %collective-permute-start.2 = (bf16[256,1024]{1,0:T(8,128)(2,1)S(1)}, bf16[256,1024]{1,0:T(8,128)(2,1)S(1)}, u32[]{:S(2)}, u32[]{:S(2)}) collective-permute-start(bf16[256,1024]{1,0:T(8,128)(2,1)S(1)} %get-tuple-element.20), channel_id=1, source_target_pairs={{0,4},{4,0},{8,12},{12,8},{16,20},{20,16},{24,28},{28,24},{1,5},{5... | collective-permute-start | bytes 1572872 | tf_op jit(solution)/shard_map/ppermute | solution.py:437
  26.6 9.2 %collective-permute-start.3 = (bf16[256,1024]{1,0:T(8,128)(2,1)S(1)}, bf16[256,1024]{1,0:T(8,128)(2,1)S(1)}, u32[]{:S(2)}, u32[]{:S(2)}) collective-permute-start(bf16[256,1024]{1,0:T(8,128)(2,1)S(1)} %add_convert_fusion.2), channel_id=1, source_target_pairs={{0,8},{4,20},{8,0},{12,28},{16,24},{20,4},{24,16},{28,12},{1,9},{5... | collective-permute-start | bytes 1572872 | tf_op jit(solution)/shard_map/ppermute | solution.py:437
  36.0 9.2 %collective-permute-start.4 = (bf16[256,1024]{1,0:T(8,128)(2,1)S(1)}, bf16[256,1024]{1,0:T(8,128)(2,1)S(1)}, u32[]{:S(2)}, u32[]{:S(2)}) collective-permute-start(bf16[256,1024]{1,0:T(8,128)(2,1)S(1)} %add_convert_fusion.1), channel_id=1, source_target_pairs={{0,16},{4,12},{8,24},{12,4},{16,0},{20,28},{24,8},{28,20},{1,17},{... | collective-permute-start | bytes 1572872 | tf_op jit(solution)/shard_map/ppermute | solution.py:437
  45.4 2.0 %collective-permute-start.5 = (bf16[256,1024]{1,0:T(8,128)(2,1)S(1)}, bf16[256,1024]{1,0:T(8,128)(2,1)S(1)}, u32[]{:S(2)}, u32[]{:S(2)}) collective-permute-start(bf16[256,1024]{1,0:T(8,128)(2,1)S(1)} %add_convert_fusion.mine), channel_id=1, source_target_pairs={{0,4},{4,0},{8,12},{12,8},{16,20},{20,16},{24,28},{28,24},{1,5},{5... | collective-permute-start | bytes 1572872 | tf_op jit(solution)/shard_map/ppermute | solution.py:437
  50.8 15.1 %collective-permute-start.6 = (bf16[2,256,512]{2,1,0:T(8,128)(2,1)S(1)}, bf16[2,256,512]{2,1,0:T(8,128)(2,1)S(1)}, u32[]{:S(2)}, u32[]{:S(2)}) collective-permute-start(bf16[2,256,512]{2,1,0:T(8,128)(2,1)S(1)} %get-tuple-element.25), channel_id=1, source_target_pairs={{0,4},{4,0},{8,12},{12,8},{16,20},{20,16},{24,28},{28,24},{1,5},{5... | collective-permute-start | bytes 1572872 | tf_op jit(solution)/shard_map/ppermute | solution.py:437
  51.0 14.9 %collective-permute-start.7 = (bf16[2,256,512]{2,1,0:T(8,128)(2,1)S(1)}, bf16[2,256,512]{2,1,0:T(8,128)(2,1)S(1)}, u32[]{:S(2)}, u32[]{:S(2)}) collective-permute-start(bf16[2,256,512]{2,1,0:T(8,128)(2,1)S(1)} %get-tuple-element.26), channel_id=1, source_target_pairs={{4,8},{12,16},{20,24},{8,4},{16,12},{24,20},{5,9},{13,17},{21,25},... | collective-permute-start | bytes 1572872 | tf_op jit(solution)/shard_map/ppermute | solution.py:442
  65.9 2.2 %copy-start.1 = (bf16[16,256,512]{2,1,0:T(8,128)(2,1)S(1)}, bf16[16,256,512]{2,1,0:T(8,128)(2,1)}, u32[]{:S(2)}) copy-start(bf16[16,256,512]{2,1,0:T(8,128)(2,1)} %get-tuple-element.23.x) | copy-start | bytes 12582916
  72.8 4.8 %collective-permute-start.8 = (bf16[4,528,128]{2,1,0:T(8,128)(2,1)S(1)}, bf16[4,528,128]{2,1,0:T(8,128)(2,1)S(1)}, u32[]{:S(2)}, u32[]{:S(2)}) collective-permute-start(bf16[4,528,128]{2,1,0:T(8,128)(2,1)S(1)} %get-tuple-element.29), channel_id=1, source_target_pairs={{0,4},{4,0},{8,12},{12,8},{16,20},{20,16},{24,28},{28,24},{1,5},{5... | collective-permute-start | bytes 1622024 | tf_op jit(solution)/shard_map/ppermute | solution.py:437
  77.7 6.5 %collective-permute-start.9 = (bf16[2,528,128]{2,1,0:T(8,128)(2,1)S(1)}, bf16[2,528,128]{2,1,0:T(8,128)(2,1)S(1)}, u32[]{:S(2)}, u32[]{:S(2)}) collective-permute-start(bf16[2,528,128]{2,1,0:T(8,128)(2,1)S(1)} %get-tuple-element.31), channel_id=1, source_target_pairs={{0,8},{4,20},{8,0},{12,28},{16,24},{20,4},{24,16},{28,12},{1,9},{5... | collective-permute-start | bytes 811016 | tf_op jit(solution)/shard_map/ppermute | solution.py:437
  84.2 5.1 %collective-permute-start.10 = (bf16[1,528,128]{2,1,0:T(8,128)(2,1)S(1)}, bf16[1,528,128]{2,1,0:T(8,128)(2,1)S(1)}, u32[]{:S(2)}, u32[]{:S(2)}) collective-permute-start(bf16[1,528,128]{2,1,0:T(8,128)(2,1)S(1)} %get-tuple-element.34), channel_id=1, source_target_pairs={{0,16},{4,12},{8,24},{12,4},{16,0},{20,28},{24,8},{28,20},{1,17},{... | collective-permute-start | bytes 405512 | tf_op jit(solution)/shard_map/ppermute | solution.py:437

commit v2 on v0

v2 whole, which is shorter than its diff:
```python
import functools

import jax
import jax.numpy as jnp
from jax import lax
from jax.experimental import pallas as pl
from jax.experimental.pallas import tpu as pltpu
from jax.sharding import PartitionSpec as P

BK = 256
KB = 4
F32 = jnp.float32
BF16 = jnp.bfloat16
ANY = pl.BlockSpec(memory_space=pl.ANY)
VMEM = pl.BlockSpec(memory_space=pltpu.VMEM)
SMEM = pl.BlockSpec(memory_space=pltpu.SMEM)


def core_of(place):
    return jnp.bitwise_and(place[0], 1)


def stay(x):
    return pltpu.with_memory_space_constraint(x, pltpu.HBM)


def params(mib=40):
    return pltpu.CompilerParams(vmem_limit_bytes=mib * 2**20)


def cost(macs, data):
    return pl.CostEstimate(flops=2 * macs, bytes_accessed=data, transcendentals=0)


def dot(a, b, dims=((1,), (0,))):
    return lax.dot_general(a, b, (dims, ((), ())), preferred_element_type=F32)


class Loads:
    def __init__(self, sems, ahead=64):
        self.sems, self.ahead = sems, ahead
        self.copies, self.started, self.done = [], 0, set()

    def start(self, src, dst):
        self.copies.append(pltpu.make_async_copy(src, dst, self.sems.at[len(self.copies)]))
        self.go()
        return len(self.copies) - 1

    def go(self):
        while self.started < min(len(self.copies), len(self.done) + self.ahead):
            self.copies[self.started].start()
            self.started += 1

    def wait(self, *which):
        for i in which:
            if i not in self.done:
                self.copies[i].wait()
                self.done.add(i)
                self.go()

    def wait_all(self):
        self.wait(*range(len(self.copies)))


def band_rows(rows, slots, off, field, cols, blocks, base, ys):
    for r, (b, slot) in enumerate(zip(rows, slots)):
        total = None
        for k in range(KB):
            term = dot(blocks[slot, k], field[b + off[k, b] + base, :, 0:cols])
            total = term if total is None else total + term
        ys[r * BK : (r + 1) * BK, :] = total.astype(BF16)


def groups_of(nblk):
    inner = list(range(2, nblk - 2))
    return [inner[i : i + 4] for i in range(0, len(inner), 4)]


def project(out, acc, ys, t_v, lo, count):
    size = count * BK
    t = t_v[lo : lo + count].reshape(size, -1)
    for at in range(0, out.shape[0], BK):
        here = slice(at, min(at + BK, out.shape[0]))
        piece = dot(ys[0:size, here], t, ((0,), (0,)))
        out[here, :] = piece if acc is None else acc[here, :] + piece


def columns(z, width):
    return pl.ds(pl.multiple_of(z * width, width), width)


def held(x):
    return pltpu.with_memory_space_constraint(x, pltpu.VMEM)


def edge_kernel(place, z, c, t, intra, inter, sems):
    last = c.shape[0] - 2
    w = c.shape[2]
    zc = intra.shape[2] - w
    loads = Loads(sems)
    for out, at in ((intra, (1 - core_of(place)) * last), (inter, core_of(place) * last)):
        loads.start(c.at[pl.ds(at, 2)], out.at[:, :, 0:w])
        loads.start(t.at[pl.ds(at, 2), :, columns(z[0], zc)], out.at[:, :, w : w + zc])
    loads.wait_all()


def edges(place, z, c, t, zc):
    _, _, w = c.shape
    pair = jax.ShapeDtypeStruct((2, BK, w + zc), BF16)
    return pl.pallas_call(
        edge_kernel,
        out_shape=(pair, pair),
        in_specs=[SMEM, SMEM, ANY, ANY],
        out_specs=(VMEM, VMEM),
        scratch_shapes=[pltpu.SemaphoreType.DMA((4,))],
        compiler_params=params(8),
    )(place, z, stay(c), stay(t))


def lead_of(nblk):
    groups = groups_of(nblk)
    cut = max(1, len(groups) - 1)
    return groups[:cut], groups[cut:]


def first_kernel(
    nblk, z, off, c, t, m, d, p_out, r_out, f, t_v, m_edge, m_v, d_v, ys, yd, sems
):
    w = c.shape[2]
    zc = f.shape[2] - w
    loads = Loads(sems, 8)
    groups = groups_of(nblk)
    lead, _ = lead_of(nblk)
    have, z_have, needs = 0, 0, []
    for g, rows in enumerate(groups):
        lo, hi = rows[0], rows[-1] + 1
        mid = min(lo + 2, hi)
        want = []
        for part in ((lo, mid), (mid, hi)):
            if part[0] == part[1]:
                continue
            upto = part[1] + 2
            ids = []
            if upto > have:
                ids.append(loads.start(c.at[have:upto], f.at[have:upto, :, 0:w]))
                have = upto
            ids.append(
                loads.start(m.at[part[0] : part[1]], m_v.at[part[0] - 2 : part[1] - 2])
            )
            want.append((list(range(*part)), ids))
        t_id = loads.start(t.at[lo:hi], t_v.at[lo:hi])
        d_ids = ()
        if g < len(lead):
            upto = hi + 2
            d_ids = (
                loads.start(d.at[lo:hi], d_v.at[lo - 2 : hi - 2]),
                loads.start(
                    t.at[z_have:upto, :, columns(z[0], zc)], f.at[z_have:upto, :, w : w + zc]
                ),
            )
            z_have = upto
        needs.append((rows, want, t_id, d_ids))
    if z_have < nblk:
        loads.start(t.at[z_have:nblk, :, columns(z[0], zc)], f.at[z_have:nblk, :, w : w + zc])
    for side, at in ((0, 0), (1, nblk - 2)):
        loads.start(t.at[at : at + 2], t_v.at[at : at + 2])
        loads.start(m.at[at : at + 2], m_edge.at[2 * side : 2 * side + 2])
    for g, (rows, want, t_id, d_ids) in enumerate(needs):
        at = 0
        for part, ids in want:
            loads.wait(*ids)
            band_rows(
                part, [b - 2 for b in part], off, f, w, m_v, 0,
                ys.at[at * BK : (at + len(part)) * BK],
            )
            at += len(part)
        loads.wait(t_id)
        project(p_out, None if g == 0 else p_out, ys, t_v, rows[0], len(rows))
        if d_ids:
            loads.wait(*d_ids)
            band_rows(rows, [b - 2 for b in rows], off, f, w + zc, d_v, 0, yd)
            project(r_out, None if g == 0 else r_out, yd, t_v, rows[0], len(rows))
    loads.ahead = 64
    loads.go()
    loads.wait_all()


def first(z, off, c, t, m, d, zc):
    nblk, _, w = c.shape
    nt = t.shape[2]
    inner = nblk - 4
    count = sum(map(len, lead_of(nblk)[0]))
    macs = inner * BK * w * (KB * BK + nt) + count * BK * (w + zc) * (KB * BK + nt)
    return pl.pallas_call(
        functools.partial(first_kernel, nblk),
        out_shape=(
            pltpu.VMEM((w, nt), F32),
            pltpu.VMEM((w + zc, nt), F32),
            pltpu.VMEM((nblk, BK, w + zc), BF16),
            pltpu.VMEM((nblk, BK, nt), BF16),
            pltpu.VMEM((4, KB, BK, BK), BF16),
        ),
        in_specs=[SMEM, SMEM, ANY, ANY, ANY, ANY],
        out_specs=(VMEM,) * 5,
        scratch_shapes=[
            pltpu.VMEM((inner, KB, BK, BK), BF16),
            pltpu.VMEM((count, KB, BK, BK), BF16),
            pltpu.VMEM((4 * BK, w), BF16),
            pltpu.VMEM((4 * BK, w + zc), BF16),
            pltpu.SemaphoreType.DMA((7 * len(groups_of(nblk)) + 5,)),
        ],
        compiler_params=params(17),
        cost_estimate=cost(macs, 30 * 2**20),
    )(z, off, stay(c), stay(t), stay(m), stay(d))


def boundary_start(nblk, core, f, intra, inter, f_v, sems):
    loads = Loads(sems)
    cols = f_v.shape[2]
    low = 10 * (1 - core)
    loads.start(intra.at[:, :, 0:cols], f_v.at[pl.ds(low, 2)])
    loads.start(inter.at[:, :, 0:cols], f_v.at[pl.ds(10 - low, 2)])
    loads.start(f.at[0:4, :, 0:cols], f_v.at[2:6])
    loads.start(f.at[nblk - 4 : nblk, :, 0:cols], f_v.at[6:10])
    return loads


def boundary_rows(nblk, loads, off, blocks, f_v, ys):
    cols = f_v.shape[2]
    loads.wait(0, 1, 2)
    band_rows([0, 1], [0, 1], off, f_v, cols, blocks, 2, ys.at[0 : 2 * BK])
    loads.wait(3)
    band_rows(
        [nblk - 2, nblk - 1], [2, 3], off, f_v, cols, blocks, 10 - nblk, ys.at[2 * BK : 4 * BK]
    )


def boundary_sum(acc, ys, t, here):
    nblk = t.shape[0]
    ends = ((0,), (0,))
    low = dot(ys[0 : 2 * BK, here], t[0:2].reshape(2 * BK, -1), ends)
    high = dot(ys[2 * BK : 4 * BK, here], t[nblk - 2 : nblk].reshape(2 * BK, -1), ends)
    return acc[here, :] + (low + high)


def boundary_scratch(cols):
    return [
        pltpu.VMEM((12, BK, cols), BF16),
        pltpu.VMEM((4 * BK, cols), BF16),
        pltpu.SemaphoreType.DMA((4,)),
    ]


def boundary_kernel(
    nblk, place, off, acc, f, intra, inter, t, m, d, send, keep, d_edge, d_rest, f_v, ys, sems, d_sems
):
    near = boundary_start(nblk, core_of(place), f, intra, inter, f_v, sems)
    loads = Loads(d_sems)
    _, rest = lead_of(nblk)
    if rest:
        loads.start(d.at[rest[0][0] : rest[-1][-1] + 1], d_rest)
    for side, at in ((0, 0), (1, nblk - 2)):
        loads.start(d.at[at : at + 2], d_edge.at[2 * side : 2 * side + 2])
    half = send.shape[0]
    boundary_rows(nblk, near, off, m, f_v, ys)
    here = pl.ds(pl.multiple_of(core_of(place) * half, half), half)
    there = pl.ds(pl.multiple_of((1 - core_of(place)) * half, half), half)
    send[...] = boundary_sum(acc, ys, t, there).astype(BF16)
    keep[...] = boundary_sum(acc, ys, t, here)
    loads.wait_all()


def project_boundary(place, off, acc, f, intra, inter, t, m, d):
    nblk, _, nt = t.shape
    w = acc.shape[0]
    others = sum(map(len, lead_of(nblk)[1]))
    return pl.pallas_call(
        functools.partial(boundary_kernel, nblk),
        out_shape=(
            jax.ShapeDtypeStruct((w // 2, nt), BF16),
            jax.ShapeDtypeStruct((w // 2, nt), F32),
            pltpu.VMEM((4, KB, BK, BK), BF16),
            pltpu.VMEM((max(others, 1), KB, BK, BK), BF16),
        ),
        in_specs=[SMEM, SMEM] + [VMEM] * 6 + [ANY],
        out_specs=(VMEM,) * 4,
        scratch_shapes=boundary_scratch(w) + [pltpu.SemaphoreType.DMA((3,))],
        compiler_params=params(10),
        cost_estimate=cost(4 * BK * w * (KB * BK + nt), 8 * 2**20),
    )(place, off, held(acc), held(f), intra, inter, held(t), held(m), stay(d))


def merge_kernel(passed, a, b, out, passed_on):
    out[...] = (a[...].astype(F32) + b[...].astype(F32)).astype(BF16)


def merge(passed, a, b):
    return pl.pallas_call(
        merge_kernel,
        out_shape=(
            jax.ShapeDtypeStruct(b.shape, BF16),
            jax.ShapeDtypeStruct(passed.shape, passed.dtype),
        ),
        in_specs=[ANY, VMEM, VMEM],
        out_specs=(VMEM, ANY),
        input_output_aliases={0: 1},
        compiler_params=params(8),
    )(passed, a, b)


def place_projection(core, mine, other, p):
    half = mine.shape[0]
    p[pl.ds(pl.multiple_of(core * half, half), half), :] = mine[...]
    p[pl.ds(pl.multiple_of((1 - core) * half, half), half), :] = other[...]


def square_sum(x):
    x = x.astype(F32)
    return jnp.sum(x * x, axis=0, keepdims=True)


def orth_rows(c, t, p):
    return (c.astype(F32) - dot(t, p, ((1,), (1,)))).astype(BF16)


def orth_kernel(part, place, mine, other, after, x_in, sq_in, f, t, x_out, sq, x_v, p, out_sems):
    nt = t.shape[2]
    w = sq.shape[1]
    stores = Loads(out_sems)
    lo, hi = part
    place_projection(core_of(place), mine, other, p)
    sq[...] = sq_in[...]
    for i, at in enumerate(range(lo, hi, 2)):
        block = f[at : at + 2, :, 0:w].reshape(2 * BK, w)
        x = orth_rows(block, t[at : at + 2].reshape(2 * BK, nt), p[...])
        x_v[2 * i : 2 * i + 2] = x.reshape(2, BK, w)
        sq[...] += square_sum(x)
        stores.start(x_v.at[2 * i : 2 * i + 2], x_out.at[at : at + 2])
    stores.wait_all()


def orthogonalize(part, place, mine, other, after, x, sq, f, t):
    nblk, _, nt = t.shape
    w = 2 * mine.shape[0]
    size = part[1] - part[0]
    return pl.pallas_call(
        functools.partial(orth_kernel, part),
        out_shape=(pltpu.HBM((nblk, BK, w), BF16), jax.ShapeDtypeStruct((1, w), F32)),
        in_specs=[SMEM, VMEM, VMEM, ANY, ANY, VMEM, VMEM, VMEM],
        out_specs=(ANY, VMEM),
        input_output_aliases={} if x is None else {4: 0},
        scratch_shapes=[
            pltpu.VMEM((size, BK, w), BF16),
            pltpu.VMEM((w, nt), BF16),
            pltpu.SemaphoreType.DMA((size // 2,)),
        ],
        compiler_params=params(7),
        cost_estimate=cost(size * BK * w * nt, 8 * 2**20),
    )(place, mine, other, after, after if x is None else x, sq, held(f), held(t))


def chip_order(bits, side):
    return [(s + side) % bits for s in range(bits)]


def dipole_rest_kernel(
    nblk, place, off, after, acc, f, intra, inter, t, d_edge, d_rest, send, keep, total, yd, f_v, ys, sems
):
    groups, cols, lanes = keep.shape
    bits = groups.bit_length() - 1
    near = boundary_start(nblk, core_of(place), f, intra, inter, f_v, sems)
    _, rest = lead_of(nblk)
    for g, rows in enumerate(rest):
        slot = rows[0] - rest[0][0]
        band_rows(rows, range(slot, slot + len(rows)), off, f, cols, d_rest, 0, yd)
        project(total, acc if g == 0 else total, yd, t, rows[0], len(rows))
    acc = total if rest else acc
    boundary_rows(nblk, near, off, d_edge, f_v, ys)
    orders = [chip_order(bits, side) for side in (0, 1)]
    for at in range(0, cols, BK):
        here = slice(at, min(at + BK, cols))
        whole = boundary_sum(acc, ys, t, here)
        for g in range(groups):
            owned = []
            for side in (0, 1):
                chip = sum(
                    ((g >> (bits - 1 - s)) & 1) << orders[side][s] for s in range(bits)
                )
                first_lane = (2 * chip + side) * lanes
                owned.append(whole[:, first_lane : first_lane + lanes])
            keep[g, here, :] = jnp.where(core_of(place) == 0, owned[0], owned[1])
            send[g, here, :] = jnp.where(core_of(place) == 0, owned[1], owned[0]).astype(BF16)


def dipole_rest(place, off, after, acc, f, intra, inter, t, d_edge, d_rest, groups):
    nblk, _, nt = t.shape
    cols = acc.shape[0]
    lanes = nt // (2 * groups)
    count = sum(map(len, lead_of(nblk)[1])) + 4
    return pl.pallas_call(
        functools.partial(dipole_rest_kernel, nblk),
        out_shape=(
            jax.ShapeDtypeStruct((groups, cols, lanes), BF16),
            jax.ShapeDtypeStruct((groups, cols, lanes), F32),
        ),
        in_specs=[SMEM, SMEM, ANY] + [VMEM] * 7,
        out_specs=(VMEM, VMEM),
        scratch_shapes=[pltpu.VMEM((cols, nt), F32), pltpu.VMEM((4 * BK, cols), BF16)]
        + boundary_scratch(cols),
        compiler_params=params(15),
        cost_estimate=cost(count * BK * cols * (KB * BK + nt), 8 * 2**20),
    )(place, off, after, held(acc), held(f), intra, inter, held(t), held(d_edge), held(d_rest))


def halve_kernel(step, place, after, keep, got, send, kept):
    half = kept.shape[0]
    orders = [chip_order(step[1], side)[step[0]] for side in (0, 1)]
    which = jnp.where(core_of(place) == 0, orders[0], orders[1])
    bit = jnp.bitwise_and(jnp.right_shift(place[0], which + 1), 1)
    for g in range(half):
        here, there = bit * half + g, (1 - bit) * half + g
        kept[g] = keep[here] + got[here].astype(F32)
        send[g] = (keep[there] + got[there].astype(F32)).astype(BF16)


def halve(step, place, after, keep, got):
    groups, cols, lanes = keep.shape
    half = groups // 2
    return pl.pallas_call(
        functools.partial(halve_kernel, step),
        out_shape=(
            jax.ShapeDtypeStruct((half, cols, lanes), BF16),
            jax.ShapeDtypeStruct((half, cols, lanes), F32),
        ),
        in_specs=[SMEM, ANY, VMEM, VMEM],
        out_specs=(VMEM,) * 2,
        compiler_params=params(8),
    )(place, after, keep, got)


def settle_kernel(w, after, keep, got, out):
    out[...] = (keep[0, w:, :] + got[0, w:, :].astype(F32)).astype(BF16)


def settle(w, after, keep, got):
    _, cols, lanes = keep.shape
    return pl.pallas_call(
        functools.partial(settle_kernel, w),
        out_shape=jax.ShapeDtypeStruct((cols - w, lanes), BF16),
        in_specs=[ANY, VMEM, VMEM],
        out_specs=VMEM,
        compiler_params=params(8),
    )(after, keep, got)


def stack_kernel(after, *refs):
    out, at = refs[-1], 0
    for piece in refs[:-1]:
        out[at : at + piece.shape[0], :] = piece[...]
        at += piece.shape[0]


def stack(after, pieces):
    rows = sum(piece.shape[0] for piece in pieces)
    return pl.pallas_call(
        stack_kernel,
        out_shape=jax.ShapeDtypeStruct((rows, pieces[0].shape[1]), BF16),
        in_specs=[ANY] + [VMEM] * len(pieces),
        out_specs=VMEM,
        compiler_params=params(8),
    )(after, *pieces)


def finish_kernel(rows, place, z, keep, got, mine, other, sq, *refs):
    pieces, (out, g_v) = refs[:-2], refs[-2:]
    half, w = mine.shape[0], sq.shape[1]
    zc = keep.shape[1] - w
    at = 0
    for piece in pieces:
        for q in range(piece.shape[0] // zc):
            where = pl.multiple_of(jnp.bitwise_xor(z[0], at) * zc, zc)
            g_v[pl.ds(where, zc), :] = piece[q * zc : (q + 1) * zc, :]
            at += 1
    norm = 1.0 / jnp.sqrt(sq[...] / rows + 1e-06)
    for side in (0, 1):
        here = slice(side * half, (side + 1) * half)
        p = jnp.where(core_of(place) == side, mine[...], other[...])
        raw = keep[0, here, :] + got[0, here, :].astype(F32) - dot(p, g_v[...])
        out[:, here] = (raw.T * norm[:, here]).astype(BF16)


def finish(rows, place, z, keep, got, mine, other, sq, pieces):
    _, cols, lanes = keep.shape
    nt = mine.shape[1]
    w = sq.shape[1]
    return pl.pallas_call(
        functools.partial(finish_kernel, rows),
        out_shape=jax.ShapeDtypeStruct((lanes, w), BF16),
        in_specs=[SMEM, SMEM] + [VMEM] * (5 + len(pieces)),
        out_specs=VMEM,
        scratch_shapes=[pltpu.VMEM((nt, lanes), BF16)],
        compiler_params=params(8),
    )(place, z, keep, got, mine, other, sq, *pieces)


def swap(block, count, mask):
    return lax.ppermute(block, "basis", [(i, i ^ mask[i % 2]) for i in range(count)])


def meet(block, count):
    pairs = [(i, i + 1) for i in range(1, count - 1, 2)]
    return lax.ppermute(block, "basis", pairs + [(b, a) for a, b in pairs])


def exchange(intra, inter, count):
    inter = meet(inter, count)
    return swap(intra, count, (1, 1)), inter


def scalar(x):
    return x.astype(jnp.int32).reshape(1)


def on_device(cont_orbitals, target_orbitals, margin_blocks, dipole_blocks, band_offsets):
    count = lax.axis_size("basis")
    planes = lax.axis_size("orb")
    rows, w = cont_orbitals.shape
    nblk = rows // BK
    nt = target_orbitals.shape[1]
    zc = nt // planes
    chips = count // 2
    bits = chips.bit_length() - 1
    place_s = scalar(lax.axis_index("basis"))
    z = lax.axis_index("orb")
    z_s = scalar(z)
    off = band_offsets.astype(jnp.int32).T
    c = cont_orbitals.reshape(nblk, BK, w)
    t = target_orbitals.reshape(nblk, BK, nt)
    zero = jnp.zeros((1, w), F32)
    both = (1, 1)
    orders = [chip_order(bits, side) for side in (0, 1)]
    masks = [(2 << orders[0][s], 2 << orders[1][s]) for s in range(bits)]

    intra, inter = exchange(*edges(place_s, z_s, c, t, zc), count)
    p_acc, r_acc, f, t_v, m_edge = first(z_s, off, c, t, margin_blocks, dipole_blocks, zc)
    send, keep, d_edge, d_rest = project_boundary(
        place_s, off, p_acc, f, intra, inter, t_v, m_edge, dipole_blocks
    )
    part, r_acc = merge(r_acc, keep, swap(send, count, both))

    got = swap(part, count, masks[0])
    send, keep = dipole_rest(
        place_s, off, part, r_acc, f, intra, inter, t_v, d_edge, d_rest, chips
    )
    part, send = merge(send, part, got)
    for s in range(1, bits):
        got = swap(part, count, masks[s])
        got_r = swap(send, count, both if s == 1 else masks[s - 2])
        send, keep = halve((s - 1, bits), place_s, part, keep, got_r)
        part, send = merge(send, part, got)
    other = swap(part, count, both)
    got_r = swap(send, count, masks[bits - 2])

    half = nblk // 4 * 2
    x, sq = orthogonalize((0, half), place_s, part, other, part, None, zero, f, t_v)
    send, keep = halve((bits - 1, bits), place_s, sq, keep, got_r)
    got_r = swap(send, count, masks[bits - 1])
    x, sq = orthogonalize((half, nblk), place_s, part, other, send, x, sq, f, t_v)
    pieces = [settle(w, sq, keep, got_r)]
    tail = [both] + masks
    step = 1
    while step < planes or tail:
        if tail:
            sq = sq + swap(sq, count, tail.pop(0))
        if step < planes:
            whole = pieces[0] if step == 1 else stack(sq, pieces)
            pieces.append(lax.ppermute(whole, "orb", [(i, i ^ step) for i in range(planes)]))
            step *= 2
    dipole_mo = finish(rows * count, place_s, z_s, keep, got_r, part, other, sq, pieces)
    return (x.reshape(rows, w), dipole_mo)


def solution(mesh):
    return jax.shard_map(
        on_device,
        mesh=mesh,
        in_specs=(
            P("basis", "orb"),
            P("basis", None),
            P("basis", None, None, None),
            P("basis", None, None, None),
            P("basis", None),
        ),
        out_specs=(P("basis", "orb"), P("basis", "orb")),
        check_vma=False,
    )
```

time: 305 us -> 81.6 us (0.27)
  matrix products: 91.9 us -> 0 us
  blocking collectives: 87.3 us -> 0 us
  local copies, waits for them, and re-layouts: 65 us -> 0.01 us
  Pallas kernels: 0 us -> 41.9 us
  other arithmetic: 14.2 us -> 0.01 us
  between operations: 14.2 us -> 0.79 us
  starting transfers between devices: 6.33 us -> 14.1 us
    dot_general x11 -> x0, matrix products: 91.9 us -> none  [the longest x8 63.9 us: band_local(): jnp.einsum('bij,bjc->bic', blocks[:, k], taken, preferred_element_type=jn...]
    psum x2 -> x0, blocking collectives: 87.3 us -> none  [the longest x1 63.9 us: on_device(): projection = lax.psum(partial_proj, 'basis')]
    gather x8 -> x0, local copies, waits for them, and re-layouts: 42.1 us -> none  [band_local(): taken = stacked[index]]
    pallas_call x0 -> x14, Pallas kernels: none -> 41.9 us  [the longest x1 18.5 us: first(): pl.pallas_call(functools.partial(first_kernel, nblk), out_shape=(pltpu.VM...]
    reduce_scatter x1 -> x0, waiting for transfers between devices: 22.7 us -> none  [on_device(): lax.psum_scatter(lax.dot_general(target_orbitals, dipole_cont, (((0,), (0...]
    ppermute x4 -> x14, waiting for transfers between devices: 2.51 us -> 24.6 us  [the longest x11 22.7 us: swap(): lax.ppermute(block, 'basis', [(i, i ^ mask[i % 2]) for i in range(count)])]
    unnamed x19 -> x2, local copies, waits for them, and re-layouts: 13.6 us -> 0.01 us
    concatenate x2 -> x0, other arithmetic: 13.1 us -> none  [padded_2(): block = jnp.concatenate([low, block, high], axis=dim)]
  transfers between devices with their start and end apart: 5 -> 14, of which waited for: 3 -> 10; matrix products, arithmetic and copies ran while one was open for 4% -> 0% of each run, Pallas kernels for 0% -> 43%
where the time goes in v2:
time: 81.6 us; the launch traced here: 81.5 us
  Pallas kernels  41.9 us (51%)
  waiting for transfers between devices  24.6 us (30%)
  starting transfers between devices  14.1 us (17%)
    ppermute x11, waiting for transfers between devices, swap(): lax.ppermute(block, 'basis', [(i, i ^ mask[i % 2]) for i in range(count)])  22.7 us
    pallas_call x1, Pallas kernels, first(): pl.pallas_call(functools.partial(first_kernel, nblk), out_shape=(pltpu.VM...  18.5 us
    pallas_call x1, Pallas kernels, dipole_rest(): pl.pallas_call(functools.partial(dipole_rest_kernel, nblk), out_shape=(ja...  9.4 us
    ppermute x11, starting transfers between devices, swap(): lax.ppermute(block, 'basis', [(i, i ^ mask[i % 2]) for i in range(count)])  9.09 us
    pallas_call x2, Pallas kernels, orthogonalize(): pl.pallas_call(functools.partial(orth_kernel, part), out_shape=(pltpu.HBM...  7.3 us
    ppermute x2, starting transfers between devices, on_device(): lax.ppermute(whole, 'orb', [(i, i ^ step) for i in range(planes)])  4.31 us
    pallas_call x1, Pallas kernels, project_boundary(): pl.pallas_call(functools.partial(boundary_kernel, nblk), out_shape=(jax.S...  3.59 us
    ppermute x2, waiting for transfers between devices, on_device(): lax.ppermute(whole, 'orb', [(i, i ^ step) for i in range(planes)])  1.95 us
  transfers between devices with their start and end apart: 14, of which 10 were waited for; matrix products, arithmetic and copies ran while one was open for 0% of the time, Pallas kernels for 43%

profile of v2, /device:TPU:0, one launch (start us, length us, event | category | flops | bytes accessed | tf_op | source)
XLA Modules:
  0.0 81.5 jit_solution(9395927719219069996)
XLA Ops:
  0.6 1.4 %shard_map.69 = (bf16[2,256,768]{2,1,0:T(8,128)(2,1)S(1)}, bf16[2,256,768]{2,1,0:T(8,128)(2,1)S(1)}) custom-call(s32[1]{0:T(128)} %bitcast.place, s32[1]{0:T(128)} %bitcast.2.z, bf16[16,256,512]{2,1,0:T(8,128)(2,1)} %bitcast.11, bf16[16,256,1024]{2,1,0:T(8,128)(2,1)} %bitcast.9), custom_call_target="tpu_custom_call" | custom-call | tf_op jit(solution)/shard_map/pallas_call | solution.py:110
  2.0 0.5 collective-permute-start
  2.6 0.7 collective-permute-start.1
  3.3 18.5 %shard_map.68 = (f32[512,1024]{1,0:T(8,128)S(1)}, f32[768,1024]{1,0:T(8,128)S(1)}, bf16[16,256,768]{2,1,0:T(8,128)(2,1)S(1)}, bf16[16,256,1024]{2,1,0:T(8,128)(2,1)S(1)}, bf16[4,4,256,256]{3,2,1,0:T(8,128)(2,1)S(1)}) custom-call(s32[1]{0:T(128)} %bitcast.2.z, s32[4,16]{1,0:T(4,128)S(1)} %bitcast.6, bf16[16,256,512]{2,1,0:T(8,128)(2,1)} %bitcast.12, ...), custom_call_target="tpu_custom_call" | custom-call | flops 12884901888 | bytes 31457280 | tf_op jit(solution)/shard_map/pallas_call | solution.py:194
  21.8 3.6 %shard_map.70 = (bf16[256,1024]{1,0:T(8,128)(2,1)S(1)}, f32[256,1024]{1,0:T(8,128)S(1)}, bf16[4,4,256,256]{3,2,1,0:T(8,128)(2,1)S(1)}, bf16[4,4,256,256]{3,2,1,0:T(8,128)(2,1)S(1)}) custom-call(s32[1]{0:T(128)} %bitcast.place, s32[4,16]{1,0:T(4,128)S(1)} %bitcast.7, f32[512,1024]{1,0:T(8,128)S(1)} %get-tuple-element.30.acc, ...), custom_call_target="tpu_custom_call" | custom-call | flops 2147483648 | bytes 8388608 | tf_op jit(solution)/shard_map/pallas_call | solution.py:277
  25.4 3.9 %collective-permute-start.2 = (bf16[256,1024]{1,0:T(8,128)(2,1)S(1)}, bf16[256,1024]{1,0:T(8,128)(2,1)S(1)}, u32[]{:S(2)}, u32[]{:S(2)}) collective-permute-start(bf16[256,1024]{1,0:T(8,128)(2,1)S(1)} %get-tuple-element.37), channel_id=1, source_target_pairs={{0,4},{4,0},{8,12},{12,8},{16,20},{20,16},{24,28},{28,24},{1,5},{5... | collective-permute-start | bytes 1572872 | tf_op jit(solution)/shard_map/ppermute | solution.py:507
  29.3 1.5 %collective-permute-done.2.b = bf16[256,1024]{1,0:T(8,128)(2,1)S(1)} collective-permute-done((bf16[256,1024]{1,0:T(8,128)(2,1)S(1)}, bf16[256,1024]{1,0:T(8,128)(2,1)S(1)}, u32[]{:S(2)}, u32[]{:S(2)}) %collective-permute-start.2) | collective-permute-done | bytes 524320 | tf_op jit(solution)/shard_map/ppermute | solution.py:507
  30.8 0.1 shard_map.71
  30.9 2.0 %collective-permute-start.3 = (bf16[256,1024]{1,0:T(8,128)(2,1)S(1)}, bf16[256,1024]{1,0:T(8,128)(2,1)S(1)}, u32[]{:S(2)}, u32[]{:S(2)}) collective-permute-start(bf16[256,1024]{1,0:T(8,128)(2,1)S(1)} %get-tuple-element.38.after.a), channel_id=1, source_target_pairs={{0,8},{4,20},{8,0},{12,28},{16,24},{20,4},{24,16},{28,12},{1,9},{5... | collective-permute-start | bytes 1572872 | tf_op jit(solution)/shard_map/ppermute | solution.py:507
  32.9 9.4 %shard_map.72 = (bf16[4,768,128]{2,1,0:T(8,128)(2,1)S(1)}, f32[4,768,128]{2,1,0:T(8,128)S(1)}) custom-call(s32[1]{0:T(128)} %bitcast.place, s32[4,16]{1,0:T(4,128)S(1)} %bitcast.8, bf16[256,1024]{1,0:T(8,128)(2,1)S(1)} %get-tuple-element.38.after.a, f32[768,1024]{1,0:T(8,128)S(1)} %get-tuple-element.39.acc, bf16[16,256,768]{2,1,0:T(8,128)(2,1)S(1)} %get-tuple-element.31.f, ...), custom_call_target="tpu_custom_call" | custom-call | flops 6442450944 | bytes 8388608 | tf_op jit(solution)/shard_map/pallas_call | solution.py:400
  42.3 0.1 shard_map.73
  42.6 0.6 collective-permute-start.5
  43.2 1.7 %collective-permute-done.4.got = bf16[4,768,128]{2,1,0:T(8,128)(2,1)S(1)} collective-permute-done((bf16[4,768,128]{2,1,0:T(8,128)(2,1)S(1)}, bf16[4,768,128]{2,1,0:T(8,128)(2,1)S(1)}, u32[]{:S(2)}, u32[]{:S(2)}) %collective-permute-start.4) | collective-permute-done | bytes 786464 | tf_op jit(solution)/shard_map/ppermute | solution.py:507
  44.8 0.2 shard_map.74
  45.0 6.8 %collective-permute-done.5.b = bf16[256,1024]{1,0:T(8,128)(2,1)S(1)} collective-permute-done((bf16[256,1024]{1,0:T(8,128)(2,1)S(1)}, bf16[256,1024]{1,0:T(8,128)(2,1)S(1)}, u32[]{:S(2)}, u32[]{:S(2)}) %collective-permute-start.5) | collective-permute-done | bytes 524320 | tf_op jit(solution)/shard_map/ppermute | solution.py:507
  51.8 0.1 shard_map.75
  52.0 0.4 collective-permute-start.7
  52.4 1.5 %collective-permute-done.6.other = bf16[256,1024]{1,0:T(8,128)(2,1)S(1)} collective-permute-done((bf16[256,1024]{1,0:T(8,128)(2,1)S(1)}, bf16[256,1024]{1,0:T(8,128)(2,1)S(1)}, u32[]{:S(2)}, u32[]{:S(2)}) %collective-permute-start.6) | collective-permute-done | bytes 524320 | tf_op jit(solution)/shard_map/ppermute | solution.py:507
  53.9 3.6 %shard_map.76 = (bf16[16,256,512]{2,1,0:T(8,128)(2,1)}, f32[1,512]{1,0:T(1,128)S(1)}) custom-call(s32[1]{0:T(128)} %bitcast.place, bf16[256,1024]{1,0:T(8,128)(2,1)S(1)} %get-tuple-element.47.mine.after.x_in, bf16[256,1024]{1,0:T(8,128)(2,1)S(1)} %collective-permute-done.6.other, bf16[256,1024]{1,0:T(8,128)(2,1)S(1)} %get-tuple-element.47.mine.after.x_in, ...), custom_call_target="tpu_custom_call" | custom-call | flops 2147483648 | bytes 8388608 | tf_op jit(solution)/shard_map/pallas_call | solution.py:346
  57.6 2.3 %collective-permute-done.7.got = bf16[2,768,128]{2,1,0:T(8,128)(2,1)S(1)} collective-permute-done((bf16[2,768,128]{2,1,0:T(8,128)(2,1)S(1)}, bf16[2,768,128]{2,1,0:T(8,128)(2,1)S(1)}, u32[]{:S(2)}, u32[]{:S(2)}) %collective-permute-start.7) | collective-permute-done | bytes 393248 | tf_op jit(solution)/shard_map/ppermute | solution.py:507
  59.9 0.6 collective-permute-start.8
  60.5 3.7 %shard_map.78 = (bf16[16,256,512]{2,1,0:T(8,128)(2,1)}, f32[1,512]{1,0:T(1,128)S(1)}) custom-call(s32[1]{0:T(128)} %bitcast.place, bf16[256,1024]{1,0:T(8,128)(2,1)S(1)} %get-tuple-element.47.mine.after.x_in, bf16[256,1024]{1,0:T(8,128)(2,1)S(1)} %collective-permute-done.6.other, ...), custom_call_target="tpu_custom_call", output_to_operand_aliasing={{0}: (4, {})} | custom-call | flops 2147483648 | bytes 8388608 | tf_op jit(solution)/shard_map/pallas_call | solution.py:346
  64.2 1.5 %collective-permute-done.8.got = bf16[1,768,128]{2,1,0:T(8,128)(2,1)S(1)} collective-permute-done((bf16[1,768,128]{2,1,0:T(8,128)(2,1)S(1)}, bf16[1,768,128]{2,1,0:T(8,128)(2,1)S(1)}, u32[]{:S(2)}, u32[]{:S(2)}) %collective-permute-start.8) | collective-permute-done | bytes 196640 | tf_op jit(solution)/shard_map/ppermute | solution.py:507
  65.7 1.6 %collective-permute-start.12 = (bf16[256,128]{1,0:T(8,128)(2,1)S(1)}, bf16[256,128]{1,0:T(8,128)(2,1)S(1)}, u32[]{:S(2)}, u32[]{:S(2)}) collective-permute-start(bf16[256,128]{1,0:T(8,128)(2,1)S(1)} %shard_map.79.refs_0_), channel_id=1, source_target_pairs={{0,1},{1,0},{2,3},{3,2},{4,5},{5,4},{6,7},{7,6},{8,9},{9,8},{10,11... | collective-permute-start | bytes 196616 | tf_op jit(solution)/shard_map/ppermute | solution.py:577
  67.3 1.2 %collective-permute-done.9 = f32[1,512]{1,0:T(1,128)S(1)} collective-permute-done((f32[1,512]{1,0:T(1,128)S(1)}, f32[1,512]{1,0:T(1,128)S(1)}, u32[]{:S(2)}, u32[]{:S(2)}) %collective-permute-start.9) | collective-permute-done | bytes 2080 | tf_op jit(solution)/shard_map/ppermute | solution.py:507
  68.5 0.3 collective-permute-start.10
  68.8 3.3 %collective-permute-done.10 = f32[1,512]{1,0:T(1,128)S(1)} collective-permute-done((f32[1,512]{1,0:T(1,128)S(1)}, f32[1,512]{1,0:T(1,128)S(1)}, u32[]{:S(2)}, u32[]{:S(2)}) %collective-permute-start.10) | collective-permute-done | bytes 2080 | tf_op jit(solution)/shard_map/ppermute | solution.py:507
  72.1 2.7 %collective-permute-start.13 = (bf16[512,128]{1,0:T(8,128)(2,1)S(1)}, bf16[512,128]{1,0:T(8,128)(2,1)S(1)}, u32[]{:S(2)}, u32[]{:S(2)}) collective-permute-start(bf16[512,128]{1,0:T(8,128)(2,1)S(1)} %shard_map.80), channel_id=1, source_target_pairs={{0,2},{1,3},{2,0},{3,1},{4,6},{5,7},{6,4},{7,5},{8,10},{9,11},{10,... | collective-permute-start | bytes 393224 | tf_op jit(solution)/shard_map/ppermute | solution.py:577
  74.8 0.5 collective-permute-start.11
  75.3 3.0 %collective-permute-done.11 = f32[1,512]{1,0:T(1,128)S(1)} collective-permute-done((f32[1,512]{1,0:T(1,128)S(1)}, f32[1,512]{1,0:T(1,128)S(1)}, u32[]{:S(2)}, u32[]{:S(2)}) %collective-permute-start.11) | collective-permute-done | bytes 2080 | tf_op jit(solution)/shard_map/ppermute | solution.py:507
  78.4 1.9 %collective-permute-done.13.refs_2_ = bf16[512,128]{1,0:T(8,128)(2,1)S(1)} collective-permute-done((bf16[512,128]{1,0:T(8,128)(2,1)S(1)}, bf16[512,128]{1,0:T(8,128)(2,1)S(1)}, u32[]{:S(2)}, u32[]{:S(2)}) %collective-permute-start.13) | collective-permute-done | bytes 131104 | tf_op jit(solution)/shard_map/ppermute | solution.py:577
  80.3 1.2 %shard_map.81 = bf16[128,512]{1,0:T(8,128)(2,1)} custom-call(s32[1]{0:T(128)} %bitcast.place, s32[1]{0:T(128)} %bitcast.2.z, f32[1,768,128]{2,1,0:T(8,128)S(1)} %get-tuple-element.54.keep, bf16[1,768,128]{2,1,0:T(8,128)(2,1)S(1)} %collective-permute-done.8.got, bf16[256,1024]{1,0:T(8,128)(2,1)S(1)} %get-tuple-element.47.mine.after.x_in, ...), custom_call_target="tpu_custom_call" | custom-call | tf_op jit(solution)/shard_map/pallas_call | solution.py:496
  (16 shorter events, 0.3 us)
Async XLA Ops:
  0.6 2.6 %copy-start = (s32[16,4]{0,1:T(4,128)S(1)}, s32[16,4]{0,1:T(4,128)}, u32[]{:S(2)}) copy-start(s32[16,4]{0,1:T(4,128)} %param.9) | copy-start | bytes 772
  2.0 19.7 %collective-permute-start = (bf16[2,256,768]{2,1,0:T(8,128)(2,1)S(1)}, bf16[2,256,768]{2,1,0:T(8,128)(2,1)S(1)}, u32[]{:S(2)}, u32[]{:S(2)}) collective-permute-start(bf16[2,256,768]{2,1,0:T(8,128)(2,1)S(1)} %get-tuple-element.32), channel_id=1, source_target_pairs={{0,4},{4,0},{8,12},{12,8},{16,20},{20,16},{24,28},{28,24},{1,5},{5... | collective-permute-start | bytes 2359304 | tf_op jit(solution)/shard_map/ppermute | solution.py:507
  2.6 19.2 %collective-permute-start.1 = (bf16[2,256,768]{2,1,0:T(8,128)(2,1)S(1)}, bf16[2,256,768]{2,1,0:T(8,128)(2,1)S(1)}, u32[]{:S(2)}, u32[]{:S(2)}) collective-permute-start(bf16[2,256,768]{2,1,0:T(8,128)(2,1)S(1)} %get-tuple-element.33), channel_id=1, source_target_pairs={{4,8},{12,16},{20,24},{8,4},{16,12},{24,20},{5,9},{13,17},{21,25},... | collective-permute-start | bytes 2359304 | tf_op jit(solution)/shard_map/ppermute | solution.py:512
  25.4 5.5 %collective-permute-start.2 = (bf16[256,1024]{1,0:T(8,128)(2,1)S(1)}, bf16[256,1024]{1,0:T(8,128)(2,1)S(1)}, u32[]{:S(2)}, u32[]{:S(2)}) collective-permute-start(bf16[256,1024]{1,0:T(8,128)(2,1)S(1)} %get-tuple-element.37), channel_id=1, source_target_pairs={{0,4},{4,0},{8,12},{12,8},{16,20},{20,16},{24,28},{28,24},{1,5},{5... | collective-permute-start | bytes 1572872 | tf_op jit(solution)/shard_map/ppermute | solution.py:507
  30.9 11.4 %collective-permute-start.3 = (bf16[256,1024]{1,0:T(8,128)(2,1)S(1)}, bf16[256,1024]{1,0:T(8,128)(2,1)S(1)}, u32[]{:S(2)}, u32[]{:S(2)}) collective-permute-start(bf16[256,1024]{1,0:T(8,128)(2,1)S(1)} %get-tuple-element.38.after.a), channel_id=1, source_target_pairs={{0,8},{4,20},{8,0},{12,28},{16,24},{20,4},{24,16},{28,12},{1,9},{5... | collective-permute-start | bytes 1572872 | tf_op jit(solution)/shard_map/ppermute | solution.py:507
  42.5 2.4 %collective-permute-start.4 = (bf16[4,768,128]{2,1,0:T(8,128)(2,1)S(1)}, bf16[4,768,128]{2,1,0:T(8,128)(2,1)S(1)}, u32[]{:S(2)}, u32[]{:S(2)}) collective-permute-start(bf16[4,768,128]{2,1,0:T(8,128)(2,1)S(1)} %get-tuple-element.45), channel_id=1, source_target_pairs={{0,4},{4,0},{8,12},{12,8},{16,20},{20,16},{24,28},{28,24},{1,5},{5... | collective-permute-start | bytes 2359304 | tf_op jit(solution)/shard_map/ppermute | solution.py:507
  42.6 9.2 %collective-permute-start.5 = (bf16[256,1024]{1,0:T(8,128)(2,1)S(1)}, bf16[256,1024]{1,0:T(8,128)(2,1)S(1)}, u32[]{:S(2)}, u32[]{:S(2)}) collective-permute-start(bf16[256,1024]{1,0:T(8,128)(2,1)S(1)} %get-tuple-element.43.after.a), channel_id=1, source_target_pairs={{0,16},{4,12},{8,24},{12,4},{16,0},{20,28},{24,8},{28,20},{1,17},{... | collective-permute-start | bytes 1572872 | tf_op jit(solution)/shard_map/ppermute | solution.py:507
  51.9 2.0 %collective-permute-start.6 = (bf16[256,1024]{1,0:T(8,128)(2,1)S(1)}, bf16[256,1024]{1,0:T(8,128)(2,1)S(1)}, u32[]{:S(2)}, u32[]{:S(2)}) collective-permute-start(bf16[256,1024]{1,0:T(8,128)(2,1)S(1)} %get-tuple-element.47.mine.after.x_in), channel_id=1, source_target_pairs={{0,4},{4,0},{8,12},{12,8},{16,20},{20,16},{24,28},{28,24},{1,5},{5... | collective-permute-start | bytes 1572872 | tf_op jit(solution)/shard_map/ppermute | solution.py:507
  52.0 7.8 %collective-permute-start.7 = (bf16[2,768,128]{2,1,0:T(8,128)(2,1)S(1)}, bf16[2,768,128]{2,1,0:T(8,128)(2,1)S(1)}, u32[]{:S(2)}, u32[]{:S(2)}) collective-permute-start(bf16[2,768,128]{2,1,0:T(8,128)(2,1)S(1)} %get-tuple-element.50), channel_id=1, source_target_pairs={{0,8},{4,20},{8,0},{12,28},{16,24},{20,4},{24,16},{28,12},{1,9},{5... | collective-permute-start | bytes 1179656 | tf_op jit(solution)/shard_map/ppermute | solution.py:507
  59.9 5.7 %collective-permute-start.8 = (bf16[1,768,128]{2,1,0:T(8,128)(2,1)S(1)}, bf16[1,768,128]{2,1,0:T(8,128)(2,1)S(1)}, u32[]{:S(2)}, u32[]{:S(2)}) collective-permute-start(bf16[1,768,128]{2,1,0:T(8,128)(2,1)S(1)} %get-tuple-element.51.after), channel_id=1, source_target_pairs={{0,16},{4,12},{8,24},{12,4},{16,0},{20,28},{24,8},{28,20},{1,17},{... | collective-permute-start | bytes 589832 | tf_op jit(solution)/shard_map/ppermute | solution.py:507
  65.7 6.4 %collective-permute-start.12 = (bf16[256,128]{1,0:T(8,128)(2,1)S(1)}, bf16[256,128]{1,0:T(8,128)(2,1)S(1)}, u32[]{:S(2)}, u32[]{:S(2)}) collective-permute-start(bf16[256,128]{1,0:T(8,128)(2,1)S(1)} %shard_map.79.refs_0_), channel_id=1, source_target_pairs={{0,1},{1,0},{2,3},{3,2},{4,5},{5,4},{6,7},{7,6},{8,9},{9,8},{10,11... | collective-permute-start | bytes 196616 | tf_op jit(solution)/shard_map/ppermute | solution.py:577
  67.3 1.2 %collective-permute-start.9 = (f32[1,512]{1,0:T(1,128)S(1)}, f32[1,512]{1,0:T(1,128)S(1)}, u32[]{:S(2)}, u32[]{:S(2)}) collective-permute-start(f32[1,512]{1,0:T(1,128)S(1)} %get-tuple-element.55.after), channel_id=1, source_target_pairs={{0,4},{4,0},{8,12},{12,8},{16,20},{20,16},{24,28},{28,24},{1,5},{5... | collective-permute-start | bytes 6152 | tf_op jit(solution)/shard_map/ppermute | solution.py:507
  68.5 3.6 %collective-permute-start.10 = (f32[1,512]{1,0:T(1,128)S(1)}, f32[1,512]{1,0:T(1,128)S(1)}, u32[]{:S(2)}, u32[]{:S(2)}) collective-permute-start(f32[1,512]{1,0:T(1,128)S(1)} %add.9), channel_id=1, source_target_pairs={{0,8},{4,20},{8,0},{12,28},{16,24},{20,4},{24,16},{28,12},{1,9},{5... | collective-permute-start | bytes 6152 | tf_op jit(solution)/shard_map/ppermute | solution.py:507
  72.1 8.2 %collective-permute-start.13 = (bf16[512,128]{1,0:T(8,128)(2,1)S(1)}, bf16[512,128]{1,0:T(8,128)(2,1)S(1)}, u32[]{:S(2)}, u32[]{:S(2)}) collective-permute-start(bf16[512,128]{1,0:T(8,128)(2,1)S(1)} %shard_map.80), channel_id=1, source_target_pairs={{0,2},{1,3},{2,0},{3,1},{4,6},{5,7},{6,4},{7,5},{8,10},{9,11},{10,... | collective-permute-start | bytes 393224 | tf_op jit(solution)/shard_map/ppermute | solution.py:577
  74.8 3.6 %collective-permute-start.11 = (f32[1,512]{1,0:T(1,128)S(1)}, f32[1,512]{1,0:T(1,128)S(1)}, u32[]{:S(2)}, u32[]{:S(2)}) collective-permute-start(f32[1,512]{1,0:T(1,128)S(1)} %add.10.after), channel_id=1, source_target_pairs={{0,16},{4,12},{8,24},{12,4},{16,0},{20,28},{24,8},{28,20},{1,17},{... | collective-permute-start | bytes 6152 | tf_op jit(solution)/shard_map/ppermute | solution.py:507

commit v3 on v2

v3 whole, which is shorter than its diff:
```python
import functools

import jax
import jax.numpy as jnp
from jax import lax
from jax.experimental import pallas as pl
from jax.experimental.pallas import tpu as pltpu
from jax.sharding import PartitionSpec as P

BK = 256
KB = 4
LEAD = 2
F32 = jnp.float32
BF16 = jnp.bfloat16
ANY = pl.BlockSpec(memory_space=pl.ANY)
VMEM = pl.BlockSpec(memory_space=pltpu.VMEM)
SMEM = pl.BlockSpec(memory_space=pltpu.SMEM)


def core_of(place):
    return jnp.bitwise_and(place[0], 1)


def stay(x):
    return pltpu.with_memory_space_constraint(x, pltpu.HBM)


def params(mib=40):
    return pltpu.CompilerParams(vmem_limit_bytes=mib * 2**20)


def cost(macs, data):
    return pl.CostEstimate(flops=2 * macs, bytes_accessed=data, transcendentals=0)


def dot(a, b, dims=((1,), (0,))):
    return lax.dot_general(a, b, (dims, ((), ())), preferred_element_type=F32)


class Loads:
    def __init__(self, sems, ahead=64):
        self.sems, self.ahead = sems, ahead
        self.copies, self.started, self.done = [], 0, set()

    def start(self, src, dst):
        self.copies.append(pltpu.make_async_copy(src, dst, self.sems.at[len(self.copies)]))
        self.go()
        return len(self.copies) - 1

    def go(self):
        while self.started < min(len(self.copies), len(self.done) + self.ahead):
            self.copies[self.started].start()
            self.started += 1

    def wait(self, *which):
        for i in which:
            if i not in self.done:
                self.copies[i].wait()
                self.done.add(i)
                self.go()

    def wait_all(self):
        self.wait(*range(len(self.copies)))


def band_rows(rows, slots, off, field, cols, blocks, base, ys, at=0):
    for r, (b, slot) in enumerate(zip(rows, slots)):
        total = None
        for k in range(KB):
            term = dot(blocks[slot, k], field[b + off[k, b] + base, :, 0:cols])
            total = term if total is None else total + term
        ys[r * BK : (r + 1) * BK, at : at + cols] = total.astype(BF16)


def groups_of(nblk):
    inner = list(range(2, nblk - 2))
    return [inner[i : i + 4] for i in range(0, len(inner), 4)]


def project(out, acc, ys, t_v, lo, count):
    size = count * BK
    t = t_v[lo : lo + count].reshape(size, -1)
    for at in range(0, out.shape[0], BK):
        here = slice(at, min(at + BK, out.shape[0]))
        piece = dot(ys[0:size, here], t, ((0,), (0,)))
        out[here, :] = piece if acc is None else acc[here, :] + piece


def columns(z, width):
    return pl.ds(pl.multiple_of(z * width, width), width)


def held(x):
    return pltpu.with_memory_space_constraint(x, pltpu.VMEM)


def edge_kernel(place, c, intra, inter, sems):
    last = c.shape[0] - 2
    loads = Loads(sems)
    loads.start(c.at[pl.ds(core_of(place) * last, 2)], inter)
    loads.start(c.at[pl.ds((1 - core_of(place)) * last, 2)], intra)
    loads.wait_all()


def edges(place, c):
    pair = jax.ShapeDtypeStruct((2,) + c.shape[1:], BF16)
    return pl.pallas_call(
        edge_kernel,
        out_shape=(pair, pair),
        in_specs=[SMEM, ANY],
        out_specs=(VMEM, VMEM),
        scratch_shapes=[pltpu.SemaphoreType.DMA((2,))],
        compiler_params=params(8),
    )(place, stay(c))


def lead_of(nblk):
    inner = list(range(2, nblk - 2))
    rest = inner[LEAD:]
    return inner[:LEAD], [rest[i : i + 4] for i in range(0, len(rest), 4)]


def first_kernel(
    nblk, z, off, c, t, m, d, p_out, r_out, f, t_v, m_edge, m_v, d_v, ys, yd, sems
):
    w = c.shape[2]
    zc = f.shape[2] - w
    loads = Loads(sems, 8)
    lead, _ = lead_of(nblk)
    have, needs = 0, []
    for g, rows in enumerate(groups_of(nblk)):
        lo, hi = rows[0], rows[-1] + 1
        mid = min(lo + 2, hi)
        want = []
        for part in ((lo, mid), (mid, hi)):
            if part[0] == part[1]:
                continue
            upto = part[1] + 2
            ids = []
            if upto > have:
                ids.append(loads.start(c.at[have:upto], f.at[have:upto, :, 0:w]))
                have = upto
            ids.append(
                loads.start(m.at[part[0] : part[1]], m_v.at[part[0] - 2 : part[1] - 2])
            )
            want.append((list(range(*part)), ids))
        t_id = loads.start(t.at[lo:hi], t_v.at[lo:hi])
        d_ids = ()
        if g == 0:
            near = lead[-1] + 3
            d_ids = (
                loads.start(d.at[lead[0] : lead[-1] + 1], d_v),
                loads.start(t.at[0:near, :, columns(z[0], zc)], f.at[0:near, :, w : w + zc]),
            )
        needs.append((rows, want, t_id, d_ids))
    for side, at in ((0, 0), (1, nblk - 2)):
        loads.start(m.at[at : at + 2], m_edge.at[2 * side : 2 * side + 2])
        loads.start(t.at[at : at + 2], t_v.at[at : at + 2])
    loads.start(t.at[near:nblk, :, columns(z[0], zc)], f.at[near:nblk, :, w : w + zc])
    for g, (rows, want, t_id, d_ids) in enumerate(needs):
        at = 0
        for part, ids in want:
            loads.wait(*ids)
            band_rows(
                part, [b - 2 for b in part], off, f, w, m_v, 0,
                ys.at[at * BK : (at + len(part)) * BK],
            )
            at += len(part)
        loads.wait(t_id)
        project(p_out, None if g == 0 else p_out, ys, t_v, rows[0], len(rows))
        if d_ids:
            loads.wait(*d_ids)
            band_rows(lead, range(len(lead)), off, f, w + zc, d_v, 0, yd)
            project(r_out, None, yd, t_v, lead[0], len(lead))
        if g == 1:
            loads.ahead = 64
            loads.go()
    loads.wait_all()


def first(z, off, c, t, m, d, zc):
    nblk, _, w = c.shape
    nt = t.shape[2]
    inner = nblk - 4
    count = len(lead_of(nblk)[0])
    macs = inner * BK * w * (KB * BK + nt) + count * BK * (w + zc) * (KB * BK + nt)
    return pl.pallas_call(
        functools.partial(first_kernel, nblk),
        out_shape=(
            pltpu.VMEM((w, nt), F32),
            pltpu.VMEM((w + zc, nt), F32),
            pltpu.VMEM((nblk, BK, w + zc), BF16),
            pltpu.VMEM((nblk, BK, nt), BF16),
            pltpu.VMEM((4, KB, BK, BK), BF16),
        ),
        in_specs=[SMEM, SMEM, ANY, ANY, ANY, ANY],
        out_specs=(VMEM,) * 5,
        scratch_shapes=[
            pltpu.VMEM((inner, KB, BK, BK), BF16),
            pltpu.VMEM((count, KB, BK, BK), BF16),
            pltpu.VMEM((4 * BK, w), BF16),
            pltpu.VMEM((count * BK, w + zc), BF16),
            pltpu.SemaphoreType.DMA((5 * len(groups_of(nblk)) + 7,)),
        ],
        compiler_params=params(15),
        cost_estimate=cost(macs, 30 * 2**20),
    )(z, off, stay(c), stay(t), stay(m), stay(d))


def middle_kernel(groups, off, after, acc, f, t, d, d_rest, out, d_edge, yd, sems):
    nblk = f.shape[0]
    loads = Loads(sems)
    for side, at in ((0, 0), (1, nblk - 2)):
        loads.start(d.at[at : at + 2], d_edge.at[2 * side : 2 * side + 2])
    for g, rows in enumerate(groups):
        slot = rows[0] - groups[0][0]
        band_rows(rows, range(slot, slot + len(rows)), off, f, f.shape[2], d_rest, 0, yd)
        project(out, acc if g == 0 else out, yd, t, rows[0], len(rows))
    loads.wait_all()


def middle(off, after, acc, f, t, d, d_rest):
    nblk, _, cols = f.shape
    nt = t.shape[2]
    groups = lead_of(nblk)[1]
    count = sum(map(len, groups))
    return pl.pallas_call(
        functools.partial(middle_kernel, groups),
        out_shape=(pltpu.VMEM((cols, nt), F32), pltpu.VMEM((4, KB, BK, BK), BF16)),
        in_specs=[SMEM, ANY, VMEM, VMEM, VMEM, ANY, VMEM],
        out_specs=(VMEM, VMEM),
        scratch_shapes=[
            pltpu.VMEM((4 * BK, cols), BF16),
            pltpu.SemaphoreType.DMA((2,)),
        ],
        compiler_params=params(6),
        cost_estimate=cost(count * BK * cols * (KB * BK + nt), 14 * 2**20),
    )(off, after, held(acc), held(f), held(t), stay(d), held(d_rest))


def boundary_start(nblk, core, f, cols, intra, inter, f_v, sems):
    loads = Loads(sems)
    low = 10 * (1 - core)
    loads.start(f.at[0:4, :, cols], f_v.at[2:6])
    loads.start(intra, f_v.at[pl.ds(low, 2)])
    loads.start(inter, f_v.at[pl.ds(10 - low, 2)])
    loads.start(f.at[nblk - 4 : nblk, :, cols], f_v.at[6:10])
    return loads


def boundary_rows(nblk, loads, off, blocks, f_v, ys, at=0):
    cols = f_v.shape[2]
    if loads:
        loads.wait(0, 1, 2)
    band_rows([0, 1], [0, 1], off, f_v, cols, blocks, 2, ys.at[0 : 2 * BK], at)
    if loads:
        loads.wait(3)
    band_rows(
        [nblk - 2, nblk - 1], [2, 3], off, f_v, cols, blocks, 10 - nblk, ys.at[2 * BK : 4 * BK], at
    )


def boundary_sum(acc, ys, t, here):
    nblk = t.shape[0]
    ends = ((0,), (0,))
    low = dot(ys[0 : 2 * BK, here], t[0:2].reshape(2 * BK, -1), ends)
    high = dot(ys[2 * BK : 4 * BK, here], t[nblk - 2 : nblk].reshape(2 * BK, -1), ends)
    return acc[here, :] + (low + high)


def boundary_kernel(
    nblk, place, off, acc, f, intra, inter, t, m, d,
    send, keep, tz_intra, tz_inter, d_rest, f_v, ys, sems, d_sems,
):
    core = core_of(place)
    w = intra.shape[2]
    near = boundary_start(nblk, core, f, slice(0, w), intra, inter, f_v, sems)
    loads = Loads(d_sems)
    _, rest = lead_of(nblk)
    last = nblk - 2
    loads.start(f.at[pl.ds(core * last, 2), :, w:], tz_inter)
    loads.start(f.at[pl.ds((1 - core) * last, 2), :, w:], tz_intra)
    loads.start(d.at[rest[0][0] : rest[-1][-1] + 1], d_rest)
    half = send.shape[0]
    boundary_rows(nblk, near, off, m, f_v, ys)
    here = pl.ds(pl.multiple_of(core * half, half), half)
    there = pl.ds(pl.multiple_of((1 - core) * half, half), half)
    send[...] = boundary_sum(acc, ys, t, there).astype(BF16)
    keep[...] = boundary_sum(acc, ys, t, here)
    loads.wait_all()


def project_boundary(place, off, acc, f, intra, inter, t, m, d):
    nblk, _, nt = t.shape
    w = acc.shape[0]
    zc = f.shape[2] - w
    others = sum(map(len, lead_of(nblk)[1]))
    return pl.pallas_call(
        functools.partial(boundary_kernel, nblk),
        out_shape=(
            jax.ShapeDtypeStruct((w // 2, nt), BF16),
            jax.ShapeDtypeStruct((w // 2, nt), F32),
            jax.ShapeDtypeStruct((2, BK, zc), BF16),
            jax.ShapeDtypeStruct((2, BK, zc), BF16),
            pltpu.VMEM((others, KB, BK, BK), BF16),
            pltpu.VMEM((12, BK, w), BF16),
        ),
        in_specs=[SMEM, SMEM] + [VMEM] * 6 + [ANY],
        out_specs=(VMEM,) * 6,
        scratch_shapes=[
            pltpu.VMEM((4 * BK, w), BF16),
            pltpu.SemaphoreType.DMA((4,)),
            pltpu.SemaphoreType.DMA((3,)),
        ],
        compiler_params=params(10),
        cost_estimate=cost(4 * BK * w * (KB * BK + nt), 8 * 2**20),
    )(place, off, held(acc), held(f), intra, inter, held(t), held(m), stay(d))


def merge_kernel(after, a, b, out, *_):
    out[...] = (a[...].astype(F32) + b[...].astype(F32)).astype(BF16)


def merge(after, a, b, hold=False):
    shapes = [jax.ShapeDtypeStruct(b.shape, BF16)]
    if hold:
        shapes.append(jax.ShapeDtypeStruct(after.shape, after.dtype))
    out = pl.pallas_call(
        merge_kernel,
        out_shape=shapes,
        in_specs=[ANY, VMEM, VMEM],
        out_specs=[VMEM, ANY][: len(shapes)],
        input_output_aliases={0: 1} if hold else {},
        compiler_params=params(8),
    )(after, a, b)
    return out if hold else out[0]


def square_sum(x):
    x = x.astype(F32)
    return jnp.sum(x * x, axis=0, keepdims=True)


def orth_rows(c, t, p):
    return (c.astype(F32) - dot(t, p, ((1,), (1,)))).astype(BF16)


def orth_kernel(own, part, place, p, after, x_in, sq_in, f, t, x_out, sq, x_v, out_sems):
    nblk, _, nt = t.shape
    half = p.shape[0]
    core = core_of(place)
    side = core if own else 1 - core
    here = pl.ds(pl.multiple_of(side * half, half), half)
    stores = Loads(out_sems)
    total = None
    for at in range(part[0], part[1], 2):
        block = f[at : at + 2, :, here].reshape(2 * BK, half)
        x = orth_rows(block, t[at : at + 2].reshape(2 * BK, nt), p[...])
        x_v[at : at + 2] = x.reshape(2, BK, half)
        squares = square_sum(x)
        total = squares if total is None else total + squares
        stores.start(x_v.at[at : at + 2], x_out.at[at : at + 2, :, here])
    sq[...] = sq_in[...]
    sq[:, here] += total
    stores.wait_all()


def orthogonalize(own, part, place, p, after, x, sq, f, t):
    nblk, _, nt = t.shape
    half = p.shape[0]
    w = 2 * half
    return pl.pallas_call(
        functools.partial(orth_kernel, own, part),
        out_shape=(pltpu.HBM((nblk, BK, w), BF16), jax.ShapeDtypeStruct((1, w), F32)),
        in_specs=[SMEM, VMEM, ANY, ANY, VMEM, VMEM, VMEM],
        out_specs=(ANY, VMEM),
        input_output_aliases={} if x is None else {3: 0},
        scratch_shapes=[
            pltpu.VMEM((nblk, BK, half), BF16),
            pltpu.SemaphoreType.DMA((nblk // 2,)),
        ],
        compiler_params=params(7),
        cost_estimate=cost(nblk * BK * half * nt, 8 * 2**20),
    )(place, p, after, after if x is None else x, sq, held(f), held(t))


def chip_order(bits, side):
    return [(s + side) % bits for s in range(bits)]


def dipole_boundary_kernel(
    nblk, place, off, after, acc, f, near, tz_intra, tz_inter, t, d, send_0, send_1, keep, f_v, ys, sems
):
    groups, cols, lanes = keep.shape
    w = near.shape[2]
    bits = groups.bit_length() - 1
    loads = boundary_start(
        nblk, core_of(place), f, slice(w, cols), tz_intra, tz_inter, f_v, sems
    )
    boundary_rows(nblk, None, off, d, near, ys)
    boundary_rows(nblk, loads, off, d, f_v, ys, w)
    orders = [chip_order(bits, side) for side in (0, 1)]
    for at in range(0, cols, BK):
        here = slice(at, min(at + BK, cols))
        whole = boundary_sum(acc, ys, t, here)
        for g in range(groups):
            owned = []
            for side in (0, 1):
                chip = sum(
                    ((g >> (bits - 1 - s)) & 1) << orders[side][s] for s in range(bits)
                )
                first_lane = (2 * chip + side) * lanes
                owned.append(whole[:, first_lane : first_lane + lanes])
            keep[g, here, :] = jnp.where(core_of(place) == 0, owned[0], owned[1])
            send = (send_0, send_1)[2 * g // groups]
            away = jnp.where(core_of(place) == 0, owned[1], owned[0])
            send[g % (groups // 2), here, :] = away.astype(BF16)


def dipole_boundary(place, off, after, acc, f, near, tz, t, d, groups):
    nblk, _, nt = t.shape
    cols = acc.shape[0]
    lanes = nt // (2 * groups)
    return pl.pallas_call(
        functools.partial(dipole_boundary_kernel, nblk),
        out_shape=(
            jax.ShapeDtypeStruct((groups // 2, cols, lanes), BF16),
            jax.ShapeDtypeStruct((groups // 2, cols, lanes), BF16),
            jax.ShapeDtypeStruct((groups, cols, lanes), F32),
        ),
        in_specs=[SMEM, SMEM, ANY] + [VMEM] * 7,
        out_specs=(VMEM,) * 3,
        scratch_shapes=[
            pltpu.VMEM((12, BK, tz[0].shape[2]), BF16),
            pltpu.VMEM((4 * BK, cols), BF16),
            pltpu.SemaphoreType.DMA((4,)),
        ],
        compiler_params=params(9),
        cost_estimate=cost(4 * BK * cols * (KB * BK + nt), 8 * 2**20),
    )(place, off, after, held(acc), held(f), held(near), *tz, held(t), held(d))


def halve_kernel(step, place, after, keep, *refs):
    got, (send, kept) = refs[:-2], refs[-2:]
    half = kept.shape[0]
    orders = [chip_order(step[1], side)[step[0]] for side in (0, 1)]
    which = jnp.where(core_of(place) == 0, orders[0], orders[1])
    bit = jnp.bitwise_and(jnp.right_shift(place[0], which + 1), 1)

    def come(of, g):
        if len(got) == 1:
            return got[0][of * half + g].astype(F32)
        return jnp.where(of == 0, got[0][g], got[1][g]).astype(F32)

    for g in range(half):
        kept[g] = keep[bit * half + g] + come(bit, g)
        send[g] = (keep[(1 - bit) * half + g] + come(1 - bit, g)).astype(BF16)


def halve(step, place, after, keep, got):
    groups, cols, lanes = keep.shape
    half = groups // 2
    return pl.pallas_call(
        functools.partial(halve_kernel, step),
        out_shape=(
            jax.ShapeDtypeStruct((half, cols, lanes), BF16),
            jax.ShapeDtypeStruct((half, cols, lanes), F32),
        ),
        in_specs=[SMEM, ANY, VMEM] + [VMEM] * len(got),
        out_specs=(VMEM,) * 2,
        compiler_params=params(8),
    )(place, after, keep, *got)


def settle_kernel(w, after, keep, got, out):
    out[...] = (keep[0, w:, :] + got[0, w:, :].astype(F32)).astype(BF16)


def settle(w, after, keep, got):
    _, cols, lanes = keep.shape
    return pl.pallas_call(
        functools.partial(settle_kernel, w),
        out_shape=jax.ShapeDtypeStruct((cols - w, lanes), BF16),
        in_specs=[ANY, VMEM, VMEM],
        out_specs=VMEM,
        compiler_params=params(8),
    )(after, keep, got)


def stack_kernel(after, *refs):
    out, at = refs[-1], 0
    for piece in refs[:-1]:
        out[at : at + piece.shape[0], :] = piece[...]
        at += piece.shape[0]


def stack(after, pieces):
    rows = sum(piece.shape[0] for piece in pieces)
    return pl.pallas_call(
        stack_kernel,
        out_shape=jax.ShapeDtypeStruct((rows, pieces[0].shape[1]), BF16),
        in_specs=[ANY] + [VMEM] * len(pieces),
        out_specs=VMEM,
        compiler_params=params(8),
    )(after, *pieces)


def finish_kernel(rows, spots, place, z, keep, got, mine, other, sq, *refs):
    pieces, (out, g_v) = refs[:-2], refs[-2:]
    half, w = mine.shape[0], sq.shape[1]
    zc = keep.shape[1] - w
    at = 0
    for piece in pieces:
        for q in range(piece.shape[0] // zc):
            where = pl.multiple_of(jnp.bitwise_xor(z[0], spots[at]) * zc, zc)
            g_v[pl.ds(where, zc), :] = piece[q * zc : (q + 1) * zc, :]
            at += 1
    norm = 1.0 / jnp.sqrt(sq[...] / rows + 1e-06)
    for side in (0, 1):
        here = slice(side * half, (side + 1) * half)
        p = jnp.where(core_of(place) == side, mine[...], other[...])
        raw = keep[0, here, :] + got[0, here, :].astype(F32) - dot(p, g_v[...])
        out[:, here] = (raw.T * norm[:, here]).astype(BF16)


def finish(rows, spots, place, z, keep, got, mine, other, sq, pieces):
    _, cols, lanes = keep.shape
    nt = mine.shape[1]
    w = sq.shape[1]
    return pl.pallas_call(
        functools.partial(finish_kernel, rows, spots),
        out_shape=jax.ShapeDtypeStruct((lanes, w), BF16),
        in_specs=[SMEM, SMEM] + [VMEM] * (5 + len(pieces)),
        out_specs=VMEM,
        scratch_shapes=[pltpu.VMEM((nt, lanes), BF16)],
        compiler_params=params(8),
    )(place, z, keep, got, mine, other, sq, *pieces)


def swap(block, count, mask):
    return lax.ppermute(block, "basis", [(i, i ^ mask[i % 2]) for i in range(count)])


def meet(block, count):
    pairs = [(i, i + 1) for i in range(1, count - 1, 2)]
    return lax.ppermute(block, "basis", pairs + [(b, a) for a, b in pairs])


def exchange(intra, inter, count):
    inter = meet(inter, count)
    return swap(intra, count, (1, 1)), inter


def scalar(x):
    return x.astype(jnp.int32).reshape(1)


def on_device(cont_orbitals, target_orbitals, margin_blocks, dipole_blocks, band_offsets):
    count = lax.axis_size("basis")
    planes = lax.axis_size("orb")
    rows, w = cont_orbitals.shape
    nblk = rows // BK
    nt = target_orbitals.shape[1]
    zc = nt // planes
    chips = count // 2
    bits = chips.bit_length() - 1
    place_s = scalar(lax.axis_index("basis"))
    z = lax.axis_index("orb")
    z_s = scalar(z)
    off = band_offsets.astype(jnp.int32).T
    c = cont_orbitals.reshape(nblk, BK, w)
    t = target_orbitals.reshape(nblk, BK, nt)
    zero = jnp.zeros((1, w), F32)
    both = (1, 1)
    orders = [chip_order(bits, side) for side in (0, 1)]
    masks = [(2 << orders[0][s], 2 << orders[1][s]) for s in range(bits)]

    halos = exchange(*edges(place_s, c), count)
    p_acc, r_acc, f, t_v, m_edge = first(z_s, off, c, t, margin_blocks, dipole_blocks, zc)
    send, keep, *tz, d_rest, near = project_boundary(
        place_s, off, p_acc, f, *halos, t_v, m_edge, dipole_blocks
    )
    tz = exchange(*tz, count)
    part, r_acc = merge(r_acc, keep, swap(send, count, both), hold=True)

    for s in range(bits):
        got = swap(part, count, masks[s])
        if s == 0:
            r_acc, d_edge = middle(off, part, r_acc, f, t_v, dipole_blocks, d_rest)
            part, r_acc = merge(r_acc, part, got, hold=True)
            continue
        if s == 1:
            *sends, keep = dipole_boundary(
                place_s, off, part, r_acc, f, near, tz, t_v, d_edge, chips
            )
            got_r = [swap(send, count, both) for send in sends]
            send = sends[0]
        else:
            send, keep = halve((s - 2, bits), place_s, part, keep, got_r)
            got_r = [swap(send, count, masks[s - 2])]
        part = merge(send, part, got)
    other = swap(part, count, both)
    send, keep = halve((bits - 2, bits), place_s, part, keep, got_r)
    got_r = [swap(send, count, masks[bits - 2])]

    half = nblk // 4 * 2
    x, sq = orthogonalize(True, (0, nblk), place_s, part, part, None, zero, f, t_v)
    x, sq = orthogonalize(False, (0, half), place_s, other, part, x, sq, f, t_v)
    send, keep = halve((bits - 1, bits), place_s, sq, keep, got_r)
    got_r = [swap(send, count, masks[bits - 1])]
    x, sq = orthogonalize(False, (half, nblk), place_s, other, send, x, sq, f, t_v)
    tail = [both] + masks
    sq = sq + swap(sq, count, tail.pop(0))
    pieces = [settle(w, sq, keep, got_r[0])]
    spots, step = [0], planes // 2
    while step:
        whole = pieces[0]
        if len(pieces) > 1:
            if tail:
                sq = sq + swap(sq, count, tail.pop(0))
            whole = stack(sq, pieces)
        pieces.append(lax.ppermute(whole, "orb", [(i, i ^ step) for i in range(planes)]))
        spots += [spot ^ step for spot in spots]
        step //= 2
    for mask in tail:
        sq = sq + swap(sq, count, mask)
    dipole_mo = finish(rows * count, spots, place_s, z_s, keep, got_r[0], part, other, sq, pieces)
    return (x.reshape(rows, w), dipole_mo)


def solution(mesh):
    return jax.shard_map(
        on_device,
        mesh=mesh,
        in_specs=(
            P("basis", "orb"),
            P("basis", None),
            P("basis", None, None, None),
            P("basis", None, None, None),
            P("basis", None),
        ),
        out_specs=(P("basis", "orb"), P("basis", "orb")),
        check_vma=False,
    )
```

time: 81.6 us -> 76.9 us (0.942)
  waiting for transfers between devices: 24.6 us -> 18.2 us
  starting transfers between devices: 14.1 us -> 15.1 us
    pallas_call x8 -> x10, Pallas kernels: 19.6 us -> 25.6 us  [the longest x1 9.42 us: middle(): pl.pallas_call(functools.partial(middle_kernel, groups), out_shape=(pltpu...]
    pallas_call x1, Pallas kernels: 18.5 us -> 13 us  [first(): pl.pallas_call(functools.partial(first_kernel, nblk), out_shape=(pltpu.VM...]
    ppermute x11 -> x13, waiting for transfers between devices: 22.7 us -> 18.2 us  [swap(): lax.ppermute(block, 'basis', [(i, i ^ mask[i % 2]) for i in range(count)])]
    ppermute x2, waiting for transfers between devices: 1.95 us -> 0.01 us  [on_device(): lax.ppermute(whole, 'orb', [(i, i ^ step) for i in range(planes)])]
    ppermute x1 -> x2, starting transfers between devices: 0.7 us -> 1.53 us  [meet(): return lax.ppermute(block, 'basis', pairs + [(b, a) for a, b in pairs])]
    ppermute x11 -> x13, starting transfers between devices: 9.09 us -> 9.24 us  [swap(): lax.ppermute(block, 'basis', [(i, i ^ mask[i % 2]) for i in range(count)])]
  transfers between devices with their start and end apart: 14 -> 17, of which waited for: 10 -> 8; matrix products, arithmetic and copies ran while one was open for 0% -> 0% of each run, Pallas kernels for 43% -> 48%
where the time goes in v3:
time: 76.9 us; the launch traced here: 76.8 us
  Pallas kernels  42.6 us (55%)
  waiting for transfers between devices  18.2 us (24%)
  starting transfers between devices  15.1 us (20%)
  between operations  0.87 us (1%)
    ppermute x13, waiting for transfers between devices, swap(): lax.ppermute(block, 'basis', [(i, i ^ mask[i % 2]) for i in range(count)])  18.2 us
    pallas_call x1, Pallas kernels, first(): pl.pallas_call(functools.partial(first_kernel, nblk), out_shape=(pltpu.VM...  13 us
    pallas_call x1, Pallas kernels, middle(): pl.pallas_call(functools.partial(middle_kernel, groups), out_shape=(pltpu...  9.42 us
    ppermute x13, starting transfers between devices, swap(): lax.ppermute(block, 'basis', [(i, i ^ mask[i % 2]) for i in range(count)])  9.24 us
    pallas_call x3, Pallas kernels, orthogonalize(): pl.pallas_call(functools.partial(orth_kernel, own, part), out_shape=(pltp...  8.54 us
    pallas_call x1, Pallas kernels, dipole_boundary(): pl.pallas_call(functools.partial(dipole_boundary_kernel, nblk), out_shape...  4.85 us
    ppermute x2, starting transfers between devices, on_device(): lax.ppermute(whole, 'orb', [(i, i ^ step) for i in range(planes)])  4.3 us
    pallas_call x1, Pallas kernels, project_boundary(): pl.pallas_call(functools.partial(boundary_kernel, nblk), out_shape=(jax.S...  3.61 us
  transfers between devices with their start and end apart: 17, of which 8 were waited for; matrix products, arithmetic and copies ran while one was open for 0% of the time, Pallas kernels for 48%

profile of v3, /device:TPU:0, one launch (start us, length us, event | category | flops | bytes accessed | tf_op | source)
XLA Modules:
  0.0 76.8 jit_solution(1813793681261416757)
XLA Ops:
  0.6 1.2 %shard_map.69 = (bf16[2,256,512]{2,1,0:T(8,128)(2,1)S(1)}, bf16[2,256,512]{2,1,0:T(8,128)(2,1)S(1)}) custom-call(s32[1]{0:T(128)} %bitcast.place, bf16[16,256,512]{2,1,0:T(8,128)(2,1)} %bitcast.11), custom_call_target="tpu_custom_call" | custom-call | tf_op jit(solution)/shard_map/pallas_call | solution.py:107
  1.9 0.5 collective-permute-start
  2.4 0.7 collective-permute-start.1
  3.1 13.0 %shard_map.68 = (f32[512,1024]{1,0:T(8,128)S(1)}, f32[768,1024]{1,0:T(8,128)S(1)}, bf16[16,256,768]{2,1,0:T(8,128)(2,1)S(1)}, bf16[16,256,1024]{2,1,0:T(8,128)(2,1)S(1)}, bf16[4,4,256,256]{3,2,1,0:T(8,128)(2,1)S(1)}) custom-call(s32[1]{0:T(128)} %bitcast.2.z, s32[4,16]{1,0:T(4,128)S(1)} %bitcast.6, bf16[16,256,512]{2,1,0:T(8,128)(2,1)} %bitcast.12, ...), custom_call_target="tpu_custom_call" | custom-call | flops 8053063680 | bytes 31457280 | tf_op jit(solution)/shard_map/pallas_call | solution.py:187
  16.1 3.6 %shard_map.70 = (bf16[256,1024]{1,0:T(8,128)(2,1)S(1)}, f32[256,1024]{1,0:T(8,128)S(1)}, bf16[2,256,256]{2,1,0:T(8,128)(2,1)S(1)}, bf16[2,256,256]{2,1,0:T(8,128...) custom-call(s32[1]{0:T(128)} %bitcast.place, s32[4,16]{1,0:T(4,128)S(1)} %bitcast.7, ...), custom_call_target="tpu_custom_call" | custom-call | flops 2147483648 | bytes 8388608 | tf_op jit(solution)/shard_map/pallas_call | solution.py:298
  19.7 3.9 %collective-permute-start.2 = (bf16[256,1024]{1,0:T(8,128)(2,1)S(1)}, bf16[256,1024]{1,0:T(8,128)(2,1)S(1)}, u32[]{:S(2)}, u32[]{:S(2)}) collective-permute-start(bf16[256,1024]{1,0:T(8,128)(2,1)S(1)} %get-tuple-element.42), channel_id=1, source_target_pairs={{0,4},{4,0},{8,12},{12,8},{16,20},{20,16},{24,28},{28,24},{1,5},{5... | collective-permute-start | bytes 1572872 | tf_op jit(solution)/shard_map/ppermute | solution.py:541
  23.7 0.8 %collective-permute-start.5 = (bf16[2,256,256]{2,1,0:T(8,128)(2,1)S(1)}, bf16[2,256,256]{2,1,0:T(8,128)(2,1)S(1)}, u32[]{:S(2)}, u32[]{:S(2)}) collective-permute-start(bf16[2,256,256]{2,1,0:T(8,128)(2,1)S(1)} %get-tuple-element.51), channel_id=1, source_target_pairs={{4,8},{12,16},{20,24},{8,4},{16,12},{24,20},{5,9},{13,17},{21,25},... | collective-permute-start | bytes 786440 | tf_op jit(solution)/shard_map/ppermute | solution.py:546
  24.6 0.6 collective-permute-done.2.b
  25.2 0.1 shard_map.71
  25.3 2.8 %collective-permute-start.3 = (bf16[256,1024]{1,0:T(8,128)(2,1)S(1)}, bf16[256,1024]{1,0:T(8,128)(2,1)S(1)}, u32[]{:S(2)}, u32[]{:S(2)}) collective-permute-start(bf16[256,1024]{1,0:T(8,128)(2,1)S(1)} %get-tuple-element.43.after.a), channel_id=1, source_target_pairs={{0,8},{4,20},{8,0},{12,28},{16,24},{20,4},{24,16},{28,12},{1,9},{5... | collective-permute-start | bytes 1572872 | tf_op jit(solution)/shard_map/ppermute | solution.py:541
  28.1 9.4 %shard_map.72 = (f32[768,1024]{1,0:T(8,128)S(1)}, bf16[4,4,256,256]{3,2,1,0:T(8,128)(2,1)S(1)}) custom-call(s32[4,16]{1,0:T(4,128)S(1)} %bitcast.8, bf16[256,1024]{1,0:T(8,128)(2,1)S(1)} %get-tuple-element.43.after.a, f32[768,1024]{1,0:T(8,128)S(1)} %get-tuple-element.44.acc, bf16[16,256,768]{2,1,0:T(8,128)(2,1)S(1)} %get-tuple-element.36.f, ...), custom_call_target="tpu_custom_call" | custom-call | flops 8053063680 | bytes 14680064 | tf_op jit(solution)/shard_map/pallas_call | solution.py:227
  37.5 3.0 %collective-permute-done.3.b = bf16[256,1024]{1,0:T(8,128)(2,1)S(1)} collective-permute-done((bf16[256,1024]{1,0:T(8,128)(2,1)S(1)}, bf16[256,1024]{1,0:T(8,128)(2,1)S(1)}, u32[]{:S(2)}, u32[]{:S(2)}) %collective-permute-start.3) | collective-permute-done | bytes 524320 | tf_op jit(solution)/shard_map/ppermute | solution.py:541
  40.5 0.1 shard_map.73
  40.7 4.8 %shard_map.74 = (bf16[2,768,128]{2,1,0:T(8,128)(2,1)S(1)}, bf16[2,768,128]{2,1,0:T(8,128)(2,1)S(1)}, f32[4,768,128]{2,1,0:T(8,128)S(1)}) custom-call(s32[1]{0:T(128)} %bitcast.place, s32[4,16]{1,0:T(4,128)S(1)} %bitcast.9, bf16[256,1024]{1,0:T(8,128)(2,1)S(1)} %get-tuple-element.47.after.a, f32[768,1024]{1,0:T(8,128)S(1)} %get-tuple-element.48.acc, ...), custom_call_target="tpu_custom_call" | custom-call | flops 3221225472 | bytes 8388608 | tf_op jit(solution)/shard_map/pallas_call | solution.py:424
  45.6 0.5 collective-permute-start.9
  46.1 3.7 %collective-permute-done.6.b = bf16[256,1024]{1,0:T(8,128)(2,1)S(1)} collective-permute-done((bf16[256,1024]{1,0:T(8,128)(2,1)S(1)}, bf16[256,1024]{1,0:T(8,128)(2,1)S(1)}, u32[]{:S(2)}, u32[]{:S(2)}) %collective-permute-start.6) | collective-permute-done | bytes 524320 | tf_op jit(solution)/shard_map/ppermute | solution.py:541
  49.8 0.1 shard_map.75.p.after.x_in.mine
  50.1 0.3 shard_map.78
  50.5 3.8 %shard_map.76 = (bf16[16,256,512]{2,1,0:T(8,128)(2,1)}, f32[1,512]{1,0:T(1,128)S(1)}) custom-call(s32[1]{0:T(128)} %bitcast.place, bf16[256,1024]{1,0:T(8,128)(2,1)S(1)} %shard_map.75.p.after.x_in.mine, bf16[256,1024]{1,0:T(8,128)(2,1)S(1)} %shard_map.75.p.after.x_in.mine, bf16[256,1024]{1,0:T(8,128)(2,1)S(1)} %shard_map.75.p.after.x_in.mine, ...), custom_call_target="tpu_custom_call" | custom-call | flops 2147483648 | bytes 8388608 | tf_op jit(solution)/shard_map/pallas_call | solution.py:372
  54.2 2.4 %shard_map.77 = (bf16[16,256,512]{2,1,0:T(8,128)(2,1)}, f32[1,512]{1,0:T(1,128)S(1)}) custom-call(s32[1]{0:T(128)} %bitcast.place, bf16[256,1024]{1,0:T(8,128)(2,1)S(1)} %collective-permute-done.7.p.other, bf16[256,1024]{1,0:T(8,128)(2,1)S(1)} %shard_map.75.p.after.x_in.mine, ...), custom_call_target="tpu_custom_call", output_to_operand_aliasing={{0}: (3, {})} | custom-call | flops 2147483648 | bytes 8388608 | tf_op jit(solution)/shard_map/pallas_call | solution.py:372
  56.6 1.6 %collective-permute-done.10.refs_0_ = bf16[2,768,128]{2,1,0:T(8,128)(2,1)S(1)} collective-permute-done((bf16[2,768,128]{2,1,0:T(8,128)(2,1)S(1)}, bf16[2,768,128]{2,1,0:T(8,128)(2,1)S(1)}, u32[]{:S(2)}, u32[]{:S(2)}) %collective-permute-start.10) | collective-permute-done | bytes 393248 | tf_op jit(solution)/shard_map/ppermute | solution.py:541
  58.3 0.4 collective-permute-start.11
  58.7 2.4 %shard_map.80 = (bf16[16,256,512]{2,1,0:T(8,128)(2,1)}, f32[1,512]{1,0:T(1,128)S(1)}) custom-call(s32[1]{0:T(128)} %bitcast.place, bf16[256,1024]{1,0:T(8,128)(2,1)S(1)} %collective-permute-done.7.p.other, bf16[1,768,128]{2,1,0:T(8,128)(2,1)S(1)} %get-tuple-element.61.after, ...), custom_call_target="tpu_custom_call", output_to_operand_aliasing={{0}: (3, {})} | custom-call | flops 2147483648 | bytes 8388608 | tf_op jit(solution)/shard_map/pallas_call | solution.py:372
  61.1 1.1 %collective-permute-done.12 = f32[1,512]{1,0:T(1,128)S(1)} collective-permute-done((f32[1,512]{1,0:T(1,128)S(1)}, f32[1,512]{1,0:T(1,128)S(1)}, u32[]{:S(2)}, u32[]{:S(2)}) %collective-permute-start.12) | collective-permute-done | bytes 2080 | tf_op jit(solution)/shard_map/ppermute | solution.py:541
  62.3 1.8 %collective-permute-done.11.got = bf16[1,768,128]{2,1,0:T(8,128)(2,1)S(1)} collective-permute-done((bf16[1,768,128]{2,1,0:T(8,128)(2,1)S(1)}, bf16[1,768,128]{2,1,0:T(8,128)(2,1)S(1)}, u32[]{:S(2)}, u32[]{:S(2)}) %collective-permute-start.11) | collective-permute-done | bytes 196640 | tf_op jit(solution)/shard_map/ppermute | solution.py:541
  64.1 2.6 %collective-permute-start.15 = (bf16[256,128]{1,0:T(8,128)(2,1)S(1)}, bf16[256,128]{1,0:T(8,128)(2,1)S(1)}, u32[]{:S(2)}, u32[]{:S(2)}) collective-permute-start(bf16[256,128]{1,0:T(8,128)(2,1)S(1)} %shard_map.81.refs_0_), channel_id=1, source_target_pairs={{0,2},{1,3},{2,0},{3,1},{4,6},{5,7},{6,4},{7,5},{8,10},{9,11},{10,... | collective-permute-start | bytes 196616 | tf_op jit(solution)/shard_map/ppermute | solution.py:622
  66.7 0.5 collective-permute-start.13
  67.2 3.1 %collective-permute-done.13 = f32[1,512]{1,0:T(1,128)S(1)} collective-permute-done((f32[1,512]{1,0:T(1,128)S(1)}, f32[1,512]{1,0:T(1,128)S(1)}, u32[]{:S(2)}, u32[]{:S(2)}) %collective-permute-start.13) | collective-permute-done | bytes 2080 | tf_op jit(solution)/shard_map/ppermute | solution.py:541
  70.3 1.6 %collective-permute-start.16 = (bf16[512,128]{1,0:T(8,128)(2,1)S(1)}, bf16[512,128]{1,0:T(8,128)(2,1)S(1)}, u32[]{:S(2)}, u32[]{:S(2)}) collective-permute-start(bf16[512,128]{1,0:T(8,128)(2,1)S(1)} %shard_map.82), channel_id=1, source_target_pairs={{0,1},{1,0},{2,3},{3,2},{4,5},{5,4},{6,7},{7,6},{8,9},{9,8},{10,11... | collective-permute-start | bytes 393224 | tf_op jit(solution)/shard_map/ppermute | solution.py:622
  72.0 0.3 collective-permute-start.14
  72.3 3.3 %collective-permute-done.14 = f32[1,512]{1,0:T(1,128)S(1)} collective-permute-done((f32[1,512]{1,0:T(1,128)S(1)}, f32[1,512]{1,0:T(1,128)S(1)}, u32[]{:S(2)}, u32[]{:S(2)}) %collective-permute-start.14) | collective-permute-done | bytes 2080 | tf_op jit(solution)/shard_map/ppermute | solution.py:541
  75.6 1.2 %shard_map.83 = bf16[128,512]{1,0:T(8,128)(2,1)} custom-call(s32[1]{0:T(128)} %bitcast.place, s32[1]{0:T(128)} %bitcast.2.z, f32[1,768,128]{2,1,0:T(8,128)S(1)} %get-tuple-element.64.keep, bf16[1,768,128]{2,1,0:T(8,128)(2,1)S(1)} %collective-permute-done.11.got, bf16[256,1024]{1,0:T(8,128)(2,1)S(1)} %shard_map.75.p.after.x_in.mine, ...), custom_call_target="tpu_custom_call" | custom-call | tf_op jit(solution)/shard_map/pallas_call | solution.py:530
  (24 shorter events, 0.6 us)
Async XLA Ops:
  0.6 2.5 %copy-start = (s32[16,4]{0,1:T(4,128)S(1)}, s32[16,4]{0,1:T(4,128)}, u32[]{:S(2)}) copy-start(s32[16,4]{0,1:T(4,128)} %param.9) | copy-start | bytes 772
  1.9 14.2 %collective-permute-start = (bf16[2,256,512]{2,1,0:T(8,128)(2,1)S(1)}, bf16[2,256,512]{2,1,0:T(8,128)(2,1)S(1)}, u32[]{:S(2)}, u32[]{:S(2)}) collective-permute-start(bf16[2,256,512]{2,1,0:T(8,128)(2,1)S(1)} %get-tuple-element.37), channel_id=1, source_target_pairs={{0,4},{4,0},{8,12},{12,8},{16,20},{20,16},{24,28},{28,24},{1,5},{5... | collective-permute-start | bytes 1572872 | tf_op jit(solution)/shard_map/ppermute | solution.py:541
  2.4 13.7 %collective-permute-start.1 = (bf16[2,256,512]{2,1,0:T(8,128)(2,1)S(1)}, bf16[2,256,512]{2,1,0:T(8,128)(2,1)S(1)}, u32[]{:S(2)}, u32[]{:S(2)}) collective-permute-start(bf16[2,256,512]{2,1,0:T(8,128)(2,1)S(1)} %get-tuple-element.38), channel_id=1, source_target_pairs={{4,8},{12,16},{20,24},{8,4},{16,12},{24,20},{5,9},{13,17},{21,25},... | collective-permute-start | bytes 1572872 | tf_op jit(solution)/shard_map/ppermute | solution.py:546
  19.7 5.5 %collective-permute-start.2 = (bf16[256,1024]{1,0:T(8,128)(2,1)S(1)}, bf16[256,1024]{1,0:T(8,128)(2,1)S(1)}, u32[]{:S(2)}, u32[]{:S(2)}) collective-permute-start(bf16[256,1024]{1,0:T(8,128)(2,1)S(1)} %get-tuple-element.42), channel_id=1, source_target_pairs={{0,4},{4,0},{8,12},{12,8},{16,20},{20,16},{24,28},{28,24},{1,5},{5... | collective-permute-start | bytes 1572872 | tf_op jit(solution)/shard_map/ppermute | solution.py:541
  23.7 17.0 %collective-permute-start.4 = (bf16[2,256,256]{2,1,0:T(8,128)(2,1)S(1)}, bf16[2,256,256]{2,1,0:T(8,128)(2,1)S(1)}, u32[]{:S(2)}, u32[]{:S(2)}) collective-permute-start(bf16[2,256,256]{2,1,0:T(8,128)(2,1)S(1)} %get-tuple-element.50), channel_id=1, source_target_pairs={{0,4},{4,0},{8,12},{12,8},{16,20},{20,16},{24,28},{28,24},{1,5},{5... | collective-permute-start | bytes 786440 | tf_op jit(solution)/shard_map/ppermute | solution.py:541
  23.7 16.9 %collective-permute-start.5 = (bf16[2,256,256]{2,1,0:T(8,128)(2,1)S(1)}, bf16[2,256,256]{2,1,0:T(8,128)(2,1)S(1)}, u32[]{:S(2)}, u32[]{:S(2)}) collective-permute-start(bf16[2,256,256]{2,1,0:T(8,128)(2,1)S(1)} %get-tuple-element.51), channel_id=1, source_target_pairs={{4,8},{12,16},{20,24},{8,4},{16,12},{24,20},{5,9},{13,17},{21,25},... | collective-permute-start | bytes 786440 | tf_op jit(solution)/shard_map/ppermute | solution.py:546
  25.3 15.1 %collective-permute-start.3 = (bf16[256,1024]{1,0:T(8,128)(2,1)S(1)}, bf16[256,1024]{1,0:T(8,128)(2,1)S(1)}, u32[]{:S(2)}, u32[]{:S(2)}) collective-permute-start(bf16[256,1024]{1,0:T(8,128)(2,1)S(1)} %get-tuple-element.43.after.a), channel_id=1, source_target_pairs={{0,8},{4,20},{8,0},{12,28},{16,24},{20,4},{24,16},{28,12},{1,9},{5... | collective-permute-start | bytes 1572872 | tf_op jit(solution)/shard_map/ppermute | solution.py:541
  40.6 9.2 %collective-permute-start.6 = (bf16[256,1024]{1,0:T(8,128)(2,1)S(1)}, bf16[256,1024]{1,0:T(8,128)(2,1)S(1)}, u32[]{:S(2)}, u32[]{:S(2)}) collective-permute-start(bf16[256,1024]{1,0:T(8,128)(2,1)S(1)} %get-tuple-element.47.after.a), channel_id=1, source_target_pairs={{0,16},{4,12},{8,24},{12,4},{16,0},{20,28},{24,8},{28,20},{1,17},{... | collective-permute-start | bytes 1572872 | tf_op jit(solution)/shard_map/ppermute | solution.py:541
  45.5 4.5 %collective-permute-start.8 = (bf16[2,768,128]{2,1,0:T(8,128)(2,1)S(1)}, bf16[2,768,128]{2,1,0:T(8,128)(2,1)S(1)}, u32[]{:S(2)}, u32[]{:S(2)}) collective-permute-start(bf16[2,768,128]{2,1,0:T(8,128)(2,1)S(1)} %get-tuple-element.53.after), channel_id=1, source_target_pairs={{0,4},{4,0},{8,12},{12,8},{16,20},{20,16},{24,28},{28,24},{1,5},{5... | collective-permute-start | bytes 1179656 | tf_op jit(solution)/shard_map/ppermute | solution.py:541
  45.6 4.4 %collective-permute-start.9 = (bf16[2,768,128]{2,1,0:T(8,128)(2,1)S(1)}, bf16[2,768,128]{2,1,0:T(8,128)(2,1)S(1)}, u32[]{:S(2)}, u32[]{:S(2)}) collective-permute-start(bf16[2,768,128]{2,1,0:T(8,128)(2,1)S(1)} %get-tuple-element.58), channel_id=1, source_target_pairs={{0,4},{4,0},{8,12},{12,8},{16,20},{20,16},{24,28},{28,24},{1,5},{5... | collective-permute-start | bytes 1179656 | tf_op jit(solution)/shard_map/ppermute | solution.py:541
  50.0 4.3 %collective-permute-start.7 = (bf16[256,1024]{1,0:T(8,128)(2,1)S(1)}, bf16[256,1024]{1,0:T(8,128)(2,1)S(1)}, u32[]{:S(2)}, u32[]{:S(2)}) collective-permute-start(bf16[256,1024]{1,0:T(8,128)(2,1)S(1)} %shard_map.75.p.after.x_in.mine), channel_id=1, source_target_pairs={{0,4},{4,0},{8,12},{12,8},{16,20},{20,16},{24,28},{28,24},{1,5},{5... | collective-permute-start | bytes 1572872 | tf_op jit(solution)/shard_map/ppermute | solution.py:541
  50.4 7.8 %collective-permute-start.10 = (bf16[2,768,128]{2,1,0:T(8,128)(2,1)S(1)}, bf16[2,768,128]{2,1,0:T(8,128)(2,1)S(1)}, u32[]{:S(2)}, u32[]{:S(2)}) collective-permute-start(bf16[2,768,128]{2,1,0:T(8,128)(2,1)S(1)} %get-tuple-element.60), channel_id=1, source_target_pairs={{0,8},{4,20},{8,0},{12,28},{16,24},{20,4},{24,16},{28,12},{1,9},{5... | collective-permute-start | bytes 1179656 | tf_op jit(solution)/shard_map/ppermute | solution.py:541
  58.3 5.7 %collective-permute-start.11 = (bf16[1,768,128]{2,1,0:T(8,128)(2,1)S(1)}, bf16[1,768,128]{2,1,0:T(8,128)(2,1)S(1)}, u32[]{:S(2)}, u32[]{:S(2)}) collective-permute-start(bf16[1,768,128]{2,1,0:T(8,128)(2,1)S(1)} %get-tuple-element.61.after), channel_id=1, source_target_pairs={{0,16},{4,12},{8,24},{12,4},{16,0},{20,28},{24,8},{28,20},{1,17},{... | collective-permute-start | bytes 589832 | tf_op jit(solution)/shard_map/ppermute | solution.py:541
  61.1 1.2 %collective-permute-start.12 = (f32[1,512]{1,0:T(1,128)S(1)}, f32[1,512]{1,0:T(1,128)S(1)}, u32[]{:S(2)}, u32[]{:S(2)}) collective-permute-start(f32[1,512]{1,0:T(1,128)S(1)} %get-tuple-element.65), channel_id=1, source_target_pairs={{0,4},{4,0},{8,12},{12,8},{16,20},{20,16},{24,28},{28,24},{1,5},{5... | collective-permute-start | bytes 6152 | tf_op jit(solution)/shard_map/ppermute | solution.py:541
  64.1 6.2 %collective-permute-start.15 = (bf16[256,128]{1,0:T(8,128)(2,1)S(1)}, bf16[256,128]{1,0:T(8,128)(2,1)S(1)}, u32[]{:S(2)}, u32[]{:S(2)}) collective-permute-start(bf16[256,128]{1,0:T(8,128)(2,1)S(1)} %shard_map.81.refs_0_), channel_id=1, source_target_pairs={{0,2},{1,3},{2,0},{3,1},{4,6},{5,7},{6,4},{7,5},{8,10},{9,11},{10,... | collective-permute-start | bytes 196616 | tf_op jit(solution)/shard_map/ppermute | solution.py:622
  66.7 3.6 %collective-permute-start.13 = (f32[1,512]{1,0:T(1,128)S(1)}, f32[1,512]{1,0:T(1,128)S(1)}, u32[]{:S(2)}, u32[]{:S(2)}) collective-permute-start(f32[1,512]{1,0:T(1,128)S(1)} %add.9.after), channel_id=1, source_target_pairs={{0,8},{4,20},{8,0},{12,28},{16,24},{20,4},{24,16},{28,12},{1,9},{5... | collective-permute-start | bytes 6152 | tf_op jit(solution)/shard_map/ppermute | solution.py:541
  70.3 5.2 %collective-permute-start.16 = (bf16[512,128]{1,0:T(8,128)(2,1)S(1)}, bf16[512,128]{1,0:T(8,128)(2,1)S(1)}, u32[]{:S(2)}, u32[]{:S(2)}) collective-permute-start(bf16[512,128]{1,0:T(8,128)(2,1)S(1)} %shard_map.82), channel_id=1, source_target_pairs={{0,1},{1,0},{2,3},{3,2},{4,5},{5,4},{6,7},{7,6},{8,9},{9,8},{10,11... | collective-permute-start | bytes 393224 | tf_op jit(solution)/shard_map/ppermute | solution.py:622
  72.0 3.6 %collective-permute-start.14 = (f32[1,512]{1,0:T(1,128)S(1)}, f32[1,512]{1,0:T(1,128)S(1)}, u32[]{:S(2)}, u32[]{:S(2)}) collective-permute-start(f32[1,512]{1,0:T(1,128)S(1)} %add.10.after), channel_id=1, source_target_pairs={{0,16},{4,12},{8,24},{12,4},{16,0},{20,28},{24,8},{28,20},{1,17},{... | collective-permute-start | bytes 6152 | tf_op jit(solution)/shard_map/ppermute | solution.py:541

commit v4 on v3

--- a/solution.py
+++ b/solution.py
@@ -9,7 +9,9 @@
 
 BK = 256
 KB = 4
-LEAD = 2
+LEAD = 1
+LAST = 2
+MOST = 5
 F32 = jnp.float32
 BF16 = jnp.bfloat16
 ANY = pl.BlockSpec(memory_space=pl.ANY)
@@ -94,30 +96,40 @@
     return pltpu.with_memory_space_constraint(x, pltpu.VMEM)
 
 
-def edge_kernel(place, c, intra, inter, sems):
+def edge_kernel(place, z, c, t, intra, inter, tz_inter, sems):
     last = c.shape[0] - 2
+    w = c.shape[2]
+    zc = intra.shape[2] - w
     loads = Loads(sems)
-    loads.start(c.at[pl.ds(core_of(place) * last, 2)], inter)
-    loads.start(c.at[pl.ds((1 - core_of(place)) * last, 2)], intra)
+    near, far = (1 - core_of(place)) * last, core_of(place) * last
+    loads.start(c.at[pl.ds(near, 2)], intra.at[:, :, 0:w])
+    loads.start(t.at[pl.ds(near, 2), :, columns(z[0], zc)], intra.at[:, :, w : w + zc])
+    loads.start(c.at[pl.ds(far, 2)], inter)
+    loads.start(t.at[pl.ds(far, 2), :, columns(z[0], zc)], tz_inter)
     loads.wait_all()
 
 
-def edges(place, c):
-    pair = jax.ShapeDtypeStruct((2,) + c.shape[1:], BF16)
+def edges(place, z, c, t, zc):
+    w = c.shape[2]
     return pl.pallas_call(
         edge_kernel,
-        out_shape=(pair, pair),
-        in_specs=[SMEM, ANY],
-        out_specs=(VMEM, VMEM),
-        scratch_shapes=[pltpu.SemaphoreType.DMA((2,))],
+        out_shape=(
+            jax.ShapeDtypeStruct((2, BK, w + zc), BF16),
+            jax.ShapeDtypeStruct((2, BK, w), BF16),
+            jax.ShapeDtypeStruct((2, BK, zc), BF16),
+        ),
+        in_specs=[SMEM, SMEM, ANY, ANY],
+        out_specs=(VMEM,) * 3,
+        scratch_shapes=[pltpu.SemaphoreType.DMA((4,))],
         compiler_params=params(8),
-    )(place, stay(c))
+    )(place, z, stay(c), stay(t))
 
 
 def lead_of(nblk):
     inner = list(range(2, nblk - 2))
-    rest = inner[LEAD:]
-    return inner[:LEAD], [rest[i : i + 4] for i in range(0, len(rest), 4)]
+    rest, last = inner[LEAD : len(inner) - LAST], inner[len(inner) - LAST :]
+    size = -(-len(rest) // -(-len(rest) // MOST))
+    return inner[:LEAD], [rest[i : i + size] for i in range(0, len(rest), size)], last
 
 
 def first_kernel(
@@ -126,28 +138,20 @@
     w = c.shape[2]
     zc = f.shape[2] - w
     loads = Loads(sems, 8)
-    lead, _ = lead_of(nblk)
-    have, needs = 0, []
+    lead, _, _ = lead_of(nblk)
+    needs = []
     for g, rows in enumerate(groups_of(nblk)):
         lo, hi = rows[0], rows[-1] + 1
-        mid = min(lo + 2, hi)
+        cuts = [lo, lo + 1, lo + 2, hi] if g == 0 else [lo, lo + 2, hi]
         want = []
-        for part in ((lo, mid), (mid, hi)):
-            if part[0] == part[1]:
-                continue
-            upto = part[1] + 2
-            ids = []
-            if upto > have:
-                ids.append(loads.start(c.at[have:upto], f.at[have:upto, :, 0:w]))
-                have = upto
-            ids.append(
-                loads.start(m.at[part[0] : part[1]], m_v.at[part[0] - 2 : part[1] - 2])
-            )
-            want.append((list(range(*part)), ids))
+        for part in zip(cuts[:-1], cuts[1:]):
+            m_id = loads.start(m.at[part[0] : part[1]], m_v.at[part[0] - 2 : part[1] - 2])
+            want.append((list(range(*part)), m_id))
         t_id = loads.start(t.at[lo:hi], t_v.at[lo:hi])
         d_ids = ()
         if g == 0:
             near = lead[-1] + 3
+            whole = loads.start(c, f.at[:, :, 0:w])
             d_ids = (
                 loads.start(d.at[lead[0] : lead[-1] + 1], d_v),
                 loads.start(t.at[0:near, :, columns(z[0], zc)], f.at[0:near, :, w : w + zc]),
@@ -159,17 +163,17 @@
     loads.start(t.at[near:nblk, :, columns(z[0], zc)], f.at[near:nblk, :, w : w + zc])
     for g, (rows, want, t_id, d_ids) in enumerate(needs):
         at = 0
-        for part, ids in want:
-            loads.wait(*ids)
+        for part, m_id in want:
+            loads.wait(m_id)
             band_rows(
-                part, [b - 2 for b in part], off, f, w, m_v, 0,
+                part, [b - 2 for b in part], off, c, w, m_v, 0,
                 ys.at[at * BK : (at + len(part)) * BK],
             )
             at += len(part)
         loads.wait(t_id)
         project(p_out, None if g == 0 else p_out, ys, t_v, rows[0], len(rows))
         if d_ids:
-            loads.wait(*d_ids)
+            loads.wait(*d_ids, whole)
             band_rows(lead, range(len(lead)), off, f, w + zc, d_v, 0, yd)
             project(r_out, None, yd, t_v, lead[0], len(lead))
         if g == 1:
@@ -193,18 +197,18 @@
             pltpu.VMEM((nblk, BK, nt), BF16),
             pltpu.VMEM((4, KB, BK, BK), BF16),
         ),
-        in_specs=[SMEM, SMEM, ANY, ANY, ANY, ANY],
+        in_specs=[SMEM, SMEM, VMEM, ANY, ANY, ANY],
         out_specs=(VMEM,) * 5,
         scratch_shapes=[
             pltpu.VMEM((inner, KB, BK, BK), BF16),
             pltpu.VMEM((count, KB, BK, BK), BF16),
             pltpu.VMEM((4 * BK, w), BF16),
             pltpu.VMEM((count * BK, w + zc), BF16),
-            pltpu.SemaphoreType.DMA((5 * len(groups_of(nblk)) + 7,)),
+            pltpu.SemaphoreType.DMA((5 * len(groups_of(nblk)) + 9,)),
         ],
         compiler_params=params(15),
         cost_estimate=cost(macs, 30 * 2**20),
-    )(z, off, stay(c), stay(t), stay(m), stay(d))
+    )(z, off, held(c), stay(t), stay(m), stay(d))
 
 
 def middle_kernel(groups, off, after, acc, f, t, d, d_rest, out, d_edge, yd, sems):
@@ -220,17 +224,17 @@
 
 
 def middle(off, after, acc, f, t, d, d_rest):
-    nblk, _, cols = f.shape
-    nt = t.shape[2]
+    nblk, _, nt = t.shape
+    cols = acc.shape[0]
     groups = lead_of(nblk)[1]
     count = sum(map(len, groups))
     return pl.pallas_call(
         functools.partial(middle_kernel, groups),
         out_shape=(pltpu.VMEM((cols, nt), F32), pltpu.VMEM((4, KB, BK, BK), BF16)),
-        in_specs=[SMEM, ANY, VMEM, VMEM, VMEM, ANY, VMEM],
+        in_specs=[SMEM, ANY] + [VMEM] * 3 + [ANY, VMEM],
         out_specs=(VMEM, VMEM),
         scratch_shapes=[
-            pltpu.VMEM((4 * BK, cols), BF16),
+            pltpu.VMEM((MOST * BK, cols), BF16),
             pltpu.SemaphoreType.DMA((2,)),
         ],
         compiler_params=params(6),
@@ -238,13 +242,13 @@
     )(off, after, held(acc), held(f), held(t), stay(d), held(d_rest))
 
 
-def boundary_start(nblk, core, f, cols, intra, inter, f_v, sems):
+def boundary_start(nblk, core, f, intra, inter, f_v, sems):
     loads = Loads(sems)
     low = 10 * (1 - core)
-    loads.start(f.at[0:4, :, cols], f_v.at[2:6])
+    loads.start(f.at[0:4], f_v.at[2:6])
     loads.start(intra, f_v.at[pl.ds(low, 2)])
     loads.start(inter, f_v.at[pl.ds(10 - low, 2)])
-    loads.start(f.at[nblk - 4 : nblk, :, cols], f_v.at[6:10])
+    loads.start(f.at[nblk - 4 : nblk], f_v.at[6:10])
     return loads
 
 
@@ -260,79 +264,83 @@
     )
 
 
-def boundary_sum(acc, ys, t, here):
+def boundary_sum(acc, ys, t, here, more=()):
     nblk = t.shape[0]
     ends = ((0,), (0,))
-    low = dot(ys[0 : 2 * BK, here], t[0:2].reshape(2 * BK, -1), ends)
-    high = dot(ys[2 * BK : 4 * BK, here], t[nblk - 2 : nblk].reshape(2 * BK, -1), ends)
-    return acc[here, :] + (low + high)
+    total = acc[here, :]
+    for at, rows in ((0, (0, 1)), (2, (nblk - 2, nblk - 1)), (4, more)):
+        if rows:
+            size = len(rows) * BK
+            block = t[rows[0] : rows[-1] + 1].reshape(size, -1)
+            total = total + dot(ys[at * BK : at * BK + size, here], block, ends)
+    return total
 
 
 def boundary_kernel(
-    nblk, place, off, acc, f, intra, inter, t, m, d,
-    send, keep, tz_intra, tz_inter, d_rest, f_v, ys, sems, d_sems,
+    nblk, place, off, acc, c, intra, inter, t, m, d,
+    send_0, send_1, send_2, send_3, keep, d_rest, f_v, ys, sems, d_sems,
 ):
     core = core_of(place)
-    w = intra.shape[2]
-    near = boundary_start(nblk, core, f, slice(0, w), intra, inter, f_v, sems)
+    w = c.shape[2]
+    near = boundary_start(nblk, core, c, intra.at[:, :, 0:w], inter, f_v, sems)
     loads = Loads(d_sems)
-    _, rest = lead_of(nblk)
-    last = nblk - 2
-    loads.start(f.at[pl.ds(core * last, 2), :, w:], tz_inter)
-    loads.start(f.at[pl.ds((1 - core) * last, 2), :, w:], tz_intra)
-    loads.start(d.at[rest[0][0] : rest[-1][-1] + 1], d_rest)
-    half = send.shape[0]
+    _, rest, _ = lead_of(nblk)
+    loads.start(d.at[rest[0][0] : nblk - 2], d_rest)
+    half = keep.shape[0]
     boundary_rows(nblk, near, off, m, f_v, ys)
     here = pl.ds(pl.multiple_of(core * half, half), half)
     there = pl.ds(pl.multiple_of((1 - core) * half, half), half)
-    send[...] = boundary_sum(acc, ys, t, there).astype(BF16)
+    away = boundary_sum(acc, ys, t, there).astype(BF16)
+    for q, send in enumerate((send_0, send_1, send_2, send_3)):
+        send[...] = away[q * half // 4 : (q + 1) * half // 4, :]
     keep[...] = boundary_sum(acc, ys, t, here)
     loads.wait_all()
 
 
-def project_boundary(place, off, acc, f, intra, inter, t, m, d):
+def project_boundary(place, off, acc, c, intra, inter, t, m, d):
     nblk, _, nt = t.shape
     w = acc.shape[0]
-    zc = f.shape[2] - w
-    others = sum(map(len, lead_of(nblk)[1]))
+    others = nblk - 2 - lead_of(nblk)[1][0][0]
     return pl.pallas_call(
         functools.partial(boundary_kernel, nblk),
         out_shape=(
-            jax.ShapeDtypeStruct((w // 2, nt), BF16),
+            *[jax.ShapeDtypeStruct((w // 8, nt), BF16)] * 4,
             jax.ShapeDtypeStruct((w // 2, nt), F32),
-            jax.ShapeDtypeStruct((2, BK, zc), BF16),
-            jax.ShapeDtypeStruct((2, BK, zc), BF16),
             pltpu.VMEM((others, KB, BK, BK), BF16),
             pltpu.VMEM((12, BK, w), BF16),
         ),
         in_specs=[SMEM, SMEM] + [VMEM] * 6 + [ANY],
-        out_specs=(VMEM,) * 6,
+        out_specs=(VMEM,) * 7,
         scratch_shapes=[
             pltpu.VMEM((4 * BK, w), BF16),
             pltpu.SemaphoreType.DMA((4,)),
-            pltpu.SemaphoreType.DMA((3,)),
+            pltpu.SemaphoreType.DMA((1,)),
         ],
         compiler_params=params(10),
-        cost_estimate=cost(4 * BK * w * (KB * BK + nt), 8 * 2**20),
-    )(place, off, held(acc), held(f), intra, inter, held(t), held(m), stay(d))
-
-
-def merge_kernel(after, a, b, out, *_):
-    out[...] = (a[...].astype(F32) + b[...].astype(F32)).astype(BF16)
-
-
-def merge(after, a, b, hold=False):
-    shapes = [jax.ShapeDtypeStruct(b.shape, BF16)]
+        cost_estimate=cost(BK, BK),
+    )(place, off, held(acc), held(c), intra, inter, held(t), held(m), stay(d))
+
+
+def merge_kernel(count, skip, after, a, *refs):
+    got, out = refs[:count], refs[count + skip]
+    rows = a.shape[0] // count
+    for q in range(count):
+        here = slice(q * rows, (q + 1) * rows)
+        out[here, :] = (a[here, :].astype(F32) + got[q][...].astype(F32)).astype(BF16)
+
+
+def merge(after, a, got, hold=False, also=()):
+    shapes = [jax.ShapeDtypeStruct(a.shape, BF16)]
     if hold:
         shapes.append(jax.ShapeDtypeStruct(after.shape, after.dtype))
     out = pl.pallas_call(
-        merge_kernel,
+        functools.partial(merge_kernel, len(got), len(also)),
         out_shape=shapes,
-        in_specs=[ANY, VMEM, VMEM],
+        in_specs=[ANY, VMEM] + [VMEM] * len(got) + [ANY] * len(also),
         out_specs=[VMEM, ANY][: len(shapes)],
         input_output_aliases={0: 1} if hold else {},
         compiler_params=params(8),
-    )(after, a, b)
+    )(after, a, *got, *also)
     return out if hold else out[0]
 
 
@@ -345,7 +353,11 @@
     return (c.astype(F32) - dot(t, p, ((1,), (1,)))).astype(BF16)
 
 
-def orth_kernel(own, part, place, p, after, x_in, sq_in, f, t, x_out, sq, x_v, out_sems):
+def orth_rows32(c, t, p):
+    return c.astype(F32) - dot(t, p, ((1,), (1,)))
+
+
+def orth_kernel(own, part, place, p, after, x_in, sq_in, c, t, x_out, sq, x_v, out_sems):
     nblk, _, nt = t.shape
     half = p.shape[0]
     core = core_of(place)
@@ -353,19 +365,19 @@
     here = pl.ds(pl.multiple_of(side * half, half), half)
     stores = Loads(out_sems)
     total = None
-    for at in range(part[0], part[1], 2):
-        block = f[at : at + 2, :, here].reshape(2 * BK, half)
-        x = orth_rows(block, t[at : at + 2].reshape(2 * BK, nt), p[...])
-        x_v[at : at + 2] = x.reshape(2, BK, half)
+    for at in range(part[0], part[1], 1):
+        block = c[at : at + 1, :, here].reshape(1 * BK, half)
+        x = orth_rows32(block, t[at : at + 1].reshape(1 * BK, nt), p[...])
+        x_v[at : at + 1] = x.astype(BF16).reshape(1, BK, half)
         squares = square_sum(x)
         total = squares if total is None else total + squares
-        stores.start(x_v.at[at : at + 2], x_out.at[at : at + 2, :, here])
+        stores.start(x_v.at[at : at + 1], x_out.at[at : at + 1, :, here])
     sq[...] = sq_in[...]
     sq[:, here] += total
     stores.wait_all()
 
 
-def orthogonalize(own, part, place, p, after, x, sq, f, t):
+def orthogonalize(own, part, place, p, after, x, sq, c, t):
     nblk, _, nt = t.shape
     half = p.shape[0]
     w = 2 * half
@@ -377,11 +389,11 @@
         input_output_aliases={} if x is None else {3: 0},
         scratch_shapes=[
             pltpu.VMEM((nblk, BK, half), BF16),
-            pltpu.SemaphoreType.DMA((nblk // 2,)),
+            pltpu.SemaphoreType.DMA((nblk,)),
         ],
         compiler_params=params(7),
         cost_estimate=cost(nblk * BK * half * nt, 8 * 2**20),
-    )(place, p, after, after if x is None else x, sq, held(f), held(t))
+    )(place, p, after, after if x is None else x, sq, held(c), held(t))
 
 
 def chip_order(bits, side):
@@ -389,20 +401,24 @@
 
 
 def dipole_boundary_kernel(
-    nblk, place, off, after, acc, f, near, tz_intra, tz_inter, t, d, send_0, send_1, keep, f_v, ys, sems
+    nblk, place, off, after, acc, f, near, intra, tz_inter, t, d, d_rest,
+    send_0, send_1, keep, f_v, ys, sems,
 ):
     groups, cols, lanes = keep.shape
     w = near.shape[2]
     bits = groups.bit_length() - 1
     loads = boundary_start(
-        nblk, core_of(place), f, slice(w, cols), tz_intra, tz_inter, f_v, sems
+        nblk, core_of(place), f.at[:, :, w:cols], intra.at[:, :, w:cols], tz_inter, f_v, sems
     )
+    _, rest, last = lead_of(nblk)
+    slot = last[0] - rest[0][0]
+    band_rows(last, range(slot, slot + len(last)), off, f, cols, d_rest, 0, ys.at[4 * BK :])
     boundary_rows(nblk, None, off, d, near, ys)
     boundary_rows(nblk, loads, off, d, f_v, ys, w)
     orders = [chip_order(bits, side) for side in (0, 1)]
     for at in range(0, cols, BK):
         here = slice(at, min(at + BK, cols))
-        whole = boundary_sum(acc, ys, t, here)
+        whole = boundary_sum(acc, ys, t, here, last)
         for g in range(groups):
             owned = []
             for side in (0, 1):
@@ -417,7 +433,7 @@
             send[g % (groups // 2), here, :] = away.astype(BF16)
 
 
-def dipole_boundary(place, off, after, acc, f, near, tz, t, d, groups):
+def dipole_boundary(place, off, after, acc, f, near, intra, tz_inter, t, d, d_rest, groups):
     nblk, _, nt = t.shape
     cols = acc.shape[0]
     lanes = nt // (2 * groups)
@@ -428,20 +444,20 @@
             jax.ShapeDtypeStruct((groups // 2, cols, lanes), BF16),
             jax.ShapeDtypeStruct((groups, cols, lanes), F32),
         ),
-        in_specs=[SMEM, SMEM, ANY] + [VMEM] * 7,
+        in_specs=[SMEM, SMEM, ANY] + [VMEM] * 8,
         out_specs=(VMEM,) * 3,
         scratch_shapes=[
-            pltpu.VMEM((12, BK, tz[0].shape[2]), BF16),
-            pltpu.VMEM((4 * BK, cols), BF16),
+            pltpu.VMEM((12, BK, tz_inter.shape[2]), BF16),
+            pltpu.VMEM(((4 + LAST) * BK, cols), BF16),
             pltpu.SemaphoreType.DMA((4,)),
         ],
-        compiler_params=params(9),
+        compiler_params=params(11),
         cost_estimate=cost(4 * BK * cols * (KB * BK + nt), 8 * 2**20),
-    )(place, off, after, held(acc), held(f), held(near), *tz, held(t), held(d))
+    )(place, off, after, held(acc), held(f), held(near), intra, tz_inter, held(t), held(d), held(d_rest))
 
 
 def halve_kernel(step, place, after, keep, *refs):
-    got, (send, kept) = refs[:-2], refs[-2:]
+    got, (send, kept, _) = refs[:-3], refs[-3:]
     half = kept.shape[0]
     orders = [chip_order(step[1], side)[step[0]] for side in (0, 1)]
     which = jnp.where(core_of(place) == 0, orders[0], orders[1])
@@ -465,9 +481,11 @@
         out_shape=(
             jax.ShapeDtypeStruct((half, cols, lanes), BF16),
             jax.ShapeDtypeStruct((half, cols, lanes), F32),
+            jax.ShapeDtypeStruct(after.shape, after.dtype),
         ),
         in_specs=[SMEM, ANY, VMEM] + [VMEM] * len(got),
-        out_specs=(VMEM,) * 2,
+        out_specs=(VMEM, VMEM, ANY),
+        input_output_aliases={1: 2},
         compiler_params=params(8),
     )(place, after, keep, *got)
 
@@ -575,49 +593,48 @@
     orders = [chip_order(bits, side) for side in (0, 1)]
     masks = [(2 << orders[0][s], 2 << orders[1][s]) for s in range(bits)]
 
-    halos = exchange(*edges(place_s, c), count)
+    intra, inter, tz_inter = edges(place_s, z_s, c, t, zc)
+    intra, inter = exchange(intra, inter, count)
+    tz_inter = meet(tz_inter, count)
     p_acc, r_acc, f, t_v, m_edge = first(z_s, off, c, t, margin_blocks, dipole_blocks, zc)
-    send, keep, *tz, d_rest, near = project_boundary(
-        place_s, off, p_acc, f, *halos, t_v, m_edge, dipole_blocks
+    *sends, keep, d_rest, near = project_boundary(
+        place_s, off, p_acc, c, intra, inter, t_v, m_edge, dipole_blocks
     )
-    tz = exchange(*tz, count)
-    part, r_acc = merge(r_acc, keep, swap(send, count, both), hold=True)
+    got = [swap(send, count, both) for send in sends]
+    part, r_acc = merge(r_acc, keep, got, hold=True, also=(tz_inter,))
 
     for s in range(bits):
-        got = swap(part, count, masks[s])
+        got = [swap(part, count, masks[s])]
         if s == 0:
             r_acc, d_edge = middle(off, part, r_acc, f, t_v, dipole_blocks, d_rest)
             part, r_acc = merge(r_acc, part, got, hold=True)
             continue
         if s == 1:
             *sends, keep = dipole_boundary(
-                place_s, off, part, r_acc, f, near, tz, t_v, d_edge, chips
+                place_s, off, part, r_acc, f, near, intra, tz_inter, t_v, d_edge, d_rest, chips
             )
             got_r = [swap(send, count, both) for send in sends]
             send = sends[0]
         else:
-            send, keep = halve((s - 2, bits), place_s, part, keep, got_r)
+            send, keep, part = halve((s - 2, bits), place_s, part, keep, got_r)
             got_r = [swap(send, count, masks[s - 2])]
         part = merge(send, part, got)
+    send, keep, part = halve((bits - 2, bits), place_s, part, keep, got_r)
+    got_r = [swap(send, count, masks[bits - 2])]
     other = swap(part, count, both)
-    send, keep = halve((bits - 2, bits), place_s, part, keep, got_r)
-    got_r = [swap(send, count, masks[bits - 2])]
-
-    half = nblk // 4 * 2
-    x, sq = orthogonalize(True, (0, nblk), place_s, part, part, None, zero, f, t_v)
-    x, sq = orthogonalize(False, (0, half), place_s, other, part, x, sq, f, t_v)
-    send, keep = halve((bits - 1, bits), place_s, sq, keep, got_r)
+
+    x, sq = orthogonalize(True, (0, nblk), place_s, part, part, None, zero, c, t_v)
+    x, sq = orthogonalize(False, (0, nblk), place_s, other, part, x, sq, c, t_v)
+    send, keep, sq = halve((bits - 1, bits), place_s, sq, keep, got_r)
     got_r = [swap(send, count, masks[bits - 1])]
-    x, sq = orthogonalize(False, (half, nblk), place_s, other, send, x, sq, f, t_v)
     tail = [both] + masks
+    sq = sq + swap(sq, count, tail.pop(0))
     sq = sq + swap(sq, count, tail.pop(0))
     pieces = [settle(w, sq, keep, got_r[0])]
     spots, step = [0], planes // 2
     while step:
         whole = pieces[0]
         if len(pieces) > 1:
-            if tail:
-                sq = sq + swap(sq, count, tail.pop(0))
             whole = stack(sq, pieces)
         pieces.append(lax.ppermute(whole, "orb", [(i, i ^ step) for i in range(planes)]))
         spots += [spot ^ step for spot in spots]

time: 76.9 us -> 74.3 us (0.966)
  waiting for transfers between devices: 18.2 us -> 11.7 us
  starting transfers between devices: 15.1 us -> 20.9 us
  Pallas kernels: 42.6 us -> 40.8 us
    ppermute x13 -> x15, waiting for transfers between devices: 18.2 us -> 8.97 us  [swap(): lax.ppermute(block, 'basis', [(i, i ^ mask[i % 2]) for i in range(count)])]
    ppermute x13 -> x15, starting transfers between devices: 9.24 us -> 15.4 us  [swap(): lax.ppermute(block, 'basis', [(i, i ^ mask[i % 2]) for i in range(count)])]
    ppermute x2, waiting for transfers between devices: 0.01 us -> 2.7 us  [on_device(): lax.ppermute(whole, 'orb', [(i, i ^ step) for i in range(planes)])]
    pallas_call x1, Pallas kernels: 4.85 us -> 6.59 us  [dipole_boundary(): pl.pallas_call(functools.partial(dipole_boundary_kernel, nblk), out_shape...]
    pallas_call x1, Pallas kernels: 13 us -> 11.5 us  [first(): pl.pallas_call(functools.partial(first_kernel, nblk), out_shape=(pltpu.VM...]
    pallas_call x3 -> x2, Pallas kernels: 8.54 us -> 7.18 us  [orthogonalize(): pl.pallas_call(functools.partial(orth_kernel, own, part), out_shape=(pltp...]
    pallas_call x1, Pallas kernels: 9.42 us -> 8.33 us  [middle(): pl.pallas_call(functools.partial(middle_kernel, groups), out_shape=(pltpu...]
  transfers between devices with their start and end apart: 17 -> 19, of which waited for: 8 -> 10; matrix products, arithmetic and copies ran while one was open for 0% -> 0% of each run, Pallas kernels for 48% -> 50%
where the time goes in v4:
time: 74.3 us; the launch traced here: 74.2 us
  Pallas kernels  40.8 us (55%)
  starting transfers between devices  20.9 us (28%)
  waiting for transfers between devices  11.7 us (16%)
  between operations  0.84 us (1%)
    ppermute x15, starting transfers between devices, swap(): lax.ppermute(block, 'basis', [(i, i ^ mask[i % 2]) for i in range(count)])  15.4 us
    pallas_call x1, Pallas kernels, first(): pl.pallas_call(functools.partial(first_kernel, nblk), out_shape=(pltpu.VM...  11.5 us
    ppermute x15, waiting for transfers between devices, swap(): lax.ppermute(block, 'basis', [(i, i ^ mask[i % 2]) for i in range(count)])  8.97 us
    pallas_call x1, Pallas kernels, middle(): pl.pallas_call(functools.partial(middle_kernel, groups), out_shape=(pltpu...  8.33 us
    pallas_call x2, Pallas kernels, orthogonalize(): pl.pallas_call(functools.partial(orth_kernel, own, part), out_shape=(pltp...  7.18 us
    pallas_call x1, Pallas kernels, dipole_boundary(): pl.pallas_call(functools.partial(dipole_boundary_kernel, nblk), out_shape...  6.59 us
    ppermute x2, starting transfers between devices, on_device(): lax.ppermute(whole, 'orb', [(i, i ^ step) for i in range(planes)])  4.15 us
    pallas_call x1, Pallas kernels, project_boundary(): pl.pallas_call(functools.partial(boundary_kernel, nblk), out_shape=(*[jax...  3.65 us
  transfers between devices with their start and end apart: 19, of which 10 were waited for; matrix products, arithmetic and copies ran while one was open for 0% of the time, Pallas kernels for 50%

profile of v4, /device:TPU:0, one launch (start us, length us, event | category | flops | bytes accessed | tf_op | source)
XLA Modules:
  0.0 74.2 jit_solution(17663732672863485678)
XLA Ops:
  0.7 1.5 %shard_map.69 = (bf16[2,256,768]{2,1,0:T(8,128)(2,1)S(1)}, bf16[2,256,512]{2,1,0:T(8,128)(2,1)S(1)}, bf16[2,256,256]{2,1,0:T(8,128)(2,1)S(1)}) custom-call(s32[1]{0:T(128)} %bitcast.place, s32[1]{0:T(128)} %bitcast.2.z, bf16[16,256,512]{2,1,0:T(8,128)(2,1)} %bitcast.6, bf16[16,256,1024]{2,1,0:T(8,128)(2,1)} %bitcast.15), custom_call_target="tpu_custom_call" | custom-call | tf_op jit(solution)/shard_map/pallas_call | solution.py:114
  2.2 0.5 collective-permute-start
  2.7 0.7 collective-permute-start.1
  3.4 0.7 collective-permute-start.6
  4.1 11.5 %shard_map.68 = (f32[512,1024]{1,0:T(8,128)S(1)}, f32[768,1024]{1,0:T(8,128)S(1)}, bf16[16,256,768]{2,1,0:T(8,128)(2,1)S(1)}, bf16[16,256,1024]{2,1,0:T(8,128)(2,1)S(1)}, bf16[4,4,256,256]{3,2,1,0:T(8,128)(2,1)S(1)}) custom-call(s32[1]{0:T(128)} %bitcast.2.z, s32[4,16]{1,0:T(4,128)S(1)} %bitcast.11, bf16[16,256,512]{2,1,0:T(8,128)(2,1)S(1)} %bitcast.7, ...), custom_call_target="tpu_custom_call" | custom-call | flops 7247757312 | bytes 31457280 | tf_op jit(solution)/shard_map/pallas_call | solution.py:191
  15.6 3.6 %shard_map.70 = (bf16[64,1024]{1,0:T(8,128)(2,1)S(1)}, bf16[64,1024]{1,0:T(8,128)(2,1)S(1)}, bf16[64,1024]{1,0:T(8,128)(2,1)S(1)}, bf16[64,1024]{1,0:T(8,128)(2,...) custom-call(s32[1]{0:T(128)} %bitcast.place, ...), custom_call_target="tpu_custom_call" | custom-call | flops 512 | bytes 256 | tf_op jit(solution)/shard_map/pallas_call | solution.py:304
  19.3 5.3 %collective-permute-start.2 = (bf16[64,1024]{1,0:T(8,128)(2,1)S(1)}, bf16[64,1024]{1,0:T(8,128)(2,1)S(1)}, u32[]{:S(2)}, u32[]{:S(2)}) collective-permute-start(bf16[64,1024]{1,0:T(8,128)(2,1)S(1)} %get-tuple-element.43), channel_id=1, source_target_pairs={{0,4},{4,0},{8,12},{12,8},{16,20},{20,16},{24,28},{28,24},{1,5},{5... | collective-permute-start | bytes 393224 | tf_op jit(solution)/shard_map/ppermute | solution.py:559
  24.7 0.4 collective-permute-start.4
  25.2 0.4 collective-permute-done.2.refs_0_
  25.6 0.4 collective-permute-done.3.refs_1_
  26.1 0.3 collective-permute-done.5.refs_3_
  26.5 2.9 %collective-permute-start.7 = (bf16[256,1024]{1,0:T(8,128)(2,1)S(1)}, bf16[256,1024]{1,0:T(8,128)(2,1)S(1)}, u32[]{:S(2)}, u32[]{:S(2)}) collective-permute-start(bf16[256,1024]{1,0:T(8,128)(2,1)S(1)} %get-tuple-element.48.after.a), channel_id=1, source_target_pairs={{0,8},{4,20},{8,0},{12,28},{16,24},{20,4},{24,16},{28,12},{1,9},{5... | collective-permute-start | bytes 1572872 | tf_op jit(solution)/shard_map/ppermute | solution.py:559
  29.5 8.3 %shard_map.72 = (f32[768,1024]{1,0:T(8,128)S(1)}, bf16[4,4,256,256]{3,2,1,0:T(8,128)(2,1)S(1)}) custom-call(s32[4,16]{1,0:T(4,128)S(1)} %bitcast.13, bf16[256,1024]{1,0:T(8,128)(2,1)S(1)} %get-tuple-element.48.after.a, f32[768,1024]{1,0:T(8,128)S(1)} %get-tuple-element.49.acc, bf16[16,256,768]{2,1,0:T(8,128)(2,1)S(1)} %get-tuple-element.50.f, ...), custom_call_target="tpu_custom_call" | custom-call | flops 7247757312 | bytes 14680064 | tf_op jit(solution)/shard_map/pallas_call | solution.py:231
  37.9 0.8 %collective-permute-start.8 = (bf16[256,1024]{1,0:T(8,128)(2,1)S(1)}, bf16[256,1024]{1,0:T(8,128)(2,1)S(1)}, u32[]{:S(2)}, u32[]{:S(2)}) collective-permute-start(bf16[256,1024]{1,0:T(8,128)(2,1)S(1)} %get-tuple-element.53.after.a), channel_id=1, source_target_pairs={{0,16},{4,12},{8,24},{12,4},{16,0},{20,28},{24,8},{28,20},{1,17},{... | collective-permute-start | bytes 1572872 | tf_op jit(solution)/shard_map/ppermute | solution.py:559
  38.7 6.6 %shard_map.74 = (bf16[2,768,128]{2,1,0:T(8,128)(2,1)S(1)}, bf16[2,768,128]{2,1,0:T(8,128)(2,1)S(1)}, f32[4,768,128]{2,1,0:T(8,128)S(1)}) custom-call(s32[1]{0:T(128)} %bitcast.place, s32[4,16]{1,0:T(4,128)S(1)} %bitcast.14, bf16[256,1024]{1,0:T(8,128)(2,1)S(1)} %get-tuple-element.53.after.a, f32[768,1024]{1,0:T(8,128)S(1)} %get-tuple-element.54.acc, ...), custom_call_target="tpu_custom_call" | custom-call | flops 3221225472 | bytes 8388608 | tf_op jit(solution)/shard_map/pallas_call | solution.py:440
  45.4 0.5 collective-permute-start.9
  45.9 1.3 %collective-permute-done.8.refs_0_ = bf16[256,1024]{1,0:T(8,128)(2,1)S(1)} collective-permute-done((bf16[256,1024]{1,0:T(8,128)(2,1)S(1)}, bf16[256,1024]{1,0:T(8,128)(2,1)S(1)}, u32[]{:S(2)}, u32[]{:S(2)}) %collective-permute-start.8) | collective-permute-done | bytes 524320 | tf_op jit(solution)/shard_map/ppermute | solution.py:559
  47.3 0.3 collective-permute-done.9.refs_0_
  47.7 0.3 shard_map.76
  48.2 1.2 %collective-permute-start.12 = (bf16[2,768,128]{2,1,0:T(8,128)(2,1)S(1)}, bf16[2,768,128]{2,1,0:T(8,128)(2,1)S(1)}, u32[]{:S(2)}, u32[]{:S(2)}) collective-permute-start(bf16[2,768,128]{2,1,0:T(8,128)(2,1)S(1)} %get-tuple-element.66), channel_id=1, source_target_pairs={{0,8},{4,20},{8,0},{12,28},{16,24},{20,4},{24,16},{28,12},{1,9},{5... | collective-permute-start | bytes 1179656 | tf_op jit(solution)/shard_map/ppermute | solution.py:559
  49.4 3.6 %shard_map.77 = (bf16[16,256,512]{2,1,0:T(8,128)(2,1)}, f32[1,512]{1,0:T(1,128)S(1)}) custom-call(s32[1]{0:T(128)} %bitcast.place, bf16[256,1024]{1,0:T(8,128)(2,1)S(1)} %get-tuple-element.60.p.after.x_in.mine, bf16[256,1024]{1,0:T(8,128)(2,1)S(1)} %get-tuple-element.60.p.after.x_in.mine, bf16[256,1024]{1,0:T(8,128)(2,1)S(1)} %get-tuple-element.60.p.after.x_in.mine, ...), custom_call_target="tpu_custom_call" | custom-call | flops 2147483648 | bytes 8388608 | tf_op jit(solution)/shard_map/pallas_call | solution.py:384
  53.0 3.6 %shard_map.78 = (bf16[16,256,512]{2,1,0:T(8,128)(2,1)}, f32[1,512]{1,0:T(1,128)S(1)}) custom-call(s32[1]{0:T(128)} %bitcast.place, bf16[256,1024]{1,0:T(8,128)(2,1)S(1)} %collective-permute-done.11.p.other, bf16[256,1024]{1,0:T(8,128)(2,1)S(1)} %get-tuple-element.60.p.after.x_in.mine, ...), custom_call_target="tpu_custom_call", output_to_operand_aliasing={{0}: (3, {})} | custom-call | flops 2147483648 | bytes 8388608 | tf_op jit(solution)/shard_map/pallas_call | solution.py:384
  56.7 1.0 %collective-permute-start.13 = (bf16[1,768,128]{2,1,0:T(8,128)(2,1)S(1)}, bf16[1,768,128]{2,1,0:T(8,128)(2,1)S(1)}, u32[]{:S(2)}, u32[]{:S(2)}) collective-permute-start(bf16[1,768,128]{2,1,0:T(8,128)(2,1)S(1)} %get-tuple-element.68), channel_id=1, source_target_pairs={{0,16},{4,12},{8,24},{12,4},{16,0},{20,28},{24,8},{28,20},{1,17},{... | collective-permute-start | bytes 589832 | tf_op jit(solution)/shard_map/ppermute | solution.py:559
  57.7 1.2 %collective-permute-done.14 = f32[1,512]{1,0:T(1,128)S(1)} collective-permute-done((f32[1,512]{1,0:T(1,128)S(1)}, f32[1,512]{1,0:T(1,128)S(1)}, u32[]{:S(2)}, u32[]{:S(2)}) %collective-permute-start.14) | collective-permute-done | bytes 2080 | tf_op jit(solution)/shard_map/ppermute | solution.py:559
  58.9 1.2 %collective-permute-start.15 = (f32[1,512]{1,0:T(1,128)S(1)}, f32[1,512]{1,0:T(1,128)S(1)}, u32[]{:S(2)}, u32[]{:S(2)}) collective-permute-start(f32[1,512]{1,0:T(1,128)S(1)} %add.9), channel_id=1, source_target_pairs={{0,8},{4,20},{8,0},{12,28},{16,24},{20,4},{24,16},{28,12},{1,9},{5... | collective-permute-start | bytes 6152 | tf_op jit(solution)/shard_map/ppermute | solution.py:559
  60.1 2.4 %collective-permute-done.15 = f32[1,512]{1,0:T(1,128)S(1)} collective-permute-done((f32[1,512]{1,0:T(1,128)S(1)}, f32[1,512]{1,0:T(1,128)S(1)}, u32[]{:S(2)}, u32[]{:S(2)}) %collective-permute-start.15) | collective-permute-done | bytes 2080 | tf_op jit(solution)/shard_map/ppermute | solution.py:559
  62.5 2.6 %collective-permute-start.17 = (bf16[256,128]{1,0:T(8,128)(2,1)S(1)}, bf16[256,128]{1,0:T(8,128)(2,1)S(1)}, u32[]{:S(2)}, u32[]{:S(2)}) collective-permute-start(bf16[256,128]{1,0:T(8,128)(2,1)S(1)} %shard_map.80.refs_0_), channel_id=1, source_target_pairs={{0,2},{1,3},{2,0},{3,1},{4,6},{5,7},{6,4},{7,5},{8,10},{9,11},{10,... | collective-permute-start | bytes 196616 | tf_op jit(solution)/shard_map/ppermute | solution.py:639
  65.1 2.7 %collective-permute-done.17.refs_1_ = bf16[256,128]{1,0:T(8,128)(2,1)S(1)} collective-permute-done((bf16[256,128]{1,0:T(8,128)(2,1)S(1)}, bf16[256,128]{1,0:T(8,128)(2,1)S(1)}, u32[]{:S(2)}, u32[]{:S(2)}) %collective-permute-start.17) | collective-permute-done | bytes 65568 | tf_op jit(solution)/shard_map/ppermute | solution.py:639
  67.8 1.5 %collective-permute-start.18 = (bf16[512,128]{1,0:T(8,128)(2,1)S(1)}, bf16[512,128]{1,0:T(8,128)(2,1)S(1)}, u32[]{:S(2)}, u32[]{:S(2)}) collective-permute-start(bf16[512,128]{1,0:T(8,128)(2,1)S(1)} %shard_map.81), channel_id=1, source_target_pairs={{0,1},{1,0},{2,3},{3,2},{4,5},{5,4},{6,7},{7,6},{8,9},{9,8},{10,11... | collective-permute-start | bytes 393224 | tf_op jit(solution)/shard_map/ppermute | solution.py:639
  69.4 1.1 %collective-permute-start.16 = (f32[1,512]{1,0:T(1,128)S(1)}, f32[1,512]{1,0:T(1,128)S(1)}, u32[]{:S(2)}, u32[]{:S(2)}) collective-permute-start(f32[1,512]{1,0:T(1,128)S(1)} %add.10.after), channel_id=1, source_target_pairs={{0,16},{4,12},{8,24},{12,4},{16,0},{20,28},{24,8},{28,20},{1,17},{... | collective-permute-start | bytes 6152 | tf_op jit(solution)/shard_map/ppermute | solution.py:559
  70.5 2.5 %collective-permute-done.16 = f32[1,512]{1,0:T(1,128)S(1)} collective-permute-done((f32[1,512]{1,0:T(1,128)S(1)}, f32[1,512]{1,0:T(1,128)S(1)}, u32[]{:S(2)}, u32[]{:S(2)}) %collective-permute-start.16) | collective-permute-done | bytes 2080 | tf_op jit(solution)/shard_map/ppermute | solution.py:559
  73.0 1.2 %shard_map.82 = bf16[128,512]{1,0:T(8,128)(2,1)} custom-call(s32[1]{0:T(128)} %bitcast.place, s32[1]{0:T(128)} %bitcast.2.z, f32[1,768,128]{2,1,0:T(8,128)S(1)} %get-tuple-element.67.keep, bf16[1,768,128]{2,1,0:T(8,128)(2,1)S(1)} %collective-permute-done.13.got, bf16[256,1024]{1,0:T(8,128)(2,1)S(1)} %get-tuple-element.60.p.after.x_in.mine, ...), custom_call_target="tpu_custom_call" | custom-call | tf_op jit(solution)/shard_map/pallas_call | solution.py:548
  (29 shorter events, 1.1 us)
Async XLA Ops:
  0.6 3.5 %copy-start = (bf16[4096,512]{1,0:T(8,128)(2,1)S(1)}, bf16[4096,512]{1,0:T(8,128)(2,1)}, u32[]{:S(2)}) copy-start(bf16[4096,512]{1,0:T(8,128)(2,1)} %param.5) | copy-start | bytes 12582916
  0.6 3.5 %copy-start.1 = (s32[16,4]{0,1:T(4,128)S(1)}, s32[16,4]{0,1:T(4,128)}, u32[]{:S(2)}) copy-start(s32[16,4]{0,1:T(4,128)} %param.9) | copy-start | bytes 772
  2.2 13.4 %collective-permute-start = (bf16[2,256,768]{2,1,0:T(8,128)(2,1)S(1)}, bf16[2,256,768]{2,1,0:T(8,128)(2,1)S(1)}, u32[]{:S(2)}, u32[]{:S(2)}) collective-permute-start(bf16[2,256,768]{2,1,0:T(8,128)(2,1)S(1)} %get-tuple-element.38), channel_id=1, source_target_pairs={{0,4},{4,0},{8,12},{12,8},{16,20},{20,16},{24,28},{28,24},{1,5},{5... | collective-permute-start | bytes 2359304 | tf_op jit(solution)/shard_map/ppermute | solution.py:559
  2.7 12.9 %collective-permute-start.1 = (bf16[2,256,512]{2,1,0:T(8,128)(2,1)S(1)}, bf16[2,256,512]{2,1,0:T(8,128)(2,1)S(1)}, u32[]{:S(2)}, u32[]{:S(2)}) collective-permute-start(bf16[2,256,512]{2,1,0:T(8,128)(2,1)S(1)} %get-tuple-element.39), channel_id=1, source_target_pairs={{4,8},{12,16},{20,24},{8,4},{16,12},{24,20},{5,9},{13,17},{21,25},... | collective-permute-start | bytes 1572872 | tf_op jit(solution)/shard_map/ppermute | solution.py:564
  3.4 21.8 %collective-permute-start.6 = (bf16[2,256,256]{2,1,0:T(8,128)(2,1)S(1)}, bf16[2,256,256]{2,1,0:T(8,128)(2,1)S(1)}, u32[]{:S(2)}, u32[]{:S(2)}) collective-permute-start(bf16[2,256,256]{2,1,0:T(8,128)(2,1)S(1)} %get-tuple-element.47), channel_id=1, source_target_pairs={{4,8},{12,16},{20,24},{8,4},{16,12},{24,20},{5,9},{13,17},{21,25},... | collective-permute-start | bytes 786440 | tf_op jit(solution)/shard_map/ppermute | solution.py:564
  19.3 6.3 %collective-permute-start.2 = (bf16[64,1024]{1,0:T(8,128)(2,1)S(1)}, bf16[64,1024]{1,0:T(8,128)(2,1)S(1)}, u32[]{:S(2)}, u32[]{:S(2)}) collective-permute-start(bf16[64,1024]{1,0:T(8,128)(2,1)S(1)} %get-tuple-element.43), channel_id=1, source_target_pairs={{0,4},{4,0},{8,12},{12,8},{16,20},{20,16},{24,28},{28,24},{1,5},{5... | collective-permute-start | bytes 393224 | tf_op jit(solution)/shard_map/ppermute | solution.py:559
  24.6 1.3 %collective-permute-start.3 = (bf16[64,1024]{1,0:T(8,128)(2,1)S(1)}, bf16[64,1024]{1,0:T(8,128)(2,1)S(1)}, u32[]{:S(2)}, u32[]{:S(2)}) collective-permute-start(bf16[64,1024]{1,0:T(8,128)(2,1)S(1)} %get-tuple-element.44), channel_id=1, source_target_pairs={{0,4},{4,0},{8,12},{12,8},{16,20},{20,16},{24,28},{28,24},{1,5},{5... | collective-permute-start | bytes 393224 | tf_op jit(solution)/shard_map/ppermute | solution.py:559
  24.7 1.5 %collective-permute-start.4 = (bf16[64,1024]{1,0:T(8,128)(2,1)S(1)}, bf16[64,1024]{1,0:T(8,128)(2,1)S(1)}, u32[]{:S(2)}, u32[]{:S(2)}) collective-permute-start(bf16[64,1024]{1,0:T(8,128)(2,1)S(1)} %get-tuple-element.45), channel_id=1, source_target_pairs={{0,4},{4,0},{8,12},{12,8},{16,20},{20,16},{24,28},{28,24},{1,5},{5... | collective-permute-start | bytes 393224 | tf_op jit(solution)/shard_map/ppermute | solution.py:559
  25.1 1.3 %collective-permute-start.5 = (bf16[64,1024]{1,0:T(8,128)(2,1)S(1)}, bf16[64,1024]{1,0:T(8,128)(2,1)S(1)}, u32[]{:S(2)}, u32[]{:S(2)}) collective-permute-start(bf16[64,1024]{1,0:T(8,128)(2,1)S(1)} %get-tuple-element.46), channel_id=1, source_target_pairs={{0,4},{4,0},{8,12},{12,8},{16,20},{20,16},{24,28},{28,24},{1,5},{5... | collective-permute-start | bytes 393224 | tf_op jit(solution)/shard_map/ppermute | solution.py:559
  26.5 11.3 %collective-permute-start.7 = (bf16[256,1024]{1,0:T(8,128)(2,1)S(1)}, bf16[256,1024]{1,0:T(8,128)(2,1)S(1)}, u32[]{:S(2)}, u32[]{:S(2)}) collective-permute-start(bf16[256,1024]{1,0:T(8,128)(2,1)S(1)} %get-tuple-element.48.after.a), channel_id=1, source_target_pairs={{0,8},{4,20},{8,0},{12,28},{16,24},{20,4},{24,16},{28,12},{1,9},{5... | collective-permute-start | bytes 1572872 | tf_op jit(solution)/shard_map/ppermute | solution.py:559
  37.9 9.2 %collective-permute-start.8 = (bf16[256,1024]{1,0:T(8,128)(2,1)S(1)}, bf16[256,1024]{1,0:T(8,128)(2,1)S(1)}, u32[]{:S(2)}, u32[]{:S(2)}) collective-permute-start(bf16[256,1024]{1,0:T(8,128)(2,1)S(1)} %get-tuple-element.53.after.a), channel_id=1, source_target_pairs={{0,16},{4,12},{8,24},{12,4},{16,0},{20,28},{24,8},{28,20},{1,17},{... | collective-permute-start | bytes 1572872 | tf_op jit(solution)/shard_map/ppermute | solution.py:559
  45.3 2.0 %collective-permute-start.10 = (bf16[2,768,128]{2,1,0:T(8,128)(2,1)S(1)}, bf16[2,768,128]{2,1,0:T(8,128)(2,1)S(1)}, u32[]{:S(2)}, u32[]{:S(2)}) collective-permute-start(bf16[2,768,128]{2,1,0:T(8,128)(2,1)S(1)} %get-tuple-element.59), channel_id=1, source_target_pairs={{0,4},{4,0},{8,12},{12,8},{16,20},{20,16},{24,28},{28,24},{1,5},{5... | collective-permute-start | bytes 1179656 | tf_op jit(solution)/shard_map/ppermute | solution.py:559
  45.4 2.3 %collective-permute-start.9 = (bf16[2,768,128]{2,1,0:T(8,128)(2,1)S(1)}, bf16[2,768,128]{2,1,0:T(8,128)(2,1)S(1)}, u32[]{:S(2)}, u32[]{:S(2)}) collective-permute-start(bf16[2,768,128]{2,1,0:T(8,128)(2,1)S(1)} %get-tuple-element.57.after), channel_id=1, source_target_pairs={{0,4},{4,0},{8,12},{12,8},{16,20},{20,16},{24,28},{28,24},{1,5},{5... | collective-permute-start | bytes 1179656 | tf_op jit(solution)/shard_map/ppermute | solution.py:559
  48.0 5.0 %collective-permute-start.11 = (bf16[256,1024]{1,0:T(8,128)(2,1)S(1)}, bf16[256,1024]{1,0:T(8,128)(2,1)S(1)}, u32[]{:S(2)}, u32[]{:S(2)}) collective-permute-start(bf16[256,1024]{1,0:T(8,128)(2,1)S(1)} %get-tuple-element.60.p.after.x_in.mine), channel_id=1, source_target_pairs={{0,4},{4,0},{8,12},{12,8},{16,20},{20,16},{24,28},{28,24},{1,5},{5... | collective-permute-start | bytes 1572872 | tf_op jit(solution)/shard_map/ppermute | solution.py:559
  48.2 8.4 %collective-permute-start.12 = (bf16[2,768,128]{2,1,0:T(8,128)(2,1)S(1)}, bf16[2,768,128]{2,1,0:T(8,128)(2,1)S(1)}, u32[]{:S(2)}, u32[]{:S(2)}) collective-permute-start(bf16[2,768,128]{2,1,0:T(8,128)(2,1)S(1)} %get-tuple-element.66), channel_id=1, source_target_pairs={{0,8},{4,20},{8,0},{12,28},{16,24},{20,4},{24,16},{28,12},{1,9},{5... | collective-permute-start | bytes 1179656 | tf_op jit(solution)/shard_map/ppermute | solution.py:559
  56.7 5.8 %collective-permute-start.13 = (bf16[1,768,128]{2,1,0:T(8,128)(2,1)S(1)}, bf16[1,768,128]{2,1,0:T(8,128)(2,1)S(1)}, u32[]{:S(2)}, u32[]{:S(2)}) collective-permute-start(bf16[1,768,128]{2,1,0:T(8,128)(2,1)S(1)} %get-tuple-element.68), channel_id=1, source_target_pairs={{0,16},{4,12},{8,24},{12,4},{16,0},{20,28},{24,8},{28,20},{1,17},{... | collective-permute-start | bytes 589832 | tf_op jit(solution)/shard_map/ppermute | solution.py:559
  57.7 1.2 %collective-permute-start.14 = (f32[1,512]{1,0:T(1,128)S(1)}, f32[1,512]{1,0:T(1,128)S(1)}, u32[]{:S(2)}, u32[]{:S(2)}) collective-permute-start(f32[1,512]{1,0:T(1,128)S(1)} %get-tuple-element.69), channel_id=1, source_target_pairs={{0,4},{4,0},{8,12},{12,8},{16,20},{20,16},{24,28},{28,24},{1,5},{5... | collective-permute-start | bytes 6152 | tf_op jit(solution)/shard_map/ppermute | solution.py:559
  58.9 3.6 %collective-permute-start.15 = (f32[1,512]{1,0:T(1,128)S(1)}, f32[1,512]{1,0:T(1,128)S(1)}, u32[]{:S(2)}, u32[]{:S(2)}) collective-permute-start(f32[1,512]{1,0:T(1,128)S(1)} %add.9), channel_id=1, source_target_pairs={{0,8},{4,20},{8,0},{12,28},{16,24},{20,4},{24,16},{28,12},{1,9},{5... | collective-permute-start | bytes 6152 | tf_op jit(solution)/shard_map/ppermute | solution.py:559
  62.5 5.3 %collective-permute-start.17 = (bf16[256,128]{1,0:T(8,128)(2,1)S(1)}, bf16[256,128]{1,0:T(8,128)(2,1)S(1)}, u32[]{:S(2)}, u32[]{:S(2)}) collective-permute-start(bf16[256,128]{1,0:T(8,128)(2,1)S(1)} %shard_map.80.refs_0_), channel_id=1, source_target_pairs={{0,2},{1,3},{2,0},{3,1},{4,6},{5,7},{6,4},{7,5},{8,10},{9,11},{10,... | collective-permute-start | bytes 196616 | tf_op jit(solution)/shard_map/ppermute | solution.py:639
  67.8 5.1 %collective-permute-start.18 = (bf16[512,128]{1,0:T(8,128)(2,1)S(1)}, bf16[512,128]{1,0:T(8,128)(2,1)S(1)}, u32[]{:S(2)}, u32[]{:S(2)}) collective-permute-start(bf16[512,128]{1,0:T(8,128)(2,1)S(1)} %shard_map.81), channel_id=1, source_target_pairs={{0,1},{1,0},{2,3},{3,2},{4,5},{5,4},{6,7},{7,6},{8,9},{9,8},{10,11... | collective-permute-start | bytes 393224 | tf_op jit(solution)/shard_map/ppermute | solution.py:639
  69.4 3.6 %collective-permute-start.16 = (f32[1,512]{1,0:T(1,128)S(1)}, f32[1,512]{1,0:T(1,128)S(1)}, u32[]{:S(2)}, u32[]{:S(2)}) collective-permute-start(f32[1,512]{1,0:T(1,128)S(1)} %add.10.after), channel_id=1, source_target_pairs={{0,16},{4,12},{8,24},{12,4},{16,0},{20,28},{24,8},{28,20},{1,17},{... | collective-permute-start | bytes 6152 | tf_op jit(solution)/shard_map/ppermute | solution.py:559

commit v5 on v4

--- a/solution.py
+++ b/solution.py
@@ -278,7 +278,7 @@
 
 def boundary_kernel(
     nblk, place, off, acc, c, intra, inter, t, m, d,
-    send_0, send_1, send_2, send_3, keep, d_rest, f_v, ys, sems, d_sems,
+    send_0, send_1, keep, d_rest, f_v, ys, sems, d_sems,
 ):
     core = core_of(place)
     w = c.shape[2]
@@ -291,8 +291,8 @@
     here = pl.ds(pl.multiple_of(core * half, half), half)
     there = pl.ds(pl.multiple_of((1 - core) * half, half), half)
     away = boundary_sum(acc, ys, t, there).astype(BF16)
-    for q, send in enumerate((send_0, send_1, send_2, send_3)):
-        send[...] = away[q * half // 4 : (q + 1) * half // 4, :]
+    for q, send in enumerate((send_0, send_1)):
+        send[...] = away[q * half // 2 : (q + 1) * half // 2, :]
     keep[...] = boundary_sum(acc, ys, t, here)
     loads.wait_all()
 
@@ -304,13 +304,13 @@
     return pl.pallas_call(
         functools.partial(boundary_kernel, nblk),
         out_shape=(
-            *[jax.ShapeDtypeStruct((w // 8, nt), BF16)] * 4,
+            *[jax.ShapeDtypeStruct((w // 4, nt), BF16)] * 2,
             jax.ShapeDtypeStruct((w // 2, nt), F32),
             pltpu.VMEM((others, KB, BK, BK), BF16),
             pltpu.VMEM((12, BK, w), BF16),
         ),
         in_specs=[SMEM, SMEM] + [VMEM] * 6 + [ANY],
-        out_specs=(VMEM,) * 7,
+        out_specs=(VMEM,) * 5,
         scratch_shapes=[
             pltpu.VMEM((4 * BK, w), BF16),
             pltpu.SemaphoreType.DMA((4,)),

time: 74.3 us -> 74.2 us (level)
    ppermute x15 -> x13, starting transfers between devices: 15.4 us -> 14.8 us  [swap(): lax.ppermute(block, 'basis', [(i, i ^ mask[i % 2]) for i in range(count)])]
    ppermute x15 -> x13, waiting for transfers between devices: 8.97 us -> 9.31 us  [swap(): lax.ppermute(block, 'basis', [(i, i ^ mask[i % 2]) for i in range(count)])]
  transfers between devices with their start and end apart: 19 -> 17, of which waited for: 10 -> 9; matrix products, arithmetic and copies ran while one was open for 0% -> 0% of each run, Pallas kernels for 50% -> 50%
where the time goes in v5:
time: 74.2 us; the launch traced here: 74 us
  Pallas kernels  40.7 us (55%)
  starting transfers between devices  20.5 us (28%)
  waiting for transfers between devices  11.9 us (16%)
  between operations  0.84 us (1%)
    ppermute x13, starting transfers between devices, swap(): lax.ppermute(block, 'basis', [(i, i ^ mask[i % 2]) for i in range(count)])  14.8 us
    pallas_call x1, Pallas kernels, first(): pl.pallas_call(functools.partial(first_kernel, nblk), out_shape=(pltpu.VM...  11.5 us
    ppermute x13, waiting for transfers between devices, swap(): lax.ppermute(block, 'basis', [(i, i ^ mask[i % 2]) for i in range(count)])  9.31 us
    pallas_call x1, Pallas kernels, middle(): pl.pallas_call(functools.partial(middle_kernel, groups), out_shape=(pltpu...  8.33 us
    pallas_call x2, Pallas kernels, orthogonalize(): pl.pallas_call(functools.partial(orth_kernel, own, part), out_shape=(pltp...  7.18 us
    pallas_call x1, Pallas kernels, dipole_boundary(): pl.pallas_call(functools.partial(dipole_boundary_kernel, nblk), out_shape...  6.59 us
    ppermute x2, starting transfers between devices, on_device(): lax.ppermute(whole, 'orb', [(i, i ^ step) for i in range(planes)])  4.28 us
    pallas_call x1, Pallas kernels, project_boundary(): pl.pallas_call(functools.partial(boundary_kernel, nblk), out_shape=(*[jax...  3.65 us
  transfers between devices with their start and end apart: 17, of which 9 were waited for; matrix products, arithmetic and copies ran while one was open for 0% of the time, Pallas kernels for 50%

profile of v5, /device:TPU:0, one launch (start us, length us, event | category | flops | bytes accessed | tf_op | source)
XLA Modules:
  0.0 74.0 jit_solution(9882533973605282517)
XLA Ops:
  0.7 1.5 %shard_map.69 = (bf16[2,256,768]{2,1,0:T(8,128)(2,1)S(1)}, bf16[2,256,512]{2,1,0:T(8,128)(2,1)S(1)}, bf16[2,256,256]{2,1,0:T(8,128)(2,1)S(1)}) custom-call(s32[1]{0:T(128)} %bitcast.place, s32[1]{0:T(128)} %bitcast.2.z, bf16[16,256,512]{2,1,0:T(8,128)(2,1)} %bitcast.6, bf16[16,256,1024]{2,1,0:T(8,128)(2,1)} %bitcast.15), custom_call_target="tpu_custom_call" | custom-call | tf_op jit(solution)/shard_map/pallas_call | solution.py:114
  2.2 0.5 collective-permute-start
  2.7 0.7 collective-permute-start.1
  3.4 0.7 collective-permute-start.4
  4.1 11.5 %shard_map.68 = (f32[512,1024]{1,0:T(8,128)S(1)}, f32[768,1024]{1,0:T(8,128)S(1)}, bf16[16,256,768]{2,1,0:T(8,128)(2,1)S(1)}, bf16[16,256,1024]{2,1,0:T(8,128)(2,1)S(1)}, bf16[4,4,256,256]{3,2,1,0:T(8,128)(2,1)S(1)}) custom-call(s32[1]{0:T(128)} %bitcast.2.z, s32[4,16]{1,0:T(4,128)S(1)} %bitcast.11, bf16[16,256,512]{2,1,0:T(8,128)(2,1)S(1)} %bitcast.7, ...), custom_call_target="tpu_custom_call" | custom-call | flops 7247757312 | bytes 31457280 | tf_op jit(solution)/shard_map/pallas_call | solution.py:191
  15.6 3.6 %shard_map.70 = (bf16[128,1024]{1,0:T(8,128)(2,1)S(1)}, bf16[128,1024]{1,0:T(8,128)(2,1)S(1)}, f32[256,1024]{1,0:T(8,128)S(1)}, bf16[11,4,256,256]{3,2,1,0:T(8,128)(2,1)S(1)}, bf16[12,256,512]{2,1,0:T(8,128)(2,1)S(1)}) custom-call(s32[1]{0:T(128)} %bitcast.place, s32[4,16]{1,0:T(4,128)S(1)} %bitcast.12, f32[512,1024]{1,0:T(8,128)S(1)} %get-tuple-element.35.acc, ...), custom_call_target="tpu_custom_call" | custom-call | flops 512 | bytes 256 | tf_op jit(solution)/shard_map/pallas_call | solution.py:304
  19.3 5.3 %collective-permute-start.2 = (bf16[128,1024]{1,0:T(8,128)(2,1)S(1)}, bf16[128,1024]{1,0:T(8,128)(2,1)S(1)}, u32[]{:S(2)}, u32[]{:S(2)}) collective-permute-start(bf16[128,1024]{1,0:T(8,128)(2,1)S(1)} %get-tuple-element.41), channel_id=1, source_target_pairs={{0,4},{4,0},{8,12},{12,8},{16,20},{20,16},{24,28},{28,24},{1,5},{5... | collective-permute-start | bytes 786440 | tf_op jit(solution)/shard_map/ppermute | solution.py:559
  24.7 1.1 %collective-permute-done.2.refs_0_ = bf16[128,1024]{1,0:T(8,128)(2,1)S(1)} collective-permute-done((bf16[128,1024]{1,0:T(8,128)(2,1)S(1)}, bf16[128,1024]{1,0:T(8,128)(2,1)S(1)}, u32[]{:S(2)}, u32[]{:S(2)}) %collective-permute-start.2) | collective-permute-done | bytes 262176 | tf_op jit(solution)/shard_map/ppermute | solution.py:559
  25.7 0.4 collective-permute-done.3.refs_1_
  26.2 2.9 %collective-permute-start.5 = (bf16[256,1024]{1,0:T(8,128)(2,1)S(1)}, bf16[256,1024]{1,0:T(8,128)(2,1)S(1)}, u32[]{:S(2)}, u32[]{:S(2)}) collective-permute-start(bf16[256,1024]{1,0:T(8,128)(2,1)S(1)} %get-tuple-element.44.after.a), channel_id=1, source_target_pairs={{0,8},{4,20},{8,0},{12,28},{16,24},{20,4},{24,16},{28,12},{1,9},{5... | collective-permute-start | bytes 1572872 | tf_op jit(solution)/shard_map/ppermute | solution.py:559
  29.1 8.3 %shard_map.72 = (f32[768,1024]{1,0:T(8,128)S(1)}, bf16[4,4,256,256]{3,2,1,0:T(8,128)(2,1)S(1)}) custom-call(s32[4,16]{1,0:T(4,128)S(1)} %bitcast.13, bf16[256,1024]{1,0:T(8,128)(2,1)S(1)} %get-tuple-element.44.after.a, f32[768,1024]{1,0:T(8,128)S(1)} %get-tuple-element.45.acc, bf16[16,256,768]{2,1,0:T(8,128)(2,1)S(1)} %get-tuple-element.46.f, ...), custom_call_target="tpu_custom_call" | custom-call | flops 7247757312 | bytes 14680064 | tf_op jit(solution)/shard_map/pallas_call | solution.py:231
  37.6 0.9 %collective-permute-start.6 = (bf16[256,1024]{1,0:T(8,128)(2,1)S(1)}, bf16[256,1024]{1,0:T(8,128)(2,1)S(1)}, u32[]{:S(2)}, u32[]{:S(2)}) collective-permute-start(bf16[256,1024]{1,0:T(8,128)(2,1)S(1)} %get-tuple-element.49.after.a), channel_id=1, source_target_pairs={{0,16},{4,12},{8,24},{12,4},{16,0},{20,28},{24,8},{28,20},{1,17},{... | collective-permute-start | bytes 1572872 | tf_op jit(solution)/shard_map/ppermute | solution.py:559
  38.6 6.6 %shard_map.74 = (bf16[2,768,128]{2,1,0:T(8,128)(2,1)S(1)}, bf16[2,768,128]{2,1,0:T(8,128)(2,1)S(1)}, f32[4,768,128]{2,1,0:T(8,128)S(1)}) custom-call(s32[1]{0:T(128)} %bitcast.place, s32[4,16]{1,0:T(4,128)S(1)} %bitcast.14, bf16[256,1024]{1,0:T(8,128)(2,1)S(1)} %get-tuple-element.49.after.a, f32[768,1024]{1,0:T(8,128)S(1)} %get-tuple-element.50.acc, ...), custom_call_target="tpu_custom_call" | custom-call | flops 3221225472 | bytes 8388608 | tf_op jit(solution)/shard_map/pallas_call | solution.py:440
  45.2 0.5 collective-permute-start.8
  45.7 1.1 %collective-permute-done.6.refs_0_ = bf16[256,1024]{1,0:T(8,128)(2,1)S(1)} collective-permute-done((bf16[256,1024]{1,0:T(8,128)(2,1)S(1)}, bf16[256,1024]{1,0:T(8,128)(2,1)S(1)}, u32[]{:S(2)}, u32[]{:S(2)}) %collective-permute-start.6) | collective-permute-done | bytes 524320 | tf_op jit(solution)/shard_map/ppermute | solution.py:559
  47.0 0.5 collective-permute-done.8.refs_1_
  47.5 0.3 shard_map.76
  47.8 0.2 collective-permute-start.9
  48.0 1.2 %collective-permute-start.10 = (bf16[2,768,128]{2,1,0:T(8,128)(2,1)S(1)}, bf16[2,768,128]{2,1,0:T(8,128)(2,1)S(1)}, u32[]{:S(2)}, u32[]{:S(2)}) collective-permute-start(bf16[2,768,128]{2,1,0:T(8,128)(2,1)S(1)} %get-tuple-element.62), channel_id=1, source_target_pairs={{0,8},{4,20},{8,0},{12,28},{16,24},{20,4},{24,16},{28,12},{1,9},{5... | collective-permute-start | bytes 1179656 | tf_op jit(solution)/shard_map/ppermute | solution.py:559
  49.2 3.6 %shard_map.77 = (bf16[16,256,512]{2,1,0:T(8,128)(2,1)}, f32[1,512]{1,0:T(1,128)S(1)}) custom-call(s32[1]{0:T(128)} %bitcast.place, bf16[256,1024]{1,0:T(8,128)(2,1)S(1)} %get-tuple-element.56.p.after.x_in.mine, bf16[256,1024]{1,0:T(8,128)(2,1)S(1)} %get-tuple-element.56.p.after.x_in.mine, bf16[256,1024]{1,0:T(8,128)(2,1)S(1)} %get-tuple-element.56.p.after.x_in.mine, ...), custom_call_target="tpu_custom_call" | custom-call | flops 2147483648 | bytes 8388608 | tf_op jit(solution)/shard_map/pallas_call | solution.py:384
  52.8 3.6 %shard_map.78 = (bf16[16,256,512]{2,1,0:T(8,128)(2,1)}, f32[1,512]{1,0:T(1,128)S(1)}) custom-call(s32[1]{0:T(128)} %bitcast.place, bf16[256,1024]{1,0:T(8,128)(2,1)S(1)} %collective-permute-done.9.p.other, bf16[256,1024]{1,0:T(8,128)(2,1)S(1)} %get-tuple-element.56.p.after.x_in.mine, ...), custom_call_target="tpu_custom_call", output_to_operand_aliasing={{0}: (3, {})} | custom-call | flops 2147483648 | bytes 8388608 | tf_op jit(solution)/shard_map/pallas_call | solution.py:384
  56.6 0.8 %collective-permute-start.11 = (bf16[1,768,128]{2,1,0:T(8,128)(2,1)S(1)}, bf16[1,768,128]{2,1,0:T(8,128)(2,1)S(1)}, u32[]{:S(2)}, u32[]{:S(2)}) collective-permute-start(bf16[1,768,128]{2,1,0:T(8,128)(2,1)S(1)} %get-tuple-element.64), channel_id=1, source_target_pairs={{0,16},{4,12},{8,24},{12,4},{16,0},{20,28},{24,8},{28,20},{1,17},{... | collective-permute-start | bytes 589832 | tf_op jit(solution)/shard_map/ppermute | solution.py:559
  57.4 1.2 %collective-permute-done.12 = f32[1,512]{1,0:T(1,128)S(1)} collective-permute-done((f32[1,512]{1,0:T(1,128)S(1)}, f32[1,512]{1,0:T(1,128)S(1)}, u32[]{:S(2)}, u32[]{:S(2)}) %collective-permute-start.12) | collective-permute-done | bytes 2080 | tf_op jit(solution)/shard_map/ppermute | solution.py:559
  58.5 1.2 %collective-permute-start.13 = (f32[1,512]{1,0:T(1,128)S(1)}, f32[1,512]{1,0:T(1,128)S(1)}, u32[]{:S(2)}, u32[]{:S(2)}) collective-permute-start(f32[1,512]{1,0:T(1,128)S(1)} %add.9), channel_id=1, source_target_pairs={{0,8},{4,20},{8,0},{12,28},{16,24},{20,4},{24,16},{28,12},{1,9},{5... | collective-permute-start | bytes 6152 | tf_op jit(solution)/shard_map/ppermute | solution.py:559
  59.7 2.4 %collective-permute-done.13 = f32[1,512]{1,0:T(1,128)S(1)} collective-permute-done((f32[1,512]{1,0:T(1,128)S(1)}, f32[1,512]{1,0:T(1,128)S(1)}, u32[]{:S(2)}, u32[]{:S(2)}) %collective-permute-start.13) | collective-permute-done | bytes 2080 | tf_op jit(solution)/shard_map/ppermute | solution.py:559
  62.1 0.2 collective-permute-done.11.got
  62.3 2.6 %collective-permute-start.15 = (bf16[256,128]{1,0:T(8,128)(2,1)S(1)}, bf16[256,128]{1,0:T(8,128)(2,1)S(1)}, u32[]{:S(2)}, u32[]{:S(2)}) collective-permute-start(bf16[256,128]{1,0:T(8,128)(2,1)S(1)} %shard_map.80.refs_0_), channel_id=1, source_target_pairs={{0,2},{1,3},{2,0},{3,1},{4,6},{5,7},{6,4},{7,5},{8,10},{9,11},{10,... | collective-permute-start | bytes 196616 | tf_op jit(solution)/shard_map/ppermute | solution.py:639
  65.0 2.6 %collective-permute-done.15.refs_1_ = bf16[256,128]{1,0:T(8,128)(2,1)S(1)} collective-permute-done((bf16[256,128]{1,0:T(8,128)(2,1)S(1)}, bf16[256,128]{1,0:T(8,128)(2,1)S(1)}, u32[]{:S(2)}, u32[]{:S(2)}) %collective-permute-start.15) | collective-permute-done | bytes 65568 | tf_op jit(solution)/shard_map/ppermute | solution.py:639
  67.6 1.6 %collective-permute-start.16 = (bf16[512,128]{1,0:T(8,128)(2,1)S(1)}, bf16[512,128]{1,0:T(8,128)(2,1)S(1)}, u32[]{:S(2)}, u32[]{:S(2)}) collective-permute-start(bf16[512,128]{1,0:T(8,128)(2,1)S(1)} %shard_map.81), channel_id=1, source_target_pairs={{0,1},{1,0},{2,3},{3,2},{4,5},{5,4},{6,7},{7,6},{8,9},{9,8},{10,11... | collective-permute-start | bytes 393224 | tf_op jit(solution)/shard_map/ppermute | solution.py:639
  69.2 1.1 %collective-permute-start.14 = (f32[1,512]{1,0:T(1,128)S(1)}, f32[1,512]{1,0:T(1,128)S(1)}, u32[]{:S(2)}, u32[]{:S(2)}) collective-permute-start(f32[1,512]{1,0:T(1,128)S(1)} %add.10.after), channel_id=1, source_target_pairs={{0,16},{4,12},{8,24},{12,4},{16,0},{20,28},{24,8},{28,20},{1,17},{... | collective-permute-start | bytes 6152 | tf_op jit(solution)/shard_map/ppermute | solution.py:559
  70.3 2.5 %collective-permute-done.14 = f32[1,512]{1,0:T(1,128)S(1)} collective-permute-done((f32[1,512]{1,0:T(1,128)S(1)}, f32[1,512]{1,0:T(1,128)S(1)}, u32[]{:S(2)}, u32[]{:S(2)}) %collective-permute-start.14) | collective-permute-done | bytes 2080 | tf_op jit(solution)/shard_map/ppermute | solution.py:559
  72.8 1.2 %shard_map.82 = bf16[128,512]{1,0:T(8,128)(2,1)} custom-call(s32[1]{0:T(128)} %bitcast.place, s32[1]{0:T(128)} %bitcast.2.z, f32[1,768,128]{2,1,0:T(8,128)S(1)} %get-tuple-element.63.keep, bf16[1,768,128]{2,1,0:T(8,128)(2,1)S(1)} %collective-permute-done.11.got, bf16[256,1024]{1,0:T(8,128)(2,1)S(1)} %get-tuple-element.56.p.after.x_in.mine, ...), custom_call_target="tpu_custom_call" | custom-call | tf_op jit(solution)/shard_map/pallas_call | solution.py:548
  (25 shorter events, 0.7 us)
Async XLA Ops:
  0.6 3.5 %copy-start = (bf16[4096,512]{1,0:T(8,128)(2,1)S(1)}, bf16[4096,512]{1,0:T(8,128)(2,1)}, u32[]{:S(2)}) copy-start(bf16[4096,512]{1,0:T(8,128)(2,1)} %param.5) | copy-start | bytes 12582916
  0.6 3.5 %copy-start.1 = (s32[16,4]{0,1:T(4,128)S(1)}, s32[16,4]{0,1:T(4,128)}, u32[]{:S(2)}) copy-start(s32[16,4]{0,1:T(4,128)} %param.9) | copy-start | bytes 772
  2.2 13.4 %collective-permute-start = (bf16[2,256,768]{2,1,0:T(8,128)(2,1)S(1)}, bf16[2,256,768]{2,1,0:T(8,128)(2,1)S(1)}, u32[]{:S(2)}, u32[]{:S(2)}) collective-permute-start(bf16[2,256,768]{2,1,0:T(8,128)(2,1)S(1)} %get-tuple-element.36), channel_id=1, source_target_pairs={{0,4},{4,0},{8,12},{12,8},{16,20},{20,16},{24,28},{28,24},{1,5},{5... | collective-permute-start | bytes 2359304 | tf_op jit(solution)/shard_map/ppermute | solution.py:559
  2.7 12.9 %collective-permute-start.1 = (bf16[2,256,512]{2,1,0:T(8,128)(2,1)S(1)}, bf16[2,256,512]{2,1,0:T(8,128)(2,1)S(1)}, u32[]{:S(2)}, u32[]{:S(2)}) collective-permute-start(bf16[2,256,512]{2,1,0:T(8,128)(2,1)S(1)} %get-tuple-element.37), channel_id=1, source_target_pairs={{4,8},{12,16},{20,24},{8,4},{16,12},{24,20},{5,9},{13,17},{21,25},... | collective-permute-start | bytes 1572872 | tf_op jit(solution)/shard_map/ppermute | solution.py:564
  3.4 21.2 %collective-permute-start.4 = (bf16[2,256,256]{2,1,0:T(8,128)(2,1)S(1)}, bf16[2,256,256]{2,1,0:T(8,128)(2,1)S(1)}, u32[]{:S(2)}, u32[]{:S(2)}) collective-permute-start(bf16[2,256,256]{2,1,0:T(8,128)(2,1)S(1)} %get-tuple-element.43), channel_id=1, source_target_pairs={{4,8},{12,16},{20,24},{8,4},{16,12},{24,20},{5,9},{13,17},{21,25},... | collective-permute-start | bytes 786440 | tf_op jit(solution)/shard_map/ppermute | solution.py:564
  19.3 6.4 %collective-permute-start.2 = (bf16[128,1024]{1,0:T(8,128)(2,1)S(1)}, bf16[128,1024]{1,0:T(8,128)(2,1)S(1)}, u32[]{:S(2)}, u32[]{:S(2)}) collective-permute-start(bf16[128,1024]{1,0:T(8,128)(2,1)S(1)} %get-tuple-element.41), channel_id=1, source_target_pairs={{0,4},{4,0},{8,12},{12,8},{16,20},{20,16},{24,28},{28,24},{1,5},{5... | collective-permute-start | bytes 786440 | tf_op jit(solution)/shard_map/ppermute | solution.py:559
  24.6 1.5 %collective-permute-start.3 = (bf16[128,1024]{1,0:T(8,128)(2,1)S(1)}, bf16[128,1024]{1,0:T(8,128)(2,1)S(1)}, u32[]{:S(2)}, u32[]{:S(2)}) collective-permute-start(bf16[128,1024]{1,0:T(8,128)(2,1)S(1)} %get-tuple-element.42), channel_id=1, source_target_pairs={{0,4},{4,0},{8,12},{12,8},{16,20},{20,16},{24,28},{28,24},{1,5},{5... | collective-permute-start | bytes 786440 | tf_op jit(solution)/shard_map/ppermute | solution.py:559
  26.2 11.3 %collective-permute-start.5 = (bf16[256,1024]{1,0:T(8,128)(2,1)S(1)}, bf16[256,1024]{1,0:T(8,128)(2,1)S(1)}, u32[]{:S(2)}, u32[]{:S(2)}) collective-permute-start(bf16[256,1024]{1,0:T(8,128)(2,1)S(1)} %get-tuple-element.44.after.a), channel_id=1, source_target_pairs={{0,8},{4,20},{8,0},{12,28},{16,24},{20,4},{24,16},{28,12},{1,9},{5... | collective-permute-start | bytes 1572872 | tf_op jit(solution)/shard_map/ppermute | solution.py:559
  37.6 9.2 %collective-permute-start.6 = (bf16[256,1024]{1,0:T(8,128)(2,1)S(1)}, bf16[256,1024]{1,0:T(8,128)(2,1)S(1)}, u32[]{:S(2)}, u32[]{:S(2)}) collective-permute-start(bf16[256,1024]{1,0:T(8,128)(2,1)S(1)} %get-tuple-element.49.after.a), channel_id=1, source_target_pairs={{0,16},{4,12},{8,24},{12,4},{16,0},{20,28},{24,8},{28,20},{1,17},{... | collective-permute-start | bytes 1572872 | tf_op jit(solution)/shard_map/ppermute | solution.py:559
  45.2 1.8 %collective-permute-start.7 = (bf16[2,768,128]{2,1,0:T(8,128)(2,1)S(1)}, bf16[2,768,128]{2,1,0:T(8,128)(2,1)S(1)}, u32[]{:S(2)}, u32[]{:S(2)}) collective-permute-start(bf16[2,768,128]{2,1,0:T(8,128)(2,1)S(1)} %get-tuple-element.53.after), channel_id=1, source_target_pairs={{0,4},{4,0},{8,12},{12,8},{16,20},{20,16},{24,28},{28,24},{1,5},{5... | collective-permute-start | bytes 1179656 | tf_op jit(solution)/shard_map/ppermute | solution.py:559
  45.2 2.3 %collective-permute-start.8 = (bf16[2,768,128]{2,1,0:T(8,128)(2,1)S(1)}, bf16[2,768,128]{2,1,0:T(8,128)(2,1)S(1)}, u32[]{:S(2)}, u32[]{:S(2)}) collective-permute-start(bf16[2,768,128]{2,1,0:T(8,128)(2,1)S(1)} %get-tuple-element.55), channel_id=1, source_target_pairs={{0,4},{4,0},{8,12},{12,8},{16,20},{20,16},{24,28},{28,24},{1,5},{5... | collective-permute-start | bytes 1179656 | tf_op jit(solution)/shard_map/ppermute | solution.py:559
  47.8 5.0 %collective-permute-start.9 = (bf16[256,1024]{1,0:T(8,128)(2,1)S(1)}, bf16[256,1024]{1,0:T(8,128)(2,1)S(1)}, u32[]{:S(2)}, u32[]{:S(2)}) collective-permute-start(bf16[256,1024]{1,0:T(8,128)(2,1)S(1)} %get-tuple-element.56.p.after.x_in.mine), channel_id=1, source_target_pairs={{0,4},{4,0},{8,12},{12,8},{16,20},{20,16},{24,28},{28,24},{1,5},{5... | collective-permute-start | bytes 1572872 | tf_op jit(solution)/shard_map/ppermute | solution.py:559
  48.0 8.4 %collective-permute-start.10 = (bf16[2,768,128]{2,1,0:T(8,128)(2,1)S(1)}, bf16[2,768,128]{2,1,0:T(8,128)(2,1)S(1)}, u32[]{:S(2)}, u32[]{:S(2)}) collective-permute-start(bf16[2,768,128]{2,1,0:T(8,128)(2,1)S(1)} %get-tuple-element.62), channel_id=1, source_target_pairs={{0,8},{4,20},{8,0},{12,28},{16,24},{20,4},{24,16},{28,12},{1,9},{5... | collective-permute-start | bytes 1179656 | tf_op jit(solution)/shard_map/ppermute | solution.py:559
  56.6 5.8 %collective-permute-start.11 = (bf16[1,768,128]{2,1,0:T(8,128)(2,1)S(1)}, bf16[1,768,128]{2,1,0:T(8,128)(2,1)S(1)}, u32[]{:S(2)}, u32[]{:S(2)}) collective-permute-start(bf16[1,768,128]{2,1,0:T(8,128)(2,1)S(1)} %get-tuple-element.64), channel_id=1, source_target_pairs={{0,16},{4,12},{8,24},{12,4},{16,0},{20,28},{24,8},{28,20},{1,17},{... | collective-permute-start | bytes 589832 | tf_op jit(solution)/shard_map/ppermute | solution.py:559
  57.4 1.2 %collective-permute-start.12 = (f32[1,512]{1,0:T(1,128)S(1)}, f32[1,512]{1,0:T(1,128)S(1)}, u32[]{:S(2)}, u32[]{:S(2)}) collective-permute-start(f32[1,512]{1,0:T(1,128)S(1)} %get-tuple-element.65), channel_id=1, source_target_pairs={{0,4},{4,0},{8,12},{12,8},{16,20},{20,16},{24,28},{28,24},{1,5},{5... | collective-permute-start | bytes 6152 | tf_op jit(solution)/shard_map/ppermute | solution.py:559
  58.5 3.6 %collective-permute-start.13 = (f32[1,512]{1,0:T(1,128)S(1)}, f32[1,512]{1,0:T(1,128)S(1)}, u32[]{:S(2)}, u32[]{:S(2)}) collective-permute-start(f32[1,512]{1,0:T(1,128)S(1)} %add.9), channel_id=1, source_target_pairs={{0,8},{4,20},{8,0},{12,28},{16,24},{20,4},{24,16},{28,12},{1,9},{5... | collective-permute-start | bytes 6152 | tf_op jit(solution)/shard_map/ppermute | solution.py:559
  62.3 5.2 %collective-permute-start.15 = (bf16[256,128]{1,0:T(8,128)(2,1)S(1)}, bf16[256,128]{1,0:T(8,128)(2,1)S(1)}, u32[]{:S(2)}, u32[]{:S(2)}) collective-permute-start(bf16[256,128]{1,0:T(8,128)(2,1)S(1)} %shard_map.80.refs_0_), channel_id=1, source_target_pairs={{0,2},{1,3},{2,0},{3,1},{4,6},{5,7},{6,4},{7,5},{8,10},{9,11},{10,... | collective-permute-start | bytes 196616 | tf_op jit(solution)/shard_map/ppermute | solution.py:639
  67.6 5.2 %collective-permute-start.16 = (bf16[512,128]{1,0:T(8,128)(2,1)S(1)}, bf16[512,128]{1,0:T(8,128)(2,1)S(1)}, u32[]{:S(2)}, u32[]{:S(2)}) collective-permute-start(bf16[512,128]{1,0:T(8,128)(2,1)S(1)} %shard_map.81), channel_id=1, source_target_pairs={{0,1},{1,0},{2,3},{3,2},{4,5},{5,4},{6,7},{7,6},{8,9},{9,8},{10,11... | collective-permute-start | bytes 393224 | tf_op jit(solution)/shard_map/ppermute | solution.py:639
  69.2 3.6 %collective-permute-start.14 = (f32[1,512]{1,0:T(1,128)S(1)}, f32[1,512]{1,0:T(1,128)S(1)}, u32[]{:S(2)}, u32[]{:S(2)}) collective-permute-start(f32[1,512]{1,0:T(1,128)S(1)} %add.10.after), channel_id=1, source_target_pairs={{0,16},{4,12},{8,24},{12,4},{16,0},{20,28},{24,8},{28,20},{1,17},{... | collective-permute-start | bytes 6152 | tf_op jit(solution)/shard_map/ppermute | solution.py:559

commit v6 on v5

--- a/solution.py
+++ b/solution.py
@@ -365,13 +365,13 @@
     here = pl.ds(pl.multiple_of(side * half, half), half)
     stores = Loads(out_sems)
     total = None
-    for at in range(part[0], part[1], 1):
-        block = c[at : at + 1, :, here].reshape(1 * BK, half)
-        x = orth_rows32(block, t[at : at + 1].reshape(1 * BK, nt), p[...])
-        x_v[at : at + 1] = x.astype(BF16).reshape(1, BK, half)
+    for at in range(part[0], part[1], 2):
+        block = c[at : at + 2, :, here].reshape(2 * BK, half)
+        x = orth_rows32(block, t[at : at + 2].reshape(2 * BK, nt), p[...])
+        x_v[at : at + 2] = x.astype(BF16).reshape(2, BK, half)
         squares = square_sum(x)
         total = squares if total is None else total + squares
-        stores.start(x_v.at[at : at + 1], x_out.at[at : at + 1, :, here])
+        stores.start(x_v.at[at : at + 2], x_out.at[at : at + 2, :, here])
     sq[...] = sq_in[...]
     sq[:, here] += total
     stores.wait_all()

time: 74.2 us -> 74.2 us (level)
  transfers between devices with their start and end apart: 17 -> 17, of which waited for: 9 -> 9; matrix products, arithmetic and copies ran while one was open for 0% -> 0% of each run, Pallas kernels for 50% -> 51%
where the time goes in v6:
time: 74.2 us; the launch traced here: 74 us
  Pallas kernels  40.8 us (55%)
  starting transfers between devices  20.5 us (28%)
  waiting for transfers between devices  11.9 us (16%)
  between operations  0.84 us (1%)
    ppermute x13, starting transfers between devices, swap(): lax.ppermute(block, 'basis', [(i, i ^ mask[i % 2]) for i in range(count)])  14.9 us
    pallas_call x1, Pallas kernels, first(): pl.pallas_call(functools.partial(first_kernel, nblk), out_shape=(pltpu.VM...  11.5 us
    ppermute x13, waiting for transfers between devices, swap(): lax.ppermute(block, 'basis', [(i, i ^ mask[i % 2]) for i in range(count)])  9.3 us
    pallas_call x1, Pallas kernels, middle(): pl.pallas_call(functools.partial(middle_kernel, groups), out_shape=(pltpu...  8.33 us
    pallas_call x2, Pallas kernels, orthogonalize(): pl.pallas_call(functools.partial(orth_kernel, own, part), out_shape=(pltp...  7.22 us
    pallas_call x1, Pallas kernels, dipole_boundary(): pl.pallas_call(functools.partial(dipole_boundary_kernel, nblk), out_shape...  6.59 us
    ppermute x2, starting transfers between devices, on_device(): lax.ppermute(whole, 'orb', [(i, i ^ step) for i in range(planes)])  4.29 us
    pallas_call x1, Pallas kernels, project_boundary(): pl.pallas_call(functools.partial(boundary_kernel, nblk), out_shape=(*[jax...  3.65 us
  transfers between devices with their start and end apart: 17, of which 9 were waited for; matrix products, arithmetic and copies ran while one was open for 0% of the time, Pallas kernels for 51%

profile of v6, /device:TPU:0, one launch (start us, length us, event | category | flops | bytes accessed | tf_op | source)
XLA Modules:
  0.0 74.0 jit_solution(8246500936898300262)
XLA Ops:
  0.7 1.5 %shard_map.69 = (bf16[2,256,768]{2,1,0:T(8,128)(2,1)S(1)}, bf16[2,256,512]{2,1,0:T(8,128)(2,1)S(1)}, bf16[2,256,256]{2,1,0:T(8,128)(2,1)S(1)}) custom-call(s32[1]{0:T(128)} %bitcast.place, s32[1]{0:T(128)} %bitcast.2.z, bf16[16,256,512]{2,1,0:T(8,128)(2,1)} %bitcast.6, bf16[16,256,1024]{2,1,0:T(8,128)(2,1)} %bitcast.15), custom_call_target="tpu_custom_call" | custom-call | tf_op jit(solution)/shard_map/pallas_call | solution.py:114
  2.2 0.5 collective-permute-start
  2.7 0.7 collective-permute-start.1
  3.4 0.7 collective-permute-start.4
  4.1 11.5 %shard_map.68 = (f32[512,1024]{1,0:T(8,128)S(1)}, f32[768,1024]{1,0:T(8,128)S(1)}, bf16[16,256,768]{2,1,0:T(8,128)(2,1)S(1)}, bf16[16,256,1024]{2,1,0:T(8,128)(2,1)S(1)}, bf16[4,4,256,256]{3,2,1,0:T(8,128)(2,1)S(1)}) custom-call(s32[1]{0:T(128)} %bitcast.2.z, s32[4,16]{1,0:T(4,128)S(1)} %bitcast.11, bf16[16,256,512]{2,1,0:T(8,128)(2,1)S(1)} %bitcast.7, ...), custom_call_target="tpu_custom_call" | custom-call | flops 7247757312 | bytes 31457280 | tf_op jit(solution)/shard_map/pallas_call | solution.py:191
  15.6 3.6 %shard_map.70 = (bf16[128,1024]{1,0:T(8,128)(2,1)S(1)}, bf16[128,1024]{1,0:T(8,128)(2,1)S(1)}, f32[256,1024]{1,0:T(8,128)S(1)}, bf16[11,4,256,256]{3,2,1,0:T(8,128)(2,1)S(1)}, bf16[12,256,512]{2,1,0:T(8,128)(2,1)S(1)}) custom-call(s32[1]{0:T(128)} %bitcast.place, s32[4,16]{1,0:T(4,128)S(1)} %bitcast.12, f32[512,1024]{1,0:T(8,128)S(1)} %get-tuple-element.35.acc, ...), custom_call_target="tpu_custom_call" | custom-call | flops 512 | bytes 256 | tf_op jit(solution)/shard_map/pallas_call | solution.py:304
  19.3 5.3 %collective-permute-start.2 = (bf16[128,1024]{1,0:T(8,128)(2,1)S(1)}, bf16[128,1024]{1,0:T(8,128)(2,1)S(1)}, u32[]{:S(2)}, u32[]{:S(2)}) collective-permute-start(bf16[128,1024]{1,0:T(8,128)(2,1)S(1)} %get-tuple-element.41), channel_id=1, source_target_pairs={{0,4},{4,0},{8,12},{12,8},{16,20},{20,16},{24,28},{28,24},{1,5},{5... | collective-permute-start | bytes 786440 | tf_op jit(solution)/shard_map/ppermute | solution.py:559
  24.7 1.1 %collective-permute-done.2.refs_0_ = bf16[128,1024]{1,0:T(8,128)(2,1)S(1)} collective-permute-done((bf16[128,1024]{1,0:T(8,128)(2,1)S(1)}, bf16[128,1024]{1,0:T(8,128)(2,1)S(1)}, u32[]{:S(2)}, u32[]{:S(2)}) %collective-permute-start.2) | collective-permute-done | bytes 262176 | tf_op jit(solution)/shard_map/ppermute | solution.py:559
  25.7 0.4 collective-permute-done.3.refs_1_
  26.2 2.9 %collective-permute-start.5 = (bf16[256,1024]{1,0:T(8,128)(2,1)S(1)}, bf16[256,1024]{1,0:T(8,128)(2,1)S(1)}, u32[]{:S(2)}, u32[]{:S(2)}) collective-permute-start(bf16[256,1024]{1,0:T(8,128)(2,1)S(1)} %get-tuple-element.44.after.a), channel_id=1, source_target_pairs={{0,8},{4,20},{8,0},{12,28},{16,24},{20,4},{24,16},{28,12},{1,9},{5... | collective-permute-start | bytes 1572872 | tf_op jit(solution)/shard_map/ppermute | solution.py:559
  29.1 8.3 %shard_map.72 = (f32[768,1024]{1,0:T(8,128)S(1)}, bf16[4,4,256,256]{3,2,1,0:T(8,128)(2,1)S(1)}) custom-call(s32[4,16]{1,0:T(4,128)S(1)} %bitcast.13, bf16[256,1024]{1,0:T(8,128)(2,1)S(1)} %get-tuple-element.44.after.a, f32[768,1024]{1,0:T(8,128)S(1)} %get-tuple-element.45.acc, bf16[16,256,768]{2,1,0:T(8,128)(2,1)S(1)} %get-tuple-element.46.f, ...), custom_call_target="tpu_custom_call" | custom-call | flops 7247757312 | bytes 14680064 | tf_op jit(solution)/shard_map/pallas_call | solution.py:231
  37.6 0.9 %collective-permute-start.6 = (bf16[256,1024]{1,0:T(8,128)(2,1)S(1)}, bf16[256,1024]{1,0:T(8,128)(2,1)S(1)}, u32[]{:S(2)}, u32[]{:S(2)}) collective-permute-start(bf16[256,1024]{1,0:T(8,128)(2,1)S(1)} %get-tuple-element.49.after.a), channel_id=1, source_target_pairs={{0,16},{4,12},{8,24},{12,4},{16,0},{20,28},{24,8},{28,20},{1,17},{... | collective-permute-start | bytes 1572872 | tf_op jit(solution)/shard_map/ppermute | solution.py:559
  38.6 6.6 %shard_map.74 = (bf16[2,768,128]{2,1,0:T(8,128)(2,1)S(1)}, bf16[2,768,128]{2,1,0:T(8,128)(2,1)S(1)}, f32[4,768,128]{2,1,0:T(8,128)S(1)}) custom-call(s32[1]{0:T(128)} %bitcast.place, s32[4,16]{1,0:T(4,128)S(1)} %bitcast.14, bf16[256,1024]{1,0:T(8,128)(2,1)S(1)} %get-tuple-element.49.after.a, f32[768,1024]{1,0:T(8,128)S(1)} %get-tuple-element.50.acc, ...), custom_call_target="tpu_custom_call" | custom-call | flops 3221225472 | bytes 8388608 | tf_op jit(solution)/shard_map/pallas_call | solution.py:440
  45.2 0.5 collective-permute-start.8
  45.7 1.1 %collective-permute-done.6.refs_0_ = bf16[256,1024]{1,0:T(8,128)(2,1)S(1)} collective-permute-done((bf16[256,1024]{1,0:T(8,128)(2,1)S(1)}, bf16[256,1024]{1,0:T(8,128)(2,1)S(1)}, u32[]{:S(2)}, u32[]{:S(2)}) %collective-permute-start.6) | collective-permute-done | bytes 524320 | tf_op jit(solution)/shard_map/ppermute | solution.py:559
  47.0 0.5 collective-permute-done.8.refs_1_
  47.5 0.3 shard_map.76
  47.8 0.2 collective-permute-start.9
  48.0 1.2 %collective-permute-start.10 = (bf16[2,768,128]{2,1,0:T(8,128)(2,1)S(1)}, bf16[2,768,128]{2,1,0:T(8,128)(2,1)S(1)}, u32[]{:S(2)}, u32[]{:S(2)}) collective-permute-start(bf16[2,768,128]{2,1,0:T(8,128)(2,1)S(1)} %get-tuple-element.62), channel_id=1, source_target_pairs={{0,8},{4,20},{8,0},{12,28},{16,24},{20,4},{24,16},{28,12},{1,9},{5... | collective-permute-start | bytes 1179656 | tf_op jit(solution)/shard_map/ppermute | solution.py:559
  49.2 3.6 %shard_map.77 = (bf16[16,256,512]{2,1,0:T(8,128)(2,1)}, f32[1,512]{1,0:T(1,128)S(1)}) custom-call(s32[1]{0:T(128)} %bitcast.place, bf16[256,1024]{1,0:T(8,128)(2,1)S(1)} %get-tuple-element.56.p.after.x_in.mine, bf16[256,1024]{1,0:T(8,128)(2,1)S(1)} %get-tuple-element.56.p.after.x_in.mine, bf16[256,1024]{1,0:T(8,128)(2,1)S(1)} %get-tuple-element.56.p.after.x_in.mine, ...), custom_call_target="tpu_custom_call" | custom-call | flops 2147483648 | bytes 8388608 | tf_op jit(solution)/shard_map/pallas_call | solution.py:384
  52.9 3.6 %shard_map.78 = (bf16[16,256,512]{2,1,0:T(8,128)(2,1)}, f32[1,512]{1,0:T(1,128)S(1)}) custom-call(s32[1]{0:T(128)} %bitcast.place, bf16[256,1024]{1,0:T(8,128)(2,1)S(1)} %collective-permute-done.9.p.other, bf16[256,1024]{1,0:T(8,128)(2,1)S(1)} %get-tuple-element.56.p.after.x_in.mine, ...), custom_call_target="tpu_custom_call", output_to_operand_aliasing={{0}: (3, {})} | custom-call | flops 2147483648 | bytes 8388608 | tf_op jit(solution)/shard_map/pallas_call | solution.py:384
  56.6 0.8 %collective-permute-start.11 = (bf16[1,768,128]{2,1,0:T(8,128)(2,1)S(1)}, bf16[1,768,128]{2,1,0:T(8,128)(2,1)S(1)}, u32[]{:S(2)}, u32[]{:S(2)}) collective-permute-start(bf16[1,768,128]{2,1,0:T(8,128)(2,1)S(1)} %get-tuple-element.64), channel_id=1, source_target_pairs={{0,16},{4,12},{8,24},{12,4},{16,0},{20,28},{24,8},{28,20},{1,17},{... | collective-permute-start | bytes 589832 | tf_op jit(solution)/shard_map/ppermute | solution.py:559
  57.4 1.2 %collective-permute-done.12 = f32[1,512]{1,0:T(1,128)S(1)} collective-permute-done((f32[1,512]{1,0:T(1,128)S(1)}, f32[1,512]{1,0:T(1,128)S(1)}, u32[]{:S(2)}, u32[]{:S(2)}) %collective-permute-start.12) | collective-permute-done | bytes 2080 | tf_op jit(solution)/shard_map/ppermute | solution.py:559
  58.6 1.2 %collective-permute-start.13 = (f32[1,512]{1,0:T(1,128)S(1)}, f32[1,512]{1,0:T(1,128)S(1)}, u32[]{:S(2)}, u32[]{:S(2)}) collective-permute-start(f32[1,512]{1,0:T(1,128)S(1)} %add.9), channel_id=1, source_target_pairs={{0,8},{4,20},{8,0},{12,28},{16,24},{20,4},{24,16},{28,12},{1,9},{5... | collective-permute-start | bytes 6152 | tf_op jit(solution)/shard_map/ppermute | solution.py:559
  59.8 2.4 %collective-permute-done.13 = f32[1,512]{1,0:T(1,128)S(1)} collective-permute-done((f32[1,512]{1,0:T(1,128)S(1)}, f32[1,512]{1,0:T(1,128)S(1)}, u32[]{:S(2)}, u32[]{:S(2)}) %collective-permute-start.13) | collective-permute-done | bytes 2080 | tf_op jit(solution)/shard_map/ppermute | solution.py:559
  62.2 0.2 collective-permute-done.11.got
  62.4 2.6 %collective-permute-start.15 = (bf16[256,128]{1,0:T(8,128)(2,1)S(1)}, bf16[256,128]{1,0:T(8,128)(2,1)S(1)}, u32[]{:S(2)}, u32[]{:S(2)}) collective-permute-start(bf16[256,128]{1,0:T(8,128)(2,1)S(1)} %shard_map.80.refs_0_), channel_id=1, source_target_pairs={{0,2},{1,3},{2,0},{3,1},{4,6},{5,7},{6,4},{7,5},{8,10},{9,11},{10,... | collective-permute-start | bytes 196616 | tf_op jit(solution)/shard_map/ppermute | solution.py:639
  65.0 2.6 %collective-permute-done.15.refs_1_ = bf16[256,128]{1,0:T(8,128)(2,1)S(1)} collective-permute-done((bf16[256,128]{1,0:T(8,128)(2,1)S(1)}, bf16[256,128]{1,0:T(8,128)(2,1)S(1)}, u32[]{:S(2)}, u32[]{:S(2)}) %collective-permute-start.15) | collective-permute-done | bytes 65568 | tf_op jit(solution)/shard_map/ppermute | solution.py:639
  67.6 1.6 %collective-permute-start.16 = (bf16[512,128]{1,0:T(8,128)(2,1)S(1)}, bf16[512,128]{1,0:T(8,128)(2,1)S(1)}, u32[]{:S(2)}, u32[]{:S(2)}) collective-permute-start(bf16[512,128]{1,0:T(8,128)(2,1)S(1)} %shard_map.81), channel_id=1, source_target_pairs={{0,1},{1,0},{2,3},{3,2},{4,5},{5,4},{6,7},{7,6},{8,9},{9,8},{10,11... | collective-permute-start | bytes 393224 | tf_op jit(solution)/shard_map/ppermute | solution.py:639
  69.3 1.1 %collective-permute-start.14 = (f32[1,512]{1,0:T(1,128)S(1)}, f32[1,512]{1,0:T(1,128)S(1)}, u32[]{:S(2)}, u32[]{:S(2)}) collective-permute-start(f32[1,512]{1,0:T(1,128)S(1)} %add.10.after), channel_id=1, source_target_pairs={{0,16},{4,12},{8,24},{12,4},{16,0},{20,28},{24,8},{28,20},{1,17},{... | collective-permute-start | bytes 6152 | tf_op jit(solution)/shard_map/ppermute | solution.py:559
  70.4 2.5 %collective-permute-done.14 = f32[1,512]{1,0:T(1,128)S(1)} collective-permute-done((f32[1,512]{1,0:T(1,128)S(1)}, f32[1,512]{1,0:T(1,128)S(1)}, u32[]{:S(2)}, u32[]{:S(2)}) %collective-permute-start.14) | collective-permute-done | bytes 2080 | tf_op jit(solution)/shard_map/ppermute | solution.py:559
  72.8 1.2 %shard_map.82 = bf16[128,512]{1,0:T(8,128)(2,1)} custom-call(s32[1]{0:T(128)} %bitcast.place, s32[1]{0:T(128)} %bitcast.2.z, f32[1,768,128]{2,1,0:T(8,128)S(1)} %get-tuple-element.63.keep, bf16[1,768,128]{2,1,0:T(8,128)(2,1)S(1)} %collective-permute-done.11.got, bf16[256,1024]{1,0:T(8,128)(2,1)S(1)} %get-tuple-element.56.p.after.x_in.mine, ...), custom_call_target="tpu_custom_call" | custom-call | tf_op jit(solution)/shard_map/pallas_call | solution.py:548
  (25 shorter events, 0.7 us)
Async XLA Ops:
  0.6 3.5 %copy-start = (bf16[4096,512]{1,0:T(8,128)(2,1)S(1)}, bf16[4096,512]{1,0:T(8,128)(2,1)}, u32[]{:S(2)}) copy-start(bf16[4096,512]{1,0:T(8,128)(2,1)} %param.5) | copy-start | bytes 12582916
  0.6 3.5 %copy-start.1 = (s32[16,4]{0,1:T(4,128)S(1)}, s32[16,4]{0,1:T(4,128)}, u32[]{:S(2)}) copy-start(s32[16,4]{0,1:T(4,128)} %param.9) | copy-start | bytes 772
  2.2 13.4 %collective-permute-start = (bf16[2,256,768]{2,1,0:T(8,128)(2,1)S(1)}, bf16[2,256,768]{2,1,0:T(8,128)(2,1)S(1)}, u32[]{:S(2)}, u32[]{:S(2)}) collective-permute-start(bf16[2,256,768]{2,1,0:T(8,128)(2,1)S(1)} %get-tuple-element.36), channel_id=1, source_target_pairs={{0,4},{4,0},{8,12},{12,8},{16,20},{20,16},{24,28},{28,24},{1,5},{5... | collective-permute-start | bytes 2359304 | tf_op jit(solution)/shard_map/ppermute | solution.py:559
  2.7 12.9 %collective-permute-start.1 = (bf16[2,256,512]{2,1,0:T(8,128)(2,1)S(1)}, bf16[2,256,512]{2,1,0:T(8,128)(2,1)S(1)}, u32[]{:S(2)}, u32[]{:S(2)}) collective-permute-start(bf16[2,256,512]{2,1,0:T(8,128)(2,1)S(1)} %get-tuple-element.37), channel_id=1, source_target_pairs={{4,8},{12,16},{20,24},{8,4},{16,12},{24,20},{5,9},{13,17},{21,25},... | collective-permute-start | bytes 1572872 | tf_op jit(solution)/shard_map/ppermute | solution.py:564
  3.4 21.2 %collective-permute-start.4 = (bf16[2,256,256]{2,1,0:T(8,128)(2,1)S(1)}, bf16[2,256,256]{2,1,0:T(8,128)(2,1)S(1)}, u32[]{:S(2)}, u32[]{:S(2)}) collective-permute-start(bf16[2,256,256]{2,1,0:T(8,128)(2,1)S(1)} %get-tuple-element.43), channel_id=1, source_target_pairs={{4,8},{12,16},{20,24},{8,4},{16,12},{24,20},{5,9},{13,17},{21,25},... | collective-permute-start | bytes 786440 | tf_op jit(solution)/shard_map/ppermute | solution.py:564
  19.3 6.4 %collective-permute-start.2 = (bf16[128,1024]{1,0:T(8,128)(2,1)S(1)}, bf16[128,1024]{1,0:T(8,128)(2,1)S(1)}, u32[]{:S(2)}, u32[]{:S(2)}) collective-permute-start(bf16[128,1024]{1,0:T(8,128)(2,1)S(1)} %get-tuple-element.41), channel_id=1, source_target_pairs={{0,4},{4,0},{8,12},{12,8},{16,20},{20,16},{24,28},{28,24},{1,5},{5... | collective-permute-start | bytes 786440 | tf_op jit(solution)/shard_map/ppermute | solution.py:559
  24.6 1.5 %collective-permute-start.3 = (bf16[128,1024]{1,0:T(8,128)(2,1)S(1)}, bf16[128,1024]{1,0:T(8,128)(2,1)S(1)}, u32[]{:S(2)}, u32[]{:S(2)}) collective-permute-start(bf16[128,1024]{1,0:T(8,128)(2,1)S(1)} %get-tuple-element.42), channel_id=1, source_target_pairs={{0,4},{4,0},{8,12},{12,8},{16,20},{20,16},{24,28},{28,24},{1,5},{5... | collective-permute-start | bytes 786440 | tf_op jit(solution)/shard_map/ppermute | solution.py:559
  26.2 11.3 %collective-permute-start.5 = (bf16[256,1024]{1,0:T(8,128)(2,1)S(1)}, bf16[256,1024]{1,0:T(8,128)(2,1)S(1)}, u32[]{:S(2)}, u32[]{:S(2)}) collective-permute-start(bf16[256,1024]{1,0:T(8,128)(2,1)S(1)} %get-tuple-element.44.after.a), channel_id=1, source_target_pairs={{0,8},{4,20},{8,0},{12,28},{16,24},{20,4},{24,16},{28,12},{1,9},{5... | collective-permute-start | bytes 1572872 | tf_op jit(solution)/shard_map/ppermute | solution.py:559
  37.6 9.2 %collective-permute-start.6 = (bf16[256,1024]{1,0:T(8,128)(2,1)S(1)}, bf16[256,1024]{1,0:T(8,128)(2,1)S(1)}, u32[]{:S(2)}, u32[]{:S(2)}) collective-permute-start(bf16[256,1024]{1,0:T(8,128)(2,1)S(1)} %get-tuple-element.49.after.a), channel_id=1, source_target_pairs={{0,16},{4,12},{8,24},{12,4},{16,0},{20,28},{24,8},{28,20},{1,17},{... | collective-permute-start | bytes 1572872 | tf_op jit(solution)/shard_map/ppermute | solution.py:559
  45.2 1.8 %collective-permute-start.7 = (bf16[2,768,128]{2,1,0:T(8,128)(2,1)S(1)}, bf16[2,768,128]{2,1,0:T(8,128)(2,1)S(1)}, u32[]{:S(2)}, u32[]{:S(2)}) collective-permute-start(bf16[2,768,128]{2,1,0:T(8,128)(2,1)S(1)} %get-tuple-element.53.after), channel_id=1, source_target_pairs={{0,4},{4,0},{8,12},{12,8},{16,20},{20,16},{24,28},{28,24},{1,5},{5... | collective-permute-start | bytes 1179656 | tf_op jit(solution)/shard_map/ppermute | solution.py:559
  45.2 2.3 %collective-permute-start.8 = (bf16[2,768,128]{2,1,0:T(8,128)(2,1)S(1)}, bf16[2,768,128]{2,1,0:T(8,128)(2,1)S(1)}, u32[]{:S(2)}, u32[]{:S(2)}) collective-permute-start(bf16[2,768,128]{2,1,0:T(8,128)(2,1)S(1)} %get-tuple-element.55), channel_id=1, source_target_pairs={{0,4},{4,0},{8,12},{12,8},{16,20},{20,16},{24,28},{28,24},{1,5},{5... | collective-permute-start | bytes 1179656 | tf_op jit(solution)/shard_map/ppermute | solution.py:559
  47.8 5.0 %collective-permute-start.9 = (bf16[256,1024]{1,0:T(8,128)(2,1)S(1)}, bf16[256,1024]{1,0:T(8,128)(2,1)S(1)}, u32[]{:S(2)}, u32[]{:S(2)}) collective-permute-start(bf16[256,1024]{1,0:T(8,128)(2,1)S(1)} %get-tuple-element.56.p.after.x_in.mine), channel_id=1, source_target_pairs={{0,4},{4,0},{8,12},{12,8},{16,20},{20,16},{24,28},{28,24},{1,5},{5... | collective-permute-start | bytes 1572872 | tf_op jit(solution)/shard_map/ppermute | solution.py:559
  48.0 8.4 %collective-permute-start.10 = (bf16[2,768,128]{2,1,0:T(8,128)(2,1)S(1)}, bf16[2,768,128]{2,1,0:T(8,128)(2,1)S(1)}, u32[]{:S(2)}, u32[]{:S(2)}) collective-permute-start(bf16[2,768,128]{2,1,0:T(8,128)(2,1)S(1)} %get-tuple-element.62), channel_id=1, source_target_pairs={{0,8},{4,20},{8,0},{12,28},{16,24},{20,4},{24,16},{28,12},{1,9},{5... | collective-permute-start | bytes 1179656 | tf_op jit(solution)/shard_map/ppermute | solution.py:559
  56.6 5.8 %collective-permute-start.11 = (bf16[1,768,128]{2,1,0:T(8,128)(2,1)S(1)}, bf16[1,768,128]{2,1,0:T(8,128)(2,1)S(1)}, u32[]{:S(2)}, u32[]{:S(2)}) collective-permute-start(bf16[1,768,128]{2,1,0:T(8,128)(2,1)S(1)} %get-tuple-element.64), channel_id=1, source_target_pairs={{0,16},{4,12},{8,24},{12,4},{16,0},{20,28},{24,8},{28,20},{1,17},{... | collective-permute-start | bytes 589832 | tf_op jit(solution)/shard_map/ppermute | solution.py:559
  57.4 1.2 %collective-permute-start.12 = (f32[1,512]{1,0:T(1,128)S(1)}, f32[1,512]{1,0:T(1,128)S(1)}, u32[]{:S(2)}, u32[]{:S(2)}) collective-permute-start(f32[1,512]{1,0:T(1,128)S(1)} %get-tuple-element.65), channel_id=1, source_target_pairs={{0,4},{4,0},{8,12},{12,8},{16,20},{20,16},{24,28},{28,24},{1,5},{5... | collective-permute-start | bytes 6152 | tf_op jit(solution)/shard_map/ppermute | solution.py:559
  58.6 3.6 %collective-permute-start.13 = (f32[1,512]{1,0:T(1,128)S(1)}, f32[1,512]{1,0:T(1,128)S(1)}, u32[]{:S(2)}, u32[]{:S(2)}) collective-permute-start(f32[1,512]{1,0:T(1,128)S(1)} %add.9), channel_id=1, source_target_pairs={{0,8},{4,20},{8,0},{12,28},{16,24},{20,4},{24,16},{28,12},{1,9},{5... | collective-permute-start | bytes 6152 | tf_op jit(solution)/shard_map/ppermute | solution.py:559
  62.4 5.2 %collective-permute-start.15 = (bf16[256,128]{1,0:T(8,128)(2,1)S(1)}, bf16[256,128]{1,0:T(8,128)(2,1)S(1)}, u32[]{:S(2)}, u32[]{:S(2)}) collective-permute-start(bf16[256,128]{1,0:T(8,128)(2,1)S(1)} %shard_map.80.refs_0_), channel_id=1, source_target_pairs={{0,2},{1,3},{2,0},{3,1},{4,6},{5,7},{6,4},{7,5},{8,10},{9,11},{10,... | collective-permute-start | bytes 196616 | tf_op jit(solution)/shard_map/ppermute | solution.py:639
  67.6 5.2 %collective-permute-start.16 = (bf16[512,128]{1,0:T(8,128)(2,1)S(1)}, bf16[512,128]{1,0:T(8,128)(2,1)S(1)}, u32[]{:S(2)}, u32[]{:S(2)}) collective-permute-start(bf16[512,128]{1,0:T(8,128)(2,1)S(1)} %shard_map.81), channel_id=1, source_target_pairs={{0,1},{1,0},{2,3},{3,2},{4,5},{5,4},{6,7},{7,6},{8,9},{9,8},{10,11... | collective-permute-start | bytes 393224 | tf_op jit(solution)/shard_map/ppermute | solution.py:639
  69.3 3.6 %collective-permute-start.14 = (f32[1,512]{1,0:T(1,128)S(1)}, f32[1,512]{1,0:T(1,128)S(1)}, u32[]{:S(2)}, u32[]{:S(2)}) collective-permute-start(f32[1,512]{1,0:T(1,128)S(1)} %add.10.after), channel_id=1, source_target_pairs={{0,16},{4,12},{8,24},{12,4},{16,0},{20,28},{24,8},{28,20},{1,17},{... | collective-permute-start | bytes 6152 | tf_op jit(solution)/shard_map/ppermute | solution.py:559
